TPU v7x, 32 devices: a whole 2x2x4 slice. The times are simulated.
32 devices in a mesh: shard: 4 (over x, core), ctx: 2 (over y), tensor: 4 (over z).
Axes of the slice: x: 2, y: 2, z: 4, core: 2. Of those that a mesh axis runs over, the one named last changes fastest.
Arguments:
- layer_input: float32 [4, 2048, 768], P('shard', 'ctx'), may hold values from -6 to 6
- encoder_out: float32 [4, 1024, 768], P('shard', 'ctx'), may hold values from -6 to 6
- enc_length: int32 [4], P('shard'), may hold values from 256 to 1024, as said below
- parent_ids: int32 [4, 16], P('shard'), may hold values from -1 to 15, as said below
- token_segment: int32 [4, 2048], P('shard'), may hold values from 0 to 15, as said below
- self_query: bfloat16 [768, 768], P('shard', 'tensor'), may hold values from -0.21875 to 0.21875
- self_key: bfloat16 [768, 768], P('shard', 'tensor'), may hold values from -0.21875 to 0.21875
- self_value: bfloat16 [768, 768], P('shard', 'tensor'), may hold values from -0.21875 to 0.21875
- self_output: bfloat16 [768, 768], P('tensor', 'shard'), may hold values from -3 to 3
- cross_query: bfloat16 [768, 768], P('shard', 'tensor'), may hold values from -0.21875 to 0.21875
- cross_key: bfloat16 [768, 768], P('shard', 'tensor'), may hold values from -0.21875 to 0.21875
- cross_value: bfloat16 [768, 768], P('shard', 'tensor'), may hold values from -0.21875 to 0.21875
- cross_output: bfloat16 [768, 768], P('tensor', 'shard'), may hold values from -3 to 3
- ffn_up: bfloat16 [768, 3072], P('shard', 'tensor'), may hold values from -0.21875 to 0.21875
- ffn_down: bfloat16 [3072, 768], P('tensor', 'shard'), may hold values from -0.109375 to 0.109375
- self_qbias: float32 [768], P('tensor'), may hold values from -3 to 3
- self_vbias: float32 [768], P('tensor'), may hold values from -3 to 3
- self_obias: float32 [768], replicated, may hold values from -3 to 3
- cross_qbias: float32 [768], P('tensor'), may hold values from -3 to 3
- cross_vbias: float32 [768], P('tensor'), may hold values from -3 to 3
- cross_obias: float32 [768], replicated, may hold values from -3 to 3
- ffn_upbias: float32 [3072], P('tensor'), may hold values from -3 to 3
- ffn_downbias: float32 [768], replicated, may hold values from -3 to 3
- norm1_gain: float32 [768], replicated, may hold values from 0.5 to 1.5
- norm1_shift: float32 [768], replicated, may hold values from -2 to 2
- norm2_gain: float32 [768], replicated, may hold values from 0.5 to 1.5
- norm2_shift: float32 [768], replicated, may hold values from -2 to 2
- norm3_gain: float32 [768], replicated, may hold values from 0.5 to 1.5
- norm3_shift: float32 [768], replicated, may hold values from -2 to 2
- out_grad: float32 [4, 2048, 768], P('shard', 'ctx'), may hold values from -6 to 6
Outputs:
- out_hidden: float32 [4, 2048, 768], P('shard', 'ctx')
- grad_input: float32 [4, 2048, 768], P('shard', 'ctx')
- grad_encoder: float32 [4, 1024, 768], P('shard', 'ctx')
- grad_self_query: float32 [768, 768], P('shard', 'tensor')
- grad_self_key: float32 [768, 768], P('shard', 'tensor')
- grad_self_value: float32 [768, 768], P('shard', 'tensor')
- grad_self_output: float32 [768, 768], P('tensor', 'shard')
- grad_cross_query: float32 [768, 768], P('shard', 'tensor')
- grad_cross_key: float32 [768, 768], P('shard', 'tensor')
- grad_cross_value: float32 [768, 768], P('shard', 'tensor')
- grad_cross_output: float32 [768, 768], P('tensor', 'shard')
- grad_ffn_up: float32 [768, 3072], P('shard', 'tensor')
- grad_ffn_down: float32 [3072, 768], P('tensor', 'shard')
- grad_self_qbias: float32 [768], P('tensor')
- grad_self_vbias: float32 [768], P('tensor')
- grad_self_obias: float32 [768], replicated
- grad_cross_qbias: float32 [768], P('tensor')
- grad_cross_vbias: float32 [768], P('tensor')
- grad_cross_obias: float32 [768], replicated
- grad_ffn_upbias: float32 [3072], P('tensor')
- grad_ffn_downbias: float32 [768], replicated
- grad_norm1_gain: float32 [768], replicated
- grad_norm1_shift: float32 [768], replicated
- grad_norm2_gain: float32 [768], replicated
- grad_norm2_shift: float32 [768], replicated
- grad_norm3_gain: float32 [768], replicated
- grad_norm3_shift: float32 [768], replicated
Inputs may be any that keep to these rules, and one draw needn't show every extreme that they name: `enc_length`: some tree uses all 1024 encoder positions. `parent_ids`: in each tree the 16 segment labels form a trunk chain of 8 segments from a root whose parent is -1, then 4 branches whose parent is the trunk's last segment, each the parent of one leaf. `token_segment`: each segment fills exactly one aligned block of 128 tokens of its tree; the trunk's segments come first in chain order, then each branch followed by its leaf.
All inputs are finite; a program needn't handle non-finite values.
Results may differ from a plain program's by a relative error of at most 0.025.
The roundings to bfloat16 on the way count: a program that leaves them out, or rounds other values in their place, can miss the bound.
Values may be sent and summed in bfloat16 or wider, within the bound.
No kernel may reach another device: no remote copies, remote signals or barrier semaphores. Data moves between devices by JAX's collectives and lax.ppermute only.
A program may use at most 256 MiB of HBM per device.

v0:
```python
import jax
import jax.numpy as jnp
from jax import lax
from jax.sharding import PartitionSpec as P

HEAD_DIM = 64


eps_norm = 1e-05
row_block = 512


def product(left_side, right_side):
    return jnp.dot(left_side, right_side, preferred_element_type=jnp.float32)


def product_transposed_left(left_side, right_side):
    return jnp.einsum("ra,rb->ab", left_side, right_side, preferred_element_type=jnp.float32)


def product_transposed_right(left_side, right_side):
    return jnp.einsum("ra,ba->rb", left_side, right_side, preferred_element_type=jnp.float32)


def gelu_exact(values):
    return jax.nn.gelu(values, approximate=False)


def layer_norm(values, gain_row, shift_row):
    center = values - jnp.mean(values, axis=-1, keepdims=True)
    inverse = lax.rsqrt(jnp.mean(center * center, axis=-1, keepdims=True) + eps_norm)
    return center * inverse * gain_row + shift_row


def norm_back(pre_sum, gain_row, grad_out):
    center = pre_sum - jnp.mean(pre_sum, axis=-1, keepdims=True)
    inverse = lax.rsqrt(jnp.mean(center * center, axis=-1, keepdims=True) + eps_norm)
    normed = center * inverse
    grad_normed = grad_out * gain_row
    grad_pre = inverse * (
        grad_normed
        - jnp.mean(grad_normed, axis=-1, keepdims=True)
        - normed * jnp.mean(grad_normed * normed, axis=-1, keepdims=True)
    )
    return (grad_pre, jnp.sum(grad_out * normed, axis=0), jnp.sum(grad_out, axis=0))


def closure_of(parent_row):
    segment_count = parent_row.shape[0]
    labels = jnp.arange(segment_count, dtype=jnp.int32)
    closure = (parent_row[:, None] == labels[None, :]).astype(jnp.float32)
    for squaring in range(max(1, segment_count.bit_length())):
        closure = jnp.minimum(closure + product(closure, closure), 1.0)
    return closure


def path_allowed(query_seg, query_pos, key_seg, closure):
    segment_count = closure.shape[0]
    labels = jnp.arange(segment_count, dtype=jnp.int32)
    query_hot = (query_seg[:, None] == labels[None, :]).astype(jnp.float32)
    key_hot = (key_seg[:, None] == labels[None, :]).astype(jnp.float32)
    ancestor_rows = product(query_hot, closure)
    strict = product_transposed_right(ancestor_rows, key_hot) > 0.5
    same_seg = product_transposed_right(query_hot, key_hot) > 0.5
    key_pos = jnp.arange(key_seg.shape[0], dtype=jnp.int32)
    return strict | same_seg & (key_pos[None, :] <= query_pos[:, None])


def attend_forward(query_block, keys_all, values_all, allowed):
    scores = jnp.einsum("qhd,khd->hqk", query_block, keys_all, preferred_element_type=jnp.float32)
    scores = jnp.where(allowed[None], scores, -jnp.inf)
    row_peak = jnp.max(scores, axis=-1, keepdims=True)
    exponent = jnp.exp(scores - row_peak)
    row_total = jnp.sum(exponent, axis=-1, keepdims=True)
    weights_soft = (exponent / row_total).astype(jnp.bfloat16)
    mixture = jnp.einsum(
        "hqk,khd->qhd", weights_soft, values_all, preferred_element_type=jnp.float32
    )
    return (mixture, (row_peak + jnp.log(row_total))[..., 0])


def attend_backward(query_block, keys_all, values_all, allowed, log_total, grad_mix):
    scores = jnp.einsum("qhd,khd->hqk", query_block, keys_all, preferred_element_type=jnp.float32)
    probs_full = jnp.exp(jnp.where(allowed[None], scores, -jnp.inf) - log_total[..., None])
    probs_low = probs_full.astype(jnp.bfloat16)
    grad_probs = jnp.einsum(
        "qhd,khd->hqk", grad_mix, values_all, preferred_element_type=jnp.float32
    )
    grad_values = jnp.einsum(
        "hqk,qhd->khd", probs_low, grad_mix, preferred_element_type=jnp.float32
    )
    grad_scores = probs_full * (
        grad_probs - jnp.sum(probs_full * grad_probs, axis=-1, keepdims=True)
    )
    scores_low = grad_scores.astype(jnp.bfloat16)
    grad_query = jnp.einsum(
        "hqk,khd->qhd", scores_low, keys_all, preferred_element_type=jnp.float32
    )
    grad_keys = jnp.einsum(
        "hqk,qhd->khd", scores_low, query_block, preferred_element_type=jnp.float32
    )
    return (grad_query, grad_keys, grad_values)


def blocks_forward(queries, keys_all, values_all, allow_fn):
    local_rows = queries.shape[0]
    block_rows = min(row_block, local_rows)
    mixtures = []
    log_parts = []
    for row_start in range(0, local_rows, block_rows):
        allowed = allow_fn(row_start, block_rows)
        mixture, log_total = attend_forward(
            queries[row_start : row_start + block_rows], keys_all, values_all, allowed
        )
        mixtures.append(mixture)
        log_parts.append(log_total)
    return (jnp.concatenate(mixtures, axis=0), jnp.concatenate(log_parts, axis=1))


def blocks_backward(queries, keys_all, values_all, log_totals, grad_mix, allow_fn):
    local_rows = queries.shape[0]
    block_rows = min(row_block, local_rows)
    query_parts = []
    grad_keys = jnp.zeros(keys_all.shape, jnp.float32)
    grad_values = jnp.zeros(values_all.shape, jnp.float32)
    for row_start in range(0, local_rows, block_rows):
        row_end = row_start + block_rows
        allowed = allow_fn(row_start, block_rows)
        part_query, part_keys, part_values = attend_backward(
            queries[row_start:row_end],
            keys_all,
            values_all,
            allowed,
            log_totals[:, row_start:row_end],
            grad_mix[row_start:row_end],
        )
        query_parts.append(part_query)
        grad_keys = grad_keys + part_keys
        grad_values = grad_values + part_values
    return (jnp.concatenate(query_parts, axis=0), grad_keys, grad_values)


def self_allow(seg_row, closure, offset):

    def allow_fn(row_start, block_rows):
        query_pos = offset + row_start + jnp.arange(block_rows, dtype=jnp.int32)
        query_seg = lax.dynamic_slice_in_dim(seg_row, offset + row_start, block_rows)
        return path_allowed(query_seg, query_pos, seg_row, closure)

    return allow_fn


def cross_allow(length, key_count):

    def allow_fn(row_start, block_rows):
        valid_keys = jnp.arange(key_count, dtype=jnp.int32) < length
        return jnp.broadcast_to(valid_keys[None, :], (block_rows, key_count))

    return allow_fn


def self_forward(queries, keys_all, values_all, segments, closures, offset):

    def per_tree(tree_args):
        tree_queries, tree_keys, tree_values, seg_row, closure = tree_args
        return blocks_forward(
            tree_queries, tree_keys, tree_values, self_allow(seg_row, closure, offset)
        )

    return lax.map(per_tree, (queries, keys_all, values_all, segments, closures))


def self_attention_backward(
    queries, keys_all, values_all, log_totals, grad_mix, segments, closures, offset
):

    def per_tree(tree_args):
        tree_queries, tree_keys, tree_values, tree_logs, tree_grad, seg_row, closure = tree_args
        return blocks_backward(
            tree_queries,
            tree_keys,
            tree_values,
            tree_logs,
            tree_grad,
            self_allow(seg_row, closure, offset),
        )

    return lax.map(
        per_tree, (queries, keys_all, values_all, log_totals, grad_mix, segments, closures)
    )


def cross_forward(queries, keys_all, values_all, lengths):

    def per_tree(tree_args):
        tree_queries, tree_keys, tree_values, length = tree_args
        return blocks_forward(
            tree_queries, tree_keys, tree_values, cross_allow(length, tree_keys.shape[0])
        )

    return lax.map(per_tree, (queries, keys_all, values_all, lengths))


def cross_backward(queries, keys_all, values_all, log_totals, grad_mix, lengths):

    def per_tree(tree_args):
        tree_queries, tree_keys, tree_values, tree_logs, tree_grad, length = tree_args
        return blocks_backward(
            tree_queries,
            tree_keys,
            tree_values,
            tree_logs,
            tree_grad,
            cross_allow(length, tree_keys.shape[0]),
        )

    return lax.map(per_tree, (queries, keys_all, values_all, log_totals, grad_mix, lengths))


def local(
    layer_input,
    encoder_out,
    enc_length,
    parent_ids,
    token_segment,
    self_query,
    self_key,
    self_value,
    self_output,
    cross_query,
    cross_key,
    cross_value,
    cross_output,
    ffn_up,
    ffn_down,
    self_qbias,
    self_vbias,
    self_obias,
    cross_qbias,
    cross_vbias,
    cross_obias,
    ffn_upbias,
    ffn_downbias,
    norm1_gain,
    norm1_shift,
    norm2_gain,
    norm2_shift,
    norm3_gain,
    norm3_shift,
    out_grad,
):
    number_of_trees, local_rows, model_width = layer_input.shape
    enc_rows = encoder_out.shape[1]
    flattened_rows = number_of_trees * local_rows
    flat_enc = number_of_trees * enc_rows
    offset = lax.axis_index("ctx") * local_rows
    scaling = HEAD_DIM ** (-0.5)

    def reduce_branch(term_part):
        return lax.psum(term_part, "tensor")

    def reduce_input(term_part):
        return lax.psum(term_part, "tensor")

    (
        full_query,
        complete_key,
        full_value,
        full_output,
        full_cquery,
        full_ckey,
        full_cvalue,
        full_coutput,
        full_up,
        full_down,
    ) = (
        lax.all_gather(self_query, "shard", axis=0, tiled=True),
        lax.all_gather(self_key, "shard", axis=0, tiled=True),
        lax.all_gather(self_value, "shard", axis=0, tiled=True),
        lax.all_gather(self_output, "shard", axis=1, tiled=True),
        lax.all_gather(cross_query, "shard", axis=0, tiled=True),
        lax.all_gather(cross_key, "shard", axis=0, tiled=True),
        lax.all_gather(cross_value, "shard", axis=0, tiled=True),
        lax.all_gather(cross_output, "shard", axis=1, tiled=True),
        lax.all_gather(ffn_up, "shard", axis=0, tiled=True),
        lax.all_gather(ffn_down, "shard", axis=1, tiled=True),
    )
    closures = jax.vmap(closure_of)(parent_ids)
    head_columns = full_query.shape[1]
    local_heads = head_columns // HEAD_DIM
    input_flat = layer_input.reshape(flattened_rows, model_width)
    input_reduced = input_flat.astype(jnp.bfloat16)
    query_self = ((product(input_reduced, full_query) + self_qbias) * scaling).astype(jnp.bfloat16)
    key_self = product(input_reduced, complete_key).astype(jnp.bfloat16)
    value_self = (product(input_reduced, full_value) + self_vbias).astype(jnp.bfloat16)
    key_gathered, value_gathered = (
        lax.all_gather(
            key_self.reshape(number_of_trees, local_rows, head_columns), "ctx", axis=1, tiled=True
        ),
        lax.all_gather(
            value_self.reshape(number_of_trees, local_rows, head_columns), "ctx", axis=1, tiled=True
        ),
    )
    tree_length = key_gathered.shape[1]
    query_heads = query_self.reshape(number_of_trees, local_rows, local_heads, HEAD_DIM)
    key_heads = key_gathered.reshape(number_of_trees, tree_length, local_heads, HEAD_DIM)
    value_heads = value_gathered.reshape(number_of_trees, tree_length, local_heads, HEAD_DIM)
    self_mix, self_logs = self_forward(
        query_heads, key_heads, value_heads, token_segment, closures, offset
    )
    self_low = self_mix.reshape(flattened_rows, head_columns).astype(jnp.bfloat16)
    sum_one = input_flat + reduce_branch(product(self_low, full_output)) + self_obias
    hidden_one = layer_norm(sum_one, norm1_gain, norm1_shift)
    hidden_one_low = hidden_one.astype(jnp.bfloat16)
    query_cross = ((product(hidden_one_low, full_cquery) + cross_qbias) * scaling).astype(
        jnp.bfloat16
    )
    encoder_low = encoder_out.reshape(flat_enc, model_width).astype(jnp.bfloat16)
    key_cross = product(encoder_low, full_ckey).astype(jnp.bfloat16)
    value_cross = (product(encoder_low, full_cvalue) + cross_vbias).astype(jnp.bfloat16)
    ckey_gathered, cvalue_gathered = (
        lax.all_gather(
            key_cross.reshape(number_of_trees, enc_rows, head_columns), "ctx", axis=1, tiled=True
        ),
        lax.all_gather(
            value_cross.reshape(number_of_trees, enc_rows, head_columns), "ctx", axis=1, tiled=True
        ),
    )
    enc_total = ckey_gathered.shape[1]
    cquery_heads = query_cross.reshape(number_of_trees, local_rows, local_heads, HEAD_DIM)
    ckey_heads = ckey_gathered.reshape(number_of_trees, enc_total, local_heads, HEAD_DIM)
    cvalue_heads = cvalue_gathered.reshape(number_of_trees, enc_total, local_heads, HEAD_DIM)
    cross_mix, cross_logs = cross_forward(cquery_heads, ckey_heads, cvalue_heads, enc_length)
    cross_low = cross_mix.reshape(flattened_rows, head_columns).astype(jnp.bfloat16)
    sum_two = hidden_one + reduce_branch(product(cross_low, full_coutput)) + cross_obias
    hidden_two = layer_norm(sum_two, norm2_gain, norm2_shift)
    hidden_two_low = hidden_two.astype(jnp.bfloat16)
    ffn_pre = product(hidden_two_low, full_up) + ffn_upbias
    ffn_act = gelu_exact(ffn_pre).astype(jnp.bfloat16)
    sum_three = hidden_two + reduce_branch(product(ffn_act, full_down)) + ffn_downbias
    result = layer_norm(sum_three, norm3_gain, norm3_shift)
    grad_three, gain3_grad, shift3_grad = norm_back(
        sum_three, norm3_gain, out_grad.reshape(flattened_rows, model_width)
    )
    downbias_grad = jnp.sum(grad_three, axis=0)
    grad_three_low = grad_three.astype(jnp.bfloat16)
    down_grad = product_transposed_left(ffn_act, grad_three_low)
    grad_act = product_transposed_right(grad_three_low, full_down)
    gelu_pull = jax.vjp(gelu_exact, ffn_pre)[1]
    grad_pre = gelu_pull(grad_act)[0]
    upbias_grad = jnp.sum(grad_pre, axis=0)
    grad_pre_low = grad_pre.astype(jnp.bfloat16)
    up_grad = product_transposed_left(hidden_two_low, grad_pre_low)
    grad_hidden_two = grad_three + reduce_input(product_transposed_right(grad_pre_low, full_up))
    grad_two, gain2_grad, shift2_grad = norm_back(sum_two, norm2_gain, grad_hidden_two)
    cobias_grad = jnp.sum(grad_two, axis=0)
    grad_two_low = grad_two.astype(jnp.bfloat16)
    coutput_grad = product_transposed_left(cross_low, grad_two_low)
    grad_cmix = (
        product_transposed_right(grad_two_low, full_coutput)
        .astype(jnp.bfloat16)
        .reshape(number_of_trees, local_rows, local_heads, HEAD_DIM)
    )
    grad_cquery, grad_ckey_all, grad_cvalue_all = cross_backward(
        cquery_heads, ckey_heads, cvalue_heads, cross_logs, grad_cmix, enc_length
    )
    grad_cquery = grad_cquery.reshape(flattened_rows, head_columns) * scaling
    cqbias_grad = jnp.sum(grad_cquery, axis=0)
    grad_cquery_low = grad_cquery.astype(jnp.bfloat16)
    cquery_grad = product_transposed_left(hidden_one_low, grad_cquery_low)
    grad_hidden_one = grad_two + reduce_input(
        product_transposed_right(grad_cquery_low, full_cquery)
    )
    grad_ckey, grad_cvalue = (
        lax.psum_scatter(
            grad_ckey_all.reshape(number_of_trees, enc_total, head_columns).astype(jnp.bfloat16),
            "ctx",
            scatter_dimension=1,
            tiled=True,
        ).astype(jnp.float32),
        lax.psum_scatter(
            grad_cvalue_all.reshape(number_of_trees, enc_total, head_columns).astype(jnp.bfloat16),
            "ctx",
            scatter_dimension=1,
            tiled=True,
        ).astype(jnp.float32),
    )
    grad_ckey = grad_ckey.reshape(flat_enc, head_columns)
    grad_cvalue = grad_cvalue.reshape(flat_enc, head_columns)
    cvbias_grad = jnp.sum(grad_cvalue, axis=0)
    grad_ckey_low = grad_ckey.astype(jnp.bfloat16)
    grad_cvalue_low = grad_cvalue.astype(jnp.bfloat16)
    ckey_grad = product_transposed_left(encoder_low, grad_ckey_low)
    cvalue_grad = product_transposed_left(encoder_low, grad_cvalue_low)
    encoder_grad = lax.psum(
        (
            product_transposed_right(grad_ckey_low, full_ckey)
            + product_transposed_right(grad_cvalue_low, full_cvalue)
        ).astype(jnp.bfloat16),
        "tensor",
    ).astype(jnp.float32)
    grad_one, gain1_grad, shift1_grad = norm_back(sum_one, norm1_gain, grad_hidden_one)
    obias_grad = jnp.sum(grad_one, axis=0)
    grad_one_low = grad_one.astype(jnp.bfloat16)
    output_grad = product_transposed_left(self_low, grad_one_low)
    grad_smix = (
        product_transposed_right(grad_one_low, full_output)
        .astype(jnp.bfloat16)
        .reshape(number_of_trees, local_rows, local_heads, HEAD_DIM)
    )
    self_query_gradient, self_key_gradient_total, self_value_gradient_total = (
        self_attention_backward(
            query_heads,
            key_heads,
            value_heads,
            self_logs,
            grad_smix,
            token_segment,
            closures,
            offset,
        )
    )
    self_key_gradient, self_value_gradient = (
        lax.psum_scatter(
            self_key_gradient_total.reshape(number_of_trees, tree_length, head_columns).astype(
                jnp.bfloat16
            ),
            "ctx",
            scatter_dimension=1,
            tiled=True,
        ).astype(jnp.float32),
        lax.psum_scatter(
            self_value_gradient_total.reshape(number_of_trees, tree_length, head_columns).astype(
                jnp.bfloat16
            ),
            "ctx",
            scatter_dimension=1,
            tiled=True,
        ).astype(jnp.float32),
    )
    self_key_gradient = self_key_gradient.reshape(flattened_rows, head_columns)
    self_value_gradient = self_value_gradient.reshape(flattened_rows, head_columns)
    self_query_gradient = self_query_gradient.reshape(flattened_rows, head_columns) * scaling
    qbias_grad = jnp.sum(self_query_gradient, axis=0)
    vbias_grad = jnp.sum(self_value_gradient, axis=0)
    grad_squery_low = self_query_gradient.astype(jnp.bfloat16)
    self_key_gradient_reduced = self_key_gradient.astype(jnp.bfloat16)
    grad_svalue_low = self_value_gradient.astype(jnp.bfloat16)
    query_grad = product_transposed_left(input_reduced, grad_squery_low)
    key_gradient = product_transposed_left(input_reduced, self_key_gradient_reduced)
    value_grad = product_transposed_left(input_reduced, grad_svalue_low)
    input_grad = grad_one + reduce_input(
        product_transposed_right(grad_squery_low, full_query)
        + product_transposed_right(self_key_gradient_reduced, complete_key)
        + product_transposed_right(grad_svalue_low, full_value)
    )
    shares = (
        lax.psum_scatter(
            query_grad.astype(jnp.bfloat16), "shard", scatter_dimension=0, tiled=True
        ).astype(jnp.float32),
        lax.psum_scatter(
            key_gradient.astype(jnp.bfloat16), "shard", scatter_dimension=0, tiled=True
        ).astype(jnp.float32),
        lax.psum_scatter(
            value_grad.astype(jnp.bfloat16), "shard", scatter_dimension=0, tiled=True
        ).astype(jnp.float32),
        lax.psum_scatter(
            output_grad.astype(jnp.bfloat16), "shard", scatter_dimension=1, tiled=True
        ).astype(jnp.float32),
        lax.psum_scatter(
            cquery_grad.astype(jnp.bfloat16), "shard", scatter_dimension=0, tiled=True
        ).astype(jnp.float32),
        lax.psum_scatter(
            ckey_grad.astype(jnp.bfloat16), "shard", scatter_dimension=0, tiled=True
        ).astype(jnp.float32),
        lax.psum_scatter(
            cvalue_grad.astype(jnp.bfloat16), "shard", scatter_dimension=0, tiled=True
        ).astype(jnp.float32),
        lax.psum_scatter(
            coutput_grad.astype(jnp.bfloat16), "shard", scatter_dimension=1, tiled=True
        ).astype(jnp.float32),
        lax.psum_scatter(
            up_grad.astype(jnp.bfloat16), "shard", scatter_dimension=0, tiled=True
        ).astype(jnp.float32),
        lax.psum_scatter(
            down_grad.astype(jnp.bfloat16), "shard", scatter_dimension=1, tiled=True
        ).astype(jnp.float32),
    )
    weight_grads = (
        lax.psum(shares[0].astype(jnp.bfloat16), "ctx").astype(jnp.float32),
        lax.psum(shares[1].astype(jnp.bfloat16), "ctx").astype(jnp.float32),
        lax.psum(shares[2].astype(jnp.bfloat16), "ctx").astype(jnp.float32),
        lax.psum(shares[3].astype(jnp.bfloat16), "ctx").astype(jnp.float32),
        lax.psum(shares[4].astype(jnp.bfloat16), "ctx").astype(jnp.float32),
        lax.psum(shares[5].astype(jnp.bfloat16), "ctx").astype(jnp.float32),
        lax.psum(shares[6].astype(jnp.bfloat16), "ctx").astype(jnp.float32),
        lax.psum(shares[7].astype(jnp.bfloat16), "ctx").astype(jnp.float32),
        lax.psum(shares[8].astype(jnp.bfloat16), "ctx").astype(jnp.float32),
        lax.psum(shares[9].astype(jnp.bfloat16), "ctx").astype(jnp.float32),
    )
    small_sums = (
        lax.psum(qbias_grad.astype(jnp.bfloat16), ("shard", "ctx")).astype(jnp.float32),
        lax.psum(vbias_grad.astype(jnp.bfloat16), ("shard", "ctx")).astype(jnp.float32),
        lax.psum(obias_grad.astype(jnp.bfloat16), ("shard", "ctx")).astype(jnp.float32),
        lax.psum(cqbias_grad.astype(jnp.bfloat16), ("shard", "ctx")).astype(jnp.float32),
        lax.psum(cvbias_grad.astype(jnp.bfloat16), ("shard", "ctx")).astype(jnp.float32),
        lax.psum(cobias_grad.astype(jnp.bfloat16), ("shard", "ctx")).astype(jnp.float32),
        lax.psum(upbias_grad.astype(jnp.bfloat16), ("shard", "ctx")).astype(jnp.float32),
        lax.psum(downbias_grad.astype(jnp.bfloat16), ("shard", "ctx")).astype(jnp.float32),
        lax.psum(gain1_grad.astype(jnp.bfloat16), ("shard", "ctx")).astype(jnp.float32),
        lax.psum(shift1_grad.astype(jnp.bfloat16), ("shard", "ctx")).astype(jnp.float32),
        lax.psum(gain2_grad.astype(jnp.bfloat16), ("shard", "ctx")).astype(jnp.float32),
        lax.psum(shift2_grad.astype(jnp.bfloat16), ("shard", "ctx")).astype(jnp.float32),
        lax.psum(gain3_grad.astype(jnp.bfloat16), ("shard", "ctx")).astype(jnp.float32),
        lax.psum(shift3_grad.astype(jnp.bfloat16), ("shard", "ctx")).astype(jnp.float32),
    )
    return (
        result.reshape(number_of_trees, local_rows, model_width),
        input_grad.reshape(number_of_trees, local_rows, model_width),
        encoder_grad.reshape(number_of_trees, enc_rows, model_width),
        weight_grads[0],
        weight_grads[1],
        weight_grads[2],
        weight_grads[3],
        weight_grads[4],
        weight_grads[5],
        weight_grads[6],
        weight_grads[7],
        weight_grads[8],
        weight_grads[9],
        small_sums[0],
        small_sums[1],
        small_sums[2],
        small_sums[3],
        small_sums[4],
        small_sums[5],
        small_sums[6],
        small_sums[7],
        small_sums[8],
        small_sums[9],
        small_sums[10],
        small_sums[11],
        small_sums[12],
        small_sums[13],
    )


def solution(mesh):
    return jax.shard_map(
        local,
        mesh=mesh,
        in_specs=(
            P("shard", "ctx", None),
            P("shard", "ctx", None),
            P("shard"),
            P("shard", None),
            P("shard", None),
            P("shard", "tensor"),
            P("shard", "tensor"),
            P("shard", "tensor"),
            P("tensor", "shard"),
            P("shard", "tensor"),
            P("shard", "tensor"),
            P("shard", "tensor"),
            P("tensor", "shard"),
            P("shard", "tensor"),
            P("tensor", "shard"),
            P("tensor"),
            P("tensor"),
            P(),
            P("tensor"),
            P("tensor"),
            P(),
            P("tensor"),
            P(),
            P(),
            P(),
            P(),
            P(),
            P(),
            P(),
            P("shard", "ctx", None),
        ),
        out_specs=(
            P("shard", "ctx", None),
            P("shard", "ctx", None),
            P("shard", "ctx", None),
            P("shard", "tensor"),
            P("shard", "tensor"),
            P("shard", "tensor"),
            P("tensor", "shard"),
            P("shard", "tensor"),
            P("shard", "tensor"),
            P("shard", "tensor"),
            P("tensor", "shard"),
            P("shard", "tensor"),
            P("tensor", "shard"),
            P("tensor"),
            P("tensor"),
            P(),
            P("tensor"),
            P("tensor"),
            P(),
            P("tensor"),
            P(),
            P(),
            P(),
            P(),
            P(),
            P(),
            P(),
        ),
        check_vma=False,
    )
```

profile of v0, /device:TPU:8, one launch (start us, length us, event | category | flops | bytes accessed | tf_op | source)
XLA Modules:
  0.0 1318.1 jit_solution(4934910665938101854)
XLA Ops:
  11.7 6.5 all_gather.47
  18.2 6.8 all_gather.44
  24.9 6.9 all_gather.45
  31.9 6.8 all_gather.42
  38.6 2.7 fusion.72
  41.4 12.1 all-gather
  54.2 11.3 all-gather.1
  67.6 3.8 fusion.102
  71.4 3.2 fusion.105
  74.6 3.6 fusion.21
  79.9 6.7 select_reduce_fusion.1
  86.6 7.8 fusion
  94.5 6.7 fusion.98
  101.2 6.7 select_reduce_fusion
  107.9 7.8 fusion.1
  115.7 6.4 fusion.99
  128.5 6.3 all_gather.51
  135.2 7.8 all-gather.3
  143.0 6.3 all_gather.48
  149.8 7.9 all-gather.2
  157.8 6.6 all_gather.53
  164.3 7.3 all_gather.50
  171.6 73.8 %all-reduce.11.cloned.1.call-done = f32[1024,768]{1,0:T(8,128)} async-done(((f32[1024,768]{1,0:T(8,128)}), f32[1024,768]{1,0:T(8,128)}) %all-reduce.11.cloned.1.call-update) | async-done | bytes 3145744 | tf_op jit(solution)/shard_map/psum | solution.py:260
  263.7 118.6 %all-reduce.13.cloned.1.call-done = f32[1024,768]{1,0:T(8,128)} async-done(((f32[1024,768]{1,0:T(8,128)}), f32[1024,768]{1,0:T(8,128)}) %all-reduce.13.cloned.1.call-update) | async-done | bytes 3145744 | tf_op jit(solution)/shard_map/psum | solution.py:260
  382.3 2.9 fusion.180
  387.5 11.7 multiply_convert_fusion.4
  399.2 4.8 fusion.199
  404.3 120.0 %all-reduce.15.cloned.1.call-done = f32[1024,768]{1,0:T(8,128)} async-done(((f32[1024,768]{1,0:T(8,128)}), f32[1024,768]{1,0:T(8,128)}) %all-reduce.15.cloned.1.call-update) | async-done | bytes 3145744 | tf_op jit(solution)/shard_map/psum | solution.py:260
  524.3 3.9 fusion.178
  532.0 3.1 fusion.175
  537.0 2.9 fusion.187
  541.1 3.1 fusion.123
  545.2 119.2 %all-reduce.17.cloned.1.call-done = f32[1024,768]{1,0:T(8,128)} async-done(((f32[1024,768]{1,0:T(8,128)}), f32[1024,768]{1,0:T(8,128)}) %all-reduce.17.cloned.1.call-update) | async-done | bytes 3145744 | tf_op jit(solution)/shard_map/psum | solution.py:263
  664.4 5.4 multiply_reduce_fusion.4
  676.2 4.9 multiply_reduce_fusion.3
  681.1 5.2 multiply_convert_fusion.3
  692.9 4.1 fusion.24
  697.1 5.0 fusion.66
  703.1 2.7 fusion.206
  707.7 105.4 %all-reduce.19.cloned.1.call-done = f32[1024,768]{1,0:T(8,128)} async-done(((f32[1024,768]{1,0:T(8,128)}), f32[1024,768]{1,0:T(8,128)}) %all-reduce.19.cloned.1.call-update) | async-done | bytes 3145744 | tf_op jit(solution)/shard_map/psum | solution.py:263
  813.1 4.4 multiply_reduce_fusion.5
  821.4 4.2 fusion.4
  825.6 8.3 multiply_reduce_fusion
  833.9 5.3 multiply_reduce_fusion.1
  839.3 4.7 multiply_convert_fusion.1
  848.9 4.0 fusion.50
  853.0 10.5 multiply_convert_fusion
  883.1 5.1 fusion.202
  888.3 5.2 fusion.203
  906.1 5.0 convolution_convert_fusion
  911.2 4.2 convolution_convert_fusion.1
  915.5 2.9 convolution_convert_fusion.2
  922.1 15.4 %reduce-scatter.53.cloned.1.call-done = bf16[192,192]{1,0:T(8,128)(2,1)} async-done(((bf16[768,192]{1,0:T(8,128)(2,1)}), bf16[192,192]{1,0:T(8,128)(2,1)}) %reduce-scatter.53.cloned.1.call-update) | async-done | bytes 73744
  939.1 21.5 %reduce-scatter.51.cloned.1.call-done = bf16[192,192]{1,0:T(8,128)(2,1)} async-done(((bf16[768,192]{1,0:T(8,128)(2,1)}), bf16[192,192]{1,0:T(8,128)(2,1)}) %reduce-scatter.51.cloned.1.call-update) | async-done | bytes 73744
  962.2 21.6 %reduce-scatter.49.cloned.1.call-done = bf16[192,192]{1,0:T(8,128)(2,1)} async-done(((bf16[768,192]{1,0:T(8,128)(2,1)}), bf16[192,192]{1,0:T(8,128)(2,1)}) %reduce-scatter.49.cloned.1.call-update) | async-done | bytes 73744
  985.5 21.5 %reduce-scatter.43.cloned.1.call-done = bf16[192,192]{1,0:T(8,128)(2,1)} async-done(((bf16[768,192]{1,0:T(8,128)(2,1)}), bf16[192,192]{1,0:T(8,128)(2,1)}) %reduce-scatter.43.cloned.1.call-update) | async-done | bytes 73744
  1008.6 21.6 %reduce-scatter.47.cloned.1.call-done = bf16[192,192]{1,0:T(8,128)(2,1)} async-done(((bf16[768,192]{1,0:T(8,128)(2,1)}), bf16[192,192]{1,0:T(8,128)(2,1)}) %reduce-scatter.47.cloned.1.call-update) | async-done | bytes 73744
  1031.9 21.5 %reduce-scatter.45.cloned.1.call-done = bf16[192,192]{1,0:T(8,128)(2,1)} async-done(((bf16[768,192]{1,0:T(8,128)(2,1)}), bf16[192,192]{1,0:T(8,128)(2,1)}) %reduce-scatter.45.cloned.1.call-update) | async-done | bytes 73744
  1055.0 26.6 %reduce-scatter.41.cloned.1.call-done = bf16[768,192]{0,1:T(8,128)(2,1)} async-done(((bf16[768,768]{0,1:T(8,128)(2,1)}), bf16[768,192]{0,1:T(8,128)(2,1)}) %reduce-scatter.41.cloned.1.call-update) | async-done | bytes 294928 | tf_op jit(solution)/shard_map/reduce_scatter | solution.py:485
  1081.6 29.0 %reduce-scatter.39.cloned.1.call-done = bf16[192,768]{1,0:T(8,128)(2,1)} async-done(((bf16[768,768]{1,0:T(8,128)(2,1)}), bf16[192,768]{1,0:T(8,128)(2,1)}) %reduce-scatter.39.cloned.1.call-update) | async-done | bytes 294928 | tf_op jit(solution)/shard_map/reduce_scatter | solution.py:482
  1110.6 23.8 %reduce-scatter.37.cloned.1.call-done = bf16[192,192]{1,0:T(8,128)(2,1)} async-done(((bf16[768,192]{1,0:T(8,128)(2,1)}), bf16[192,192]{1,0:T(8,128)(2,1)}) %reduce-scatter.37.cloned.1.call-update) | async-done | bytes 73744 | tf_op jit(solution)/shard_map/reduce_scatter | solution.py:470
  1149.2 24.8 %all-reduce = (bf16[192]{0:T(256)(128)(2,1)S(1)}, bf16[192]{0:T(256)(128)(2,1)S(1)}, bf16[768]{0:T(1024)(128)(2,1)S(1)}, bf16[192]{0:T(256)(128)(2,1)S(1)}, bf16...) all-reduce(bf16[192]{0:T(256)(128)(2,1)} %convert_element_type.513,, ...), channel_id=1, replica_groups=mesh['shard'=4,'ctx'=2,'tensor'=4] {'shard','ctx'}, use_global_device_ids=true, to_apply=%region_56.57 | all-reduce | flops 8448 | bytes 33792 | tf_op jit(solution)/shard_map/psum | solution.py:502
  1200.0 106.3 %all-reduce.21.cloned.1.call-done = f32[1024,768]{1,0:T(8,128)} async-done(((f32[1024,768]{1,0:T(8,128)}), f32[1024,768]{1,0:T(8,128)}) %all-reduce.21.cloned.1.call-update) | async-done | bytes 3145744 | tf_op jit(solution)/shard_map/psum | solution.py:263
  1306.3 3.9 add_bitcast_fusion
  (463 shorter events, 153.3 us)
Async XLA Ops:
  8.0 237.4 %all-reduce.11.cloned.1.call-start = ((), (), s32[]{:S(2)}) async-start(), calls=%async_computation.14 | async-start | bytes 6291456 | tf_op jit(solution)/shard_map/psum | solution.py:260
  18.2 104.1 %copy-start.54 = (bf16[192,768]{0,1:T(8,128)(2,1)}, bf16[192,768]{0,1:T(8,128)(2,1)S(1)}, u32[]{:S(2)}) copy-start(bf16[192,768]{0,1:T(8,128)(2,1)S(1)} %all_gather.47) | copy-start | bytes 884740
  24.9 40.6 %copy-start.42 = (bf16[768,192]{1,0:T(8,128)(2,1)}, bf16[768,192]{1,0:T(8,128)(2,1)S(1)}, u32[]{:S(2)}) copy-start(bf16[768,192]{1,0:T(8,128)(2,1)S(1)} %all_gather.44) | copy-start | bytes 884740
  24.9 28.6 %copy-start.2 = (f32[1,1024,768]{2,1,0:T(8,128)S(1)}, f32[1,1024,768]{2,1,0:T(8,128)}, u32[]{:S(2)}) copy-start(f32[1,1024,768]{2,1,0:T(8,128)} %param.30) | copy-start | bytes 9437188
  31.9 22.4 %copy-start.52 = (bf16[768,192]{1,0:T(8,128)(2,1)}, bf16[768,192]{1,0:T(8,128)(2,1)S(1)}, u32[]{:S(2)}) copy-start(bf16[768,192]{1,0:T(8,128)(2,1)S(1)} %all_gather.45) | copy-start | bytes 884740
  38.6 15.6 %copy-start.34 = (bf16[768,192]{1,0:T(8,128)(2,1)}, bf16[768,192]{1,0:T(8,128)(2,1)S(1)}, u32[]{:S(2)}) copy-start(bf16[768,192]{1,0:T(8,128)(2,1)S(1)} %all_gather.42) | copy-start | bytes 884740
  41.4 24.2 %copy-start.122 = (f32[192]{0:T(256)S(1)}, f32[192]{0:T(256)}, u32[]{:S(2)}) copy-start(f32[192]{0:T(256)} %param.45) | copy-start | bytes 2308
  54.2 12.8 copy-start.97
  78.2 37.5 %copy-start.11 = (pred[512,2048]{1,0:T(8,128)(4,1)}, pred[512,2048]{1,0:T(8,128)(4,1)S(1)}, u32[]{:S(2)}) copy-start(pred[512,2048]{1,0:T(8,128)(4,1)S(1)} %fusion.21) | copy-start | bytes 3145732
  79.9 14.6 %copy-start.13 = (pred[512,2048]{1,0:T(8,128)(4,1)}, pred[512,2048]{1,0:T(8,128)(4,1)S(1)}, u32[]{:S(2)}) copy-start(pred[512,2048]{1,0:T(8,128)(4,1)S(1)} %fusion.19) | copy-start | bytes 3145732
  125.3 24.1 %copy-start.123 = (f32[192]{0:T(256)S(1)}, f32[192]{0:T(256)}, u32[]{:S(2)}) copy-start(f32[192]{0:T(256)} %param.49) | copy-start | bytes 2308
  125.3 257.0 %all-reduce.13.cloned.1.call-start = ((), (), s32[]{:S(2)}) async-start(), calls=%async_computation.15 | async-start | bytes 6291456 | tf_op jit(solution)/shard_map/psum | solution.py:260
  126.9 30.8 %copy-start.74 = (bf16[192,192]{0,1:T(8,128)(2,1)S(1)}, bf16[192,192]{0,1:T(8,128)(2,1)}, u32[]{:S(2)}) copy-start(bf16[192,192]{0,1:T(8,128)(2,1)} %copy.68) | copy-start | bytes 221188
  128.4 20.9 %copy-start.26 = (bf16[1,512,768]{2,1,0:T(8,128)(2,1)}, bf16[1,512,768]{2,1,0:T(8,128)(2,1)S(1)}, u32[]{:S(2)}) copy-start(bf16[1,512,768]{2,1,0:T(8,128)(2,1)S(1)} %convert_element_type.438) | copy-start | bytes 2359300
  128.5 35.9 %copy-start.86 = (bf16[192,192]{1,0:T(8,128)(2,1)S(1)}, bf16[192,192]{1,0:T(8,128)(2,1)}, u32[]{:S(2)}) copy-start(bf16[192,192]{1,0:T(8,128)(2,1)} %param.39) | copy-start | bytes 221188
  128.5 117.0 %copy-start.116 = (f32[768]{0:T(1024)S(1)}, f32[768]{0:T(1024)}, u32[]{:S(2)}) copy-start(f32[768]{0:T(1024)} %param.47) | copy-start | bytes 9220
  134.8 15.0 %copy-start.38 = (bf16[768,192]{1,0:T(8,128)(2,1)}, bf16[768,192]{1,0:T(8,128)(2,1)S(1)}, u32[]{:S(2)}) copy-start(bf16[768,192]{1,0:T(8,128)(2,1)S(1)} %all_gather.51) | copy-start | bytes 884740
  149.4 8.4 copy-start.40
  171.6 85.4 %copy-start.98 = (pred[1024]{0:T(1024)(128)(4,1)}, pred[1024]{0:T(1024)(128)(4,1)S(1)}, u32[]{:S(2)}) copy-start(pred[1024]{0:T(1024)(128)(4,1)S(1)} %iota_compare_fusion.17) | copy-start | bytes 3076
  247.8 134.5 %copy-start.76 = (f32[1024]{0:T(1024)}, f32[1024]{0:T(1024)S(1)}, u32[]{:S(2)}) copy-start(f32[1024]{0:T(1024)S(1)} %broadcast_multiply_fusion.8) | copy-start | bytes 12292
  248.5 133.8 %copy-start.82 = (f32[1024]{0:T(1024)}, f32[1024]{0:T(1024)S(1)}, u32[]{:S(2)}) copy-start(f32[1024]{0:T(1024)S(1)} %add_rsqrt_fusion.2) | copy-start | bytes 12292
  259.7 122.6 %copy-start.5 = (f32[1024,768]{1,0:T(8,128)S(1)}, f32[1024,768]{1,0:T(8,128)}, u32[]{:S(2)}) copy-start(f32[1024,768]{1,0:T(8,128)} %copy-done.4) | copy-start | bytes 9437188
  259.7 122.6 %copy-start.110 = (f32[768]{0:T(1024)S(1)}, f32[768]{0:T(1024)}, u32[]{:S(2)}) copy-start(f32[768]{0:T(1024)} %param.54) | copy-start | bytes 9220
  262.0 125.4 %all-gather.7.cloned.1.call-start = ((), (), s32[]{:S(2)}) async-start(), calls=%async_computation.16 | async-start | bytes 1474560 | tf_op jit(solution)/shard_map/all_gather | solution.py:285
  262.6 136.6 %all-gather.9.cloned.1.call-start = ((), (), s32[]{:S(2)}) async-start(), calls=%async_computation.17 | async-start | bytes 1474560 | tf_op jit(solution)/shard_map/all_gather | solution.py:286
  263.2 261.1 %all-reduce.15.cloned.1.call-start = ((), (), s32[]{:S(2)}) async-start(), calls=%async_computation.18 | async-start | bytes 6291456 | tf_op jit(solution)/shard_map/psum | solution.py:260
  385.3 139.0 %copy-start.79 = (f32[1024]{0:T(1024)}, f32[1024]{0:T(1024)S(1)}, u32[]{:S(2)}) copy-start(f32[1024]{0:T(1024)S(1)} %broadcast_multiply_fusion.7) | copy-start | bytes 12292
  387.4 136.9 %copy-start.94 = (f32[1024]{0:T(1024)}, f32[1024]{0:T(1024)S(1)}, u32[]{:S(2)}) copy-start(f32[1024]{0:T(1024)S(1)} %add_rsqrt_fusion.1) | copy-start | bytes 12292
  404.0 120.3 %copy-start.117 = (f32[768]{0:T(1024)S(1)}, f32[768]{0:T(1024)}, u32[]{:S(2)}) copy-start(f32[768]{0:T(1024)} %param.52) | copy-start | bytes 9220
  404.1 260.3 %all-reduce.17.cloned.1.call-start = ((), (), s32[]{:S(2)}) async-start(), calls=%async_computation.19 | async-start | bytes 6291456 | tf_op jit(solution)/shard_map/psum | solution.py:263
  544.2 268.9 %all-reduce.19.cloned.1.call-start = ((), (), s32[]{:S(2)}) async-start(), calls=%async_computation.20 | async-start | bytes 6291456 | tf_op jit(solution)/shard_map/psum | solution.py:263
  545.2 135.9 %copy-start.78 = (f32[3,512]{1,0:T(4,128)}, f32[3,512]{1,0:T(4,128)S(1)}, u32[]{:S(2)}) copy-start(f32[3,512]{1,0:T(4,128)S(1)} %get-tuple-element.309) | copy-start | bytes 18436
  692.8 178.6 %reduce-scatter.35.cloned.1.call-start = ((), (), s32[]{:S(2)}) async-start(), calls=%async_computation.25 | async-start | bytes 589824 | tf_op jit(solution)/shard_map/reduce_scatter | solution.py:381
  702.1 173.6 %reduce-scatter.33.cloned.1.call-start = ((), (), s32[]{:S(2)}) async-start(), calls=%async_computation.24 | async-start | bytes 589824 | tf_op jit(solution)/shard_map/reduce_scatter | solution.py:375
  705.7 107.3 %copy-start.77 = (f32[1024]{0:T(1024)S(1)}, f32[1024]{0:T(1024)}, u32[]{:S(2)}) copy-start(f32[1024]{0:T(1024)} %copy-done.76) | copy-start | bytes 12292
  705.8 107.3 %copy-start.83 = (f32[1024]{0:T(1024)S(1)}, f32[1024]{0:T(1024)}, u32[]{:S(2)}) copy-start(f32[1024]{0:T(1024)} %copy-done.82) | copy-start | bytes 12292
  705.8 107.3 %copy-start.93 = (f32[768]{0:T(1024)S(1)}, f32[768]{0:T(1024)}, u32[]{:S(2)}) copy-start(f32[768]{0:T(1024)} %param.53) | copy-start | bytes 9220
  707.2 190.5 %reduce-scatter.31.cloned.1.call-start = ((), (), s32[]{:S(2)}) async-start(), calls=%async_computation.22 | async-start | bytes 1179648 | tf_op jit(solution)/shard_map/reduce_scatter | solution.py:432
  821.4 12.5 slice-start.3
  825.6 8.3 slice-start.4
  825.6 8.3 slice-start.5
  853.0 48.9 %reduce-scatter.29.cloned.1.call-start = ((), (), s32[]{:S(2)}) async-start(), calls=%async_computation.21 | async-start | bytes 1179648 | tf_op jit(solution)/shard_map/reduce_scatter | solution.py:424
  853.0 10.6 copy-start.31
  853.0 10.6 copy-start.59
  867.2 53.2 %reduce-scatter.55.cloned.1.call-start = ((), (), s32[]{:S(2)}) async-start(), calls=%async_computation.36 | async-start | bytes 491520
  869.3 10.7 copy-start.16
  869.3 10.7 copy-start.45
  871.4 66.0 %reduce-scatter.53.cloned.1.call-start = ((), (), s32[]{:S(2)}) async-start(), calls=%async_computation.35 | async-start | bytes 491520
  875.7 84.9 %reduce-scatter.51.cloned.1.call-start = ((), (), s32[]{:S(2)}) async-start(), calls=%async_computation.34 | async-start | bytes 491520
  880.0 103.9 %reduce-scatter.49.cloned.1.call-start = ((), (), s32[]{:S(2)}) async-start(), calls=%async_computation.33 | async-start | bytes 491520
  888.3 118.7 %reduce-scatter.43.cloned.1.call-start = ((), (), s32[]{:S(2)}) async-start(), calls=%async_computation.30 | async-start | bytes 491520
  897.4 132.8 %reduce-scatter.47.cloned.1.call-start = ((), (), s32[]{:S(2)}) async-start(), calls=%async_computation.32 | async-start | bytes 491520
  901.8 151.5 %reduce-scatter.45.cloned.1.call-start = ((), (), s32[]{:S(2)}) async-start(), calls=%async_computation.31 | async-start | bytes 491520
  906.1 175.5 %reduce-scatter.41.cloned.1.call-start = ((), (), s32[]{:S(2)}) async-start(), calls=%async_computation.29 | async-start | bytes 1474560 | tf_op jit(solution)/shard_map/reduce_scatter | solution.py:485
  911.1 199.5 %reduce-scatter.39.cloned.1.call-start = ((), (), s32[]{:S(2)}) async-start(), calls=%async_computation.28 | async-start | bytes 1474560 | tf_op jit(solution)/shard_map/reduce_scatter | solution.py:482
  915.5 219.0 %reduce-scatter.37.cloned.1.call-start = ((), (), s32[]{:S(2)}) async-start(), calls=%async_computation.27 | async-start | bytes 491520 | tf_op jit(solution)/shard_map/reduce_scatter | solution.py:470
  918.5 226.2 %all-reduce.23.cloned.1.call-start = ((), (), s32[]{:S(2)}) async-start(), calls=%async_computation.26 | async-start | bytes 1572864 | tf_op jit(solution)/shard_map/psum | solution.py:395
  919.0 215.6 %copy-start.37 = (f32[3,64,512]{2,1,0:T(8,128)S(1)}, f32[3,64,512]{2,1,0:T(8,128)}, u32[]{:S(2)}) copy-start(f32[3,64,512]{2,1,0:T(8,128)} %copy-done.36) | copy-start | bytes 1179652
  919.0 216.3 %copy-start.43 = (bf16[768,192]{1,0:T(8,128)(2,1)S(1)}, bf16[768,192]{1,0:T(8,128)(2,1)}, u32[]{:S(2)}) copy-start(bf16[768,192]{1,0:T(8,128)(2,1)} %copy-done.42) | copy-start | bytes 884740
  920.3 263.8 %all-reduce.25.cloned.1.call-start = ((), (), s32[]{:S(2)}) async-start(), calls=%async_computation.37 | async-start | bytes 2752512 | tf_op jit(solution)/shard_map/psum | solution.py:490
  1134.5 171.8 %all-reduce.21.cloned.1.call-start = ((), (), s32[]{:S(2)}) async-start(), calls=%async_computation.23 | async-start | bytes 6291456 | tf_op jit(solution)/shard_map/psum | solution.py:263
  1141.0 8.1 copy-start.115
  1144.7 161.6 %copy-start.17 = (f32[1024,768]{1,0:T(8,128)S(1)}, f32[1024,768]{1,0:T(8,128)}, u32[]{:S(2)}) copy-start(f32[1024,768]{1,0:T(8,128)} %copy-done.15) | copy-start | bytes 9437188
  1184.2 15.0 %copy-start.75 = (bf16[768,192]{0,1:T(8,128)(2,1)S(1)}, bf16[768,192]{0,1:T(8,128)(2,1)}, u32[]{:S(2)}) copy-start(bf16[768,192]{0,1:T(8,128)(2,1)} %get-tuple-element.260) | copy-start | bytes 884740
  (101 other events, 352.5 us)
Sparse Core Ops, SparseCore 0:
  125.4 119.9 all-reduce.10
  262.2 120.0 all-reduce.12
  404.2 120.0 all-reduce.14
  544.3 120.0 all-reduce.16
  692.9 120.0 all-reduce.18
  921.4 44.3 all-reduce.22
  1134.6 49.5 all-reduce.24
  1187.2 119.0 all-reduce.20
Sparse Core Ops, SparseCore 1:
  264.1 18.2 all-gather.6
  283.8 17.3 all-gather.8
  702.2 14.4 reduce-scatter.34
  719.1 13.0 reduce-scatter.32
  853.0 18.3 reduce-scatter.30
  873.8 17.3 reduce-scatter.28
  893.5 20.7 reduce-scatter.54
  916.7 20.7 reduce-scatter.52
  939.8 20.7 reduce-scatter.50
  963.1 20.7 reduce-scatter.48
  986.3 20.7 reduce-scatter.42
  1009.5 20.7 reduce-scatter.46
  1032.6 20.7 reduce-scatter.44
  1055.9 25.6 reduce-scatter.40
  1084.9 25.6 reduce-scatter.38
  1113.7 20.7 reduce-scatter.36
where the time goes:
time: 1330 us; the launch traced here: 1320 us
  waiting for transfers between devices  849 us (64%)
  matrix products  172 us (13%)
  blocking collectives  117 us (9%)
  other arithmetic  97.7 us (7%)
  local copies, waits for them, and re-layouts  61 us (5%)
  between operations  18.5 us (1%)
    psum x3, waiting for transfers between devices, reduce_input(): return lax.psum(term_part, 'tensor')  331 us
    psum x3, waiting for transfers between devices, reduce_branch(): return lax.psum(term_part, 'tensor')  312 us
    unnamed x31, waiting for transfers between devices  125 us
    unnamed x303, local copies, waits for them, and re-layouts  57 us
    reduce_scatter x1, waiting for transfers between devices, local(): lax.psum_scatter(up_grad.astype(jnp.bfloat16), 'shard', scatter_dimension...  29 us
    dot_general x15, matrix products, product(): return jnp.dot(left_side, right_side, preferred_element_type=jnp.float32)  28.2 us
    dot_general x14, matrix products, product_transposed_right(): jnp.einsum('ra,ba->rb', left_side, right_side, preferred_element_type=jnp...  27.2 us
    reduce_scatter x1, waiting for transfers between devices, local(): lax.psum_scatter(down_grad.astype(jnp.bfloat16), 'shard', scatter_dimensi...  26.6 us
  transfers between devices with their start and end apart: 24, of which 16 were waited for; matrix products, arithmetic and copies ran while one was open for 14% of the time, Pallas kernels for 0%

commit v1 on v0

v1 whole, which is shorter than its diff:
```python
import functools

import jax
import jax.numpy as jnp
from jax import lax
from jax.experimental import pallas as pl
from jax.experimental.pallas import tpu as pltpu
from jax.sharding import PartitionSpec as P

HEAD_DIM = 64
LANES = 128
TILE = 256
NEG = -1e30
EPS = 1e-05
F32 = jnp.float32
BF16 = jnp.bfloat16
VMEM_LIMIT = 56 * 1024 * 1024


def dot_of(a, b, a_dim, b_dim):
    return lax.dot_general(a, b, (((a_dim,), (b_dim,)), ((), ())), preferred_element_type=F32)


def nn(a, b):
    return dot_of(a, b, 1, 0)


def nt(a, b):
    return dot_of(a, b, 1, 1)


def tn(a, b):
    return dot_of(a, b, 0, 0)


def head_lanes(rows, half):
    lane = lax.broadcasted_iota(jnp.int32, (rows, LANES), 1)
    return (lane < HEAD_DIM) if half == 0 else (lane >= HEAD_DIM)


def flags_of(rows, seg):
    lane = lax.broadcasted_iota(jnp.int32, (rows, LANES), 1) % HEAD_DIM
    row = lax.broadcasted_iota(jnp.int32, (rows, LANES), 0)
    return jnp.where(lane == row // seg, 1.0, 0.0).astype(BF16)


def causal_keep(size, seg):
    key = lax.broadcasted_iota(jnp.int32, (size, size), 0)
    query = lax.broadcasted_iota(jnp.int32, (size, size), 1)
    return (key // seg != query // seg) | (key <= query)


def flip(a):
    return a.astype(F32).T.astype(a.dtype)


def fold_forward(state, queries, key_tile, value_tile, bias_tile, heads, keep):
    out = []
    for h in range(heads):
        g, half = divmod(h, 2)
        lanes = slice(g * LANES, (g + 1) * LANES)
        if half == 0:
            value_rows = flip(value_tile[:, lanes])
        keys = jnp.where(head_lanes(TILE, half), key_tile[:, lanes], bias_tile)
        scores = nt(keys, queries[h])
        if keep is not None:
            scores = jnp.where(keep, scores, NEG)
        peak, total, mix = state[3 * h : 3 * h + 3]
        new_peak = jnp.maximum(peak, jnp.max(scores, axis=0, keepdims=True))
        weights = jnp.exp(scores - new_peak)
        shrink = jnp.exp(peak - new_peak)
        total = total * shrink + jnp.sum(weights, axis=0, keepdims=True)
        mix = mix * shrink + nn(
            value_rows[half * HEAD_DIM : (half + 1) * HEAD_DIM], weights.astype(BF16)
        )
        out += [new_peak, total, mix]
    return tuple(out)


def fresh_state(heads, rows):
    state = []
    for _ in range(heads):
        state += [
            jnp.full((1, rows), NEG, F32),
            jnp.zeros((1, rows), F32),
            jnp.zeros((HEAD_DIM, rows), F32),
        ]
    return tuple(state)


def flagged_queries(q, heads, seg):
    rows = q.shape[0]
    flags = flags_of(rows, seg)
    return [
        jnp.where(
            head_lanes(rows, h % 2), q[:, (h // 2) * LANES : (h // 2 + 1) * LANES], flags
        )
        for h in range(heads)
    ]


def put_mix(state, heads, groups, mix_ref, log_ref):
    rows = mix_ref.shape[0]
    for g in range(groups):
        parts = []
        for h in (2 * g, 2 * g + 1):
            if h < heads:
                parts.append(state[3 * h + 2] / state[3 * h + 1])
            else:
                parts.append(jnp.zeros((HEAD_DIM, rows), F32))
        mix_ref[:, g * LANES : (g + 1) * LANES] = jnp.concatenate(parts, axis=0).T.astype(BF16)
    for h in range(heads):
        log_ref[h : h + 1, :] = state[3 * h] + jnp.log(state[3 * h + 1])


def self_forward_kernel(
    count_ref, q_ref, k_ref, v_ref, trunk_ref, bias_ref, mix_ref, log_ref, *, heads, seg
):
    groups = (heads + 1) // 2
    width = groups * LANES
    queries = flagged_queries(q_ref[...], heads, seg)
    prefix = bias_ref.shape[1] - TILE
    state = fold_forward(
        fresh_state(heads, TILE),
        queries,
        k_ref[...],
        v_ref[...],
        bias_ref[0, prefix:, :],
        heads,
        causal_keep(TILE, seg),
    )

    def body(c, state):
        rows = pl.ds(pl.multiple_of(c * TILE, TILE), TILE)
        return fold_forward(
            state,
            queries,
            trunk_ref[rows, :width],
            trunk_ref[rows, width:],
            bias_ref[0, rows, :],
            heads,
            None,
        )

    state = lax.fori_loop(0, count_ref[pl.program_id(0)], body, state)
    log_ref[...] = jnp.zeros_like(log_ref)
    put_mix(state, heads, groups, mix_ref, log_ref)


def self_forward(counts, qkv, trunk, bias, heads, seg):
    rows = qkv.shape[0]
    width = qkv.shape[1] // 3
    blocks = rows // TILE
    keys = bias.shape[1]
    return pl.pallas_call(
        functools.partial(self_forward_kernel, heads=heads, seg=seg),
        grid_spec=pltpu.PrefetchScalarGridSpec(
            num_scalar_prefetch=1,
            grid=(blocks,),
            in_specs=[
                pl.BlockSpec((TILE, width), lambda b, n: (b, 0)),
                pl.BlockSpec((TILE, width), lambda b, n: (b, 1)),
                pl.BlockSpec((TILE, width), lambda b, n: (b, 2)),
                pl.BlockSpec(trunk.shape, lambda b, n: (0, 0)),
                pl.BlockSpec((1, keys, LANES), lambda b, n: (b, 0, 0)),
            ],
            out_specs=[
                pl.BlockSpec((TILE, width), lambda b, n: (b, 0)),
                pl.BlockSpec((8, TILE), lambda b, n: (0, b)),
            ],
        ),
        out_shape=[
            jax.ShapeDtypeStruct((rows, width), BF16),
            jax.ShapeDtypeStruct((8, rows), F32),
        ],
        compiler_params=pltpu.CompilerParams(vmem_limit_bytes=VMEM_LIMIT),
        cost_estimate=pl.CostEstimate(
            flops=rows * keys * heads * HEAD_DIM * 16,
            bytes_accessed=rows * width * 12 + trunk.size * 2,
            transcendentals=rows * keys * heads,
        ),
    )(counts, qkv, qkv, qkv, trunk, bias)


def fold_backward(
    queries, plain, grads, logs, deltas, key_tile, value_tile, bias_tile, heads, keep
):
    grad_keys, grad_values, grad_queries = [], [], []
    for h in range(heads):
        g, half = divmod(h, 2)
        lanes = slice(g * LANES, (g + 1) * LANES)
        if half == 0:
            key_rows = flip(key_tile[:, lanes])
        keys = jnp.where(head_lanes(TILE, half), key_tile[:, lanes], bias_tile)
        scores = nt(keys, queries[h])
        if keep is not None:
            scores = jnp.where(keep, scores, NEG)
        probs = jnp.exp(scores - logs[h])
        grad_probs = nt(value_tile[:, lanes], grads[h])
        grad_scores = (probs * (grad_probs - deltas[h])).astype(BF16)
        part_values = nn(probs.astype(BF16), grads[h])
        part_keys = nn(grad_scores, plain[h])
        if half == 0:
            grad_values.append(part_values)
            grad_keys.append(part_keys)
        else:
            grad_values[g] = grad_values[g] + part_values
            grad_keys[g] = grad_keys[g] + part_keys
        grad_queries.append(
            nn(key_rows[half * HEAD_DIM : (half + 1) * HEAD_DIM], grad_scores)
        )
    return grad_keys, grad_values, tuple(grad_queries)


def backward_sides(q, grad, mix, heads, seg):
    rows = q.shape[0]
    queries = flagged_queries(q, heads, seg)
    plain, grads, deltas = [], [], []
    for h in range(heads):
        g, half = divmod(h, 2)
        lanes = slice(g * LANES, (g + 1) * LANES)
        mask = head_lanes(rows, half)
        plain.append(jnp.where(mask, q[:, lanes], jnp.zeros((), BF16)))
        grads.append(jnp.where(mask, grad[:, lanes], jnp.zeros((), BF16)))
        if half == 0:
            product = (grad[:, lanes].astype(F32) * mix[:, lanes].astype(F32)).T
        deltas.append(
            jnp.sum(product[half * HEAD_DIM : (half + 1) * HEAD_DIM], axis=0, keepdims=True)
        )
    return queries, plain, grads, deltas


def put_queries(grad_queries, heads, groups, scale, dq_ref):
    rows = dq_ref.shape[0]
    for g in range(groups):
        parts = [
            grad_queries[h] if h < heads else jnp.zeros((HEAD_DIM, rows), F32)
            for h in (2 * g, 2 * g + 1)
        ]
        dq_ref[:, g * LANES : (g + 1) * LANES] = (
            jnp.concatenate(parts, axis=0).T * scale
        ).astype(BF16)


def self_backward_kernel(
    count_ref,
    q_ref,
    k_ref,
    v_ref,
    trunk_ref,
    bias_ref,
    grad_ref,
    mix_ref,
    log_ref,
    dq_ref,
    dk_ref,
    dv_ref,
    dtrunk_ref,
    *,
    heads,
    seg,
    scale,
):
    groups = (heads + 1) // 2
    width = groups * LANES
    prefix = bias_ref.shape[1] - TILE
    queries, plain, grads, deltas = backward_sides(
        q_ref[...], grad_ref[...], mix_ref[...], heads, seg
    )
    logs = [log_ref[h : h + 1, :] for h in range(heads)]

    @pl.when(pl.program_id(0) == 0)
    def _():
        dtrunk_ref[...] = jnp.zeros_like(dtrunk_ref)

    grad_keys, grad_values, grad_queries = fold_backward(
        queries,
        plain,
        grads,
        logs,
        deltas,
        k_ref[...],
        v_ref[...],
        bias_ref[0, prefix:, :],
        heads,
        causal_keep(TILE, seg),
    )
    for g in range(groups):
        lanes = slice(g * LANES, (g + 1) * LANES)
        dk_ref[:, lanes] = grad_keys[g]
        dv_ref[:, lanes] = grad_values[g]

    def body(c, grad_queries):
        rows = pl.ds(pl.multiple_of(c * TILE, TILE), TILE)
        grad_keys, grad_values, more = fold_backward(
            queries,
            plain,
            grads,
            logs,
            deltas,
            trunk_ref[rows, :width],
            trunk_ref[rows, width:],
            bias_ref[0, rows, :],
            heads,
            None,
        )
        for g in range(groups):
            lanes = slice(g * LANES, (g + 1) * LANES)
            late = slice(width + g * LANES, width + (g + 1) * LANES)
            dtrunk_ref[rows, lanes] += grad_keys[g]
            dtrunk_ref[rows, late] += grad_values[g]
        return tuple(a + b for a, b in zip(grad_queries, more))

    grad_queries = lax.fori_loop(0, count_ref[pl.program_id(0)], body, grad_queries)
    put_queries(grad_queries, heads, groups, scale, dq_ref)


def self_backward(counts, qkv, trunk, bias, grad, mix, logs, heads, seg, scale):
    rows = qkv.shape[0]
    width = qkv.shape[1] // 3
    blocks = rows // TILE
    keys = bias.shape[1]
    tile = pl.BlockSpec((TILE, width), lambda b, n: (b, 0))
    return pl.pallas_call(
        functools.partial(self_backward_kernel, heads=heads, seg=seg, scale=scale),
        grid_spec=pltpu.PrefetchScalarGridSpec(
            num_scalar_prefetch=1,
            grid=(blocks,),
            in_specs=[
                tile,
                pl.BlockSpec((TILE, width), lambda b, n: (b, 1)),
                pl.BlockSpec((TILE, width), lambda b, n: (b, 2)),
                pl.BlockSpec(trunk.shape, lambda b, n: (0, 0)),
                pl.BlockSpec((1, keys, LANES), lambda b, n: (b, 0, 0)),
                tile,
                tile,
                pl.BlockSpec((8, TILE), lambda b, n: (0, b)),
            ],
            out_specs=[tile, tile, tile, pl.BlockSpec(trunk.shape, lambda b, n: (0, 0))],
        ),
        out_shape=[
            jax.ShapeDtypeStruct((rows, width), BF16),
            jax.ShapeDtypeStruct((rows, width), F32),
            jax.ShapeDtypeStruct((rows, width), F32),
            jax.ShapeDtypeStruct(trunk.shape, F32),
        ],
        compiler_params=pltpu.CompilerParams(vmem_limit_bytes=VMEM_LIMIT),
        cost_estimate=pl.CostEstimate(
            flops=rows * keys * heads * HEAD_DIM * 40,
            bytes_accessed=rows * width * 24 + trunk.size * 6,
            transcendentals=rows * keys * heads,
        ),
    )(counts, qkv, qkv, qkv, trunk, bias, grad, mix, logs)


def cross_forward_kernel(q_ref, k_ref, v_ref, bias_ref, mix_ref, log_ref):
    rows = q_ref.shape[0]
    queries = flagged_queries(q_ref[...], 2, rows)
    state = fresh_state(2, rows)
    for c in range(k_ref.shape[0] // TILE):
        part = slice(c * TILE, (c + 1) * TILE)
        state = fold_forward(
            state, queries, k_ref[part, :], v_ref[part, :], bias_ref[part, :], 2, None
        )
    log_ref[...] = jnp.zeros_like(log_ref)
    put_mix(state, 2, 1, mix_ref, log_ref)


def cross_forward(q, k, v, bias):
    rows, width = q.shape
    keys = k.shape[0]
    groups = width // LANES
    part = pl.BlockSpec((rows, LANES), lambda g: (0, g))
    side = pl.BlockSpec((keys, LANES), lambda g: (0, g))
    return pl.pallas_call(
        cross_forward_kernel,
        grid=(groups,),
        in_specs=[part, side, side, pl.BlockSpec((keys, LANES), lambda g: (0, 0))],
        out_specs=[part, pl.BlockSpec((8, rows), lambda g: (g, 0))],
        out_shape=[
            jax.ShapeDtypeStruct((rows, width), BF16),
            jax.ShapeDtypeStruct((8 * groups, rows), F32),
        ],
        compiler_params=pltpu.CompilerParams(vmem_limit_bytes=VMEM_LIMIT),
        cost_estimate=pl.CostEstimate(
            flops=rows * keys * width * 16,
            bytes_accessed=rows * width * 4 + keys * width * 4,
            transcendentals=rows * keys * groups * 2,
        ),
    )(q, k, v, bias)


def cross_backward_kernel(
    q_ref, k_ref, v_ref, bias_ref, grad_ref, mix_ref, log_ref, dq_ref, dk_ref, dv_ref, *, scale
):
    rows = q_ref.shape[0]
    queries, plain, grads, deltas = backward_sides(
        q_ref[...], grad_ref[...], mix_ref[...], 2, rows
    )
    logs = [log_ref[h : h + 1, :] for h in range(2)]
    total = (jnp.zeros((HEAD_DIM, rows), F32),) * 2
    for c in range(k_ref.shape[0] // TILE):
        part = slice(c * TILE, (c + 1) * TILE)
        grad_keys, grad_values, more = fold_backward(
            queries,
            plain,
            grads,
            logs,
            deltas,
            k_ref[part, :],
            v_ref[part, :],
            bias_ref[part, :],
            2,
            None,
        )
        dk_ref[part, :] = grad_keys[0].astype(BF16)
        dv_ref[part, :] = grad_values[0].astype(BF16)
        total = tuple(a + b for a, b in zip(total, more))
    put_queries(total, 2, 1, scale, dq_ref)


def cross_backward(q, k, v, bias, grad, mix, logs, scale):
    rows, width = q.shape
    keys = k.shape[0]
    groups = width // LANES
    part = pl.BlockSpec((rows, LANES), lambda g: (0, g))
    side = pl.BlockSpec((keys, LANES), lambda g: (0, g))
    return pl.pallas_call(
        functools.partial(cross_backward_kernel, scale=scale),
        grid=(groups,),
        in_specs=[
            part,
            side,
            side,
            pl.BlockSpec((keys, LANES), lambda g: (0, 0)),
            part,
            part,
            pl.BlockSpec((8, rows), lambda g: (g, 0)),
        ],
        out_specs=[part, side, side],
        out_shape=[
            jax.ShapeDtypeStruct((rows, width), BF16),
            jax.ShapeDtypeStruct((keys, width), BF16),
            jax.ShapeDtypeStruct((keys, width), BF16),
        ],
        compiler_params=pltpu.CompilerParams(vmem_limit_bytes=VMEM_LIMIT),
        cost_estimate=pl.CostEstimate(
            flops=rows * keys * width * 40,
            bytes_accessed=rows * width * 8 + keys * width * 8,
            transcendentals=rows * keys * groups * 2,
        ),
    )(q, k, v, bias, grad, mix, logs)


def gelu_exact(values):
    return jax.nn.gelu(values, approximate=False)


def norm_parts(values):
    center = values - jnp.mean(values, axis=-1, keepdims=True)
    inverse = lax.rsqrt(jnp.mean(center * center, axis=-1, keepdims=True) + EPS)
    return center * inverse, inverse


def layer_norm(values, gain, shift):
    return norm_parts(values)[0] * gain + shift


def norm_back(pre_sum, gain, grad_out):
    normed, inverse = norm_parts(pre_sum)
    grad_normed = grad_out * gain
    grad_pre = inverse * (
        grad_normed
        - jnp.mean(grad_normed, axis=-1, keepdims=True)
        - normed * jnp.mean(grad_normed * normed, axis=-1, keepdims=True)
    )
    return grad_pre, jnp.sum(grad_out * normed, axis=0), jnp.sum(grad_out, axis=0)


def closure_of(parent_row):
    count = parent_row.shape[0]
    labels = jnp.arange(count, dtype=jnp.int32)
    closure = (parent_row[:, None] == labels[None, :]).astype(F32)
    for _ in range(max(1, count.bit_length())):
        closure = jnp.minimum(closure + nn(closure, closure), 1.0)
    return closure


def pick(a, index, dim):
    return lax.dynamic_index_in_dim(a, index, dim, keepdims=False)


def local(sizes, *args):
    (
        layer_input,
        encoder_out,
        enc_length,
        parent_ids,
        token_segment,
        self_query,
        self_key,
        self_value,
        self_output,
        cross_query,
        cross_key,
        cross_value,
        cross_output,
        ffn_up,
        ffn_down,
        self_qbias,
        self_vbias,
        self_obias,
        cross_qbias,
        cross_vbias,
        cross_obias,
        ffn_upbias,
        ffn_downbias,
        norm1_gain,
        norm1_shift,
        norm2_gain,
        norm2_shift,
        norm3_gain,
        norm3_shift,
        out_grad,
    ) = args
    place = {axis: lax.axis_index(axis) for axis in sizes}
    shards, ctxs, tensors = sizes["shard"], sizes["ctx"], sizes["tensor"]
    me_ctx, me_tensor = place["ctx"], place["tensor"]
    scale = HEAD_DIM ** (-0.5)

    def bits_of(axis):
        return [1 << k for k in reversed(range(sizes[axis].bit_length() - 1))]

    def swap(a, axis, bit):
        return lax.ppermute(a, axis, [(i, i ^ bit) for i in range(sizes[axis])])

    def is_high(axis, bit):
        return (place[axis] & bit) != 0

    def grow(a, axis, bit, dim):
        other = swap(a, axis, bit)
        high = is_high(axis, bit)
        return jnp.concatenate([jnp.where(high, other, a), jnp.where(high, a, other)], axis=dim)

    row_dims = [("shard", bit) for bit in bits_of("shard")] + [
        ("ctx", bit) for bit in bits_of("ctx")
    ]
    outer = [d for d in row_dims if d != ("shard", 1)]
    shard_outer = [d for d in outer if d[0] == "shard"]
    ctx_dims = [d for d in outer if d[0] == "ctx"]
    ctx_first = ctx_dims + shard_outer
    shard_first = shard_outer + ctx_dims

    def climb(a, order, dims):
        rows, width = a.shape
        a = a.reshape((1,) * len(dims) + (rows, width))
        for axis, bit in order:
            a = grow(a, axis, bit, dims.index((axis, bit)))
        return a.reshape(-1, width)

    def spread(pieces, order):
        packed = jnp.concatenate(pieces, axis=1)
        share = packed.shape[0] // ctxs
        mine = lax.dynamic_slice_in_dim(packed, me_ctx * share, share, 0)
        parts = [mine] + [swap(mine, "tensor", j) for j in range(1, tensors)]
        columns, start = [], 0
        for piece in pieces:
            columns += [part[:, start : start + piece.shape[1]] for part in parts]
            start += piece.shape[1]
        whole = climb(jnp.concatenate(columns, axis=1), order + [("shard", 1)], row_dims)
        out, start = [], 0
        for piece in pieces:
            out.append(whole[:, start : start + tensors * piece.shape[1]])
            start += tensors * piece.shape[1]
        return out

    def reduce_rows(sides, order):
        core = place["shard"] & 1
        kept, sent = [], []
        for left, right in sides:
            left = left.reshape(left.shape[0], shards // 2, 2, -1)
            near = pick(left, core, 2).reshape(left.shape[0], -1)
            away = pick(left, 1 - core, 2).reshape(left.shape[0], -1)
            sent.append(tn(away, right).astype(BF16))
            kept.append(tn(near, right))
        arrived = swap(jnp.concatenate(sent, axis=1), "shard", 1)
        total = (jnp.concatenate(kept, axis=1) + arrived.astype(F32)).astype(BF16)
        dims = list(outer)
        width = total.shape[1]
        total = total.reshape((2,) * len(dims) + (-1, width))
        for axis, bit in reversed(order):
            dim = dims.index((axis, bit))
            at = is_high(axis, bit).astype(jnp.int32)
            arrived = swap(pick(total, 1 - at, dim), axis, bit)
            total = (pick(total, at, dim).astype(F32) + arrived.astype(F32)).astype(BF16)
            del dims[dim]
        return total

    def finish_rows(total, widths):
        whole = climb(total.astype(BF16), ctx_dims, ctx_dims).astype(F32)
        out, start = [], 0
        for width in widths:
            out.append(whole[:, start : start + width])
            start += width
        return out

    def collect(sides, order):
        total = reduce_rows(sides, order)
        widths = [right.shape[1] // tensors for _, right in sides]

        def block(j):
            parts, start = [], 0
            for width in widths:
                parts.append(total[:, start + j * width : start + (j + 1) * width])
                start += tensors * width
            return jnp.concatenate(parts, axis=1)

        mine = block(0).astype(F32)
        for j in range(1, tensors):
            mine = mine + swap(block(j), "tensor", j).astype(F32)
        return finish_rows(mine, widths)

    def spread_vector(vector):
        return jnp.concatenate(
            [vector] + [swap(vector, "tensor", j) for j in range(1, tensors)], axis=0
        )

    def by_tensor(parts):
        stacked = jnp.stack(parts)
        return jnp.concatenate([pick(stacked, me_tensor ^ i, 0) for i in range(tensors)], axis=0)

    def gather_rows(rows):
        return by_tensor([rows] + [swap(rows, "tensor", j) for j in range(1, tensors)])

    local_rows, model_width = layer_input.shape[1:]
    head_columns = self_query.shape[1]
    heads = head_columns // HEAD_DIM
    padded = -(-head_columns // LANES) * LANES
    pad = padded - head_columns
    quarter = local_rows // tensors
    seg_count = parent_ids.shape[1]
    seg = token_segment.shape[1] // seg_count
    blocks = local_rows // TILE

    qkv_piece = jnp.concatenate([self_query, self_key, self_value], axis=1)
    shard_dims = [("shard", bit) for bit in bits_of("shard")]
    qkv_weights = climb(qkv_piece, shard_dims, shard_dims)
    zeros = jnp.zeros((model_width, pad), BF16)
    qkv_weights = jnp.concatenate(
        [
            part
            for i in range(3)
            for part in (qkv_weights[:, i * head_columns : (i + 1) * head_columns], zeros)
        ],
        axis=1,
    )
    enc_low = climb(encoder_out[0].astype(BF16), ctx_dims, ctx_dims)
    weight_ck, weight_cv = spread([cross_key, cross_value], shard_first)
    weight_o, weight_cq = spread([self_output.T, cross_query], ctx_first)
    weight_co, weight_up = spread([cross_output.T, ffn_up], shard_first)
    (weight_down,) = spread([ffn_down.T], ctx_first)
    bias_all = spread_vector(jnp.concatenate([cross_qbias, cross_vbias, ffn_upbias]))
    bias_all = bias_all.reshape(tensors, -1)
    cq_bias = bias_all[:, :head_columns].reshape(-1)
    cv_bias = bias_all[:, head_columns : 2 * head_columns].reshape(-1)
    up_bias = bias_all[:, 2 * head_columns :].reshape(-1)

    block_label = token_segment[0].reshape(seg_count, seg)[:, 0]
    closure = closure_of(parent_ids[0])
    hot = (block_label[:, None] == jnp.arange(seg_count)[None, :]).astype(F32)
    ancestor = nt(nn(hot, closure), hot) > 0.5
    seg_bias = jnp.where(ancestor, 0.0, NEG)
    own_segs = local_rows // seg
    mine = lax.dynamic_slice_in_dim(seg_bias, me_ctx * own_segs, own_segs, 0)
    own = lax.dynamic_slice_in_dim(mine, me_ctx * own_segs, own_segs, 1)
    own = jnp.where(jnp.eye(own_segs, dtype=bool), 0.0, own)
    per = TILE // seg
    own = jnp.stack([own[b * per : (b + 1) * per, b * per : (b + 1) * per] for b in range(blocks)])
    trunk_bias = mine[:, :own_segs].reshape(blocks, per, own_segs)
    seg_rows = jnp.swapaxes(jnp.concatenate([trunk_bias, own], axis=2), 1, 2)
    seg_rows = jnp.pad(seg_rows, ((0, 0), (0, 0), (0, HEAD_DIM - per))).astype(BF16)
    seg_rows = jnp.concatenate([seg_rows, seg_rows], axis=2)
    self_bias = jnp.repeat(seg_rows, seg, axis=1)
    counts = jnp.where(me_ctx == 0, jnp.arange(blocks, dtype=jnp.int32), blocks).astype(jnp.int32)
    enc_total = enc_low.shape[0]
    lane = jnp.arange(LANES) % HEAD_DIM
    cross_bias = jnp.where(
        (jnp.arange(enc_total)[:, None] >= enc_length[0]) & (lane[None, :] == 0), NEG, 0.0
    ).astype(BF16)

    input_low = layer_input[0].astype(BF16)
    gap = jnp.zeros((pad,), F32)
    none = jnp.zeros((padded,), F32)
    qkv_bias = jnp.concatenate([self_qbias, gap, none, self_vbias, gap])
    qkv_scale = jnp.concatenate([none + scale, none + 1.0, none + 1.0])
    qkv = ((nn(input_low, qkv_weights) + qkv_bias) * qkv_scale).astype(BF16)
    own_kv = qkv[:, padded:]
    sent_kv = lax.ppermute(own_kv, "ctx", [(0, 1)])
    trunk = jnp.where(me_ctx == 0, own_kv, sent_kv)
    mix, self_logs = self_forward(counts, qkv, trunk, self_bias, heads, seg)

    def row_part(a, index):
        return lax.dynamic_slice_in_dim(a, index * quarter, quarter, 0)

    def to_rows(a):
        parts = [row_part(a, me_tensor)] + [
            swap(row_part(a, me_tensor ^ j), "tensor", j) for j in range(1, tensors)
        ]
        return jnp.concatenate(parts, axis=1)

    def to_heads(a):
        width = a.shape[1] // tensors
        parts = [a[:, j * width : (j + 1) * width] for j in range(tensors)]
        return by_tensor(parts[:1] + [swap(parts[j], "tensor", j) for j in range(1, tensors)])

    mix_rows = to_rows(mix[:, :head_columns])
    sum_one = row_part(layer_input[0], me_tensor) + nt(mix_rows, weight_o) + self_obias
    hidden_one = layer_norm(sum_one, norm1_gain, norm1_shift)
    one_low = hidden_one.astype(BF16)

    cq = ((nn(one_low, weight_cq) + cq_bias) * scale).astype(BF16)
    ck = nn(enc_low, weight_ck).astype(BF16)
    cv = (nn(enc_low, weight_cv) + cv_bias).astype(BF16)
    cross_mix, cross_logs = cross_forward(cq, ck, cv, cross_bias)
    sum_two = hidden_one + nt(cross_mix, weight_co) + cross_obias
    hidden_two = layer_norm(sum_two, norm2_gain, norm2_shift)
    two_low = hidden_two.astype(BF16)

    pre = nn(two_low, weight_up) + up_bias
    act = gelu_exact(pre).astype(BF16)
    sum_three = hidden_two + nt(act, weight_down) + ffn_downbias
    result = layer_norm(sum_three, norm3_gain, norm3_shift)
    result_all = gather_rows(result.astype(BF16)).astype(F32)

    grad_three, gain3, shift3 = norm_back(sum_three, norm3_gain, row_part(out_grad[0], me_tensor))
    downbias = jnp.sum(grad_three, axis=0)
    three_low = grad_three.astype(BF16)
    (grad_down,) = collect([(three_low, act)], ctx_first)
    grad_act = nn(three_low, weight_down)
    grad_pre = jax.vjp(gelu_exact, pre)[1](grad_act)[0]
    upbias = jnp.sum(grad_pre, axis=0)
    pre_low = grad_pre.astype(BF16)
    (grad_up,) = collect([(two_low, pre_low)], shard_first)
    grad_hidden_two = grad_three + nt(pre_low, weight_up)

    grad_two, gain2, shift2 = norm_back(sum_two, norm2_gain, grad_hidden_two)
    cobias = jnp.sum(grad_two, axis=0)
    two_grad_low = grad_two.astype(BF16)
    grad_cmix = nn(two_grad_low, weight_co).astype(BF16)
    dcq, dck, dcv = cross_backward(cq, ck, cv, cross_bias, grad_cmix, cross_mix, cross_logs, scale)
    cqbias = jnp.sum(dcq.astype(F32), axis=0)
    cvbias = jnp.sum(dcv.astype(F32), axis=0)
    grad_co, grad_cq, grad_ck, grad_cv = collect(
        [(two_grad_low, cross_mix), (one_low, dcq), (enc_low, dck), (enc_low, dcv)], ctx_first
    )
    enc_part = nt(dck, weight_ck) + nt(dcv, weight_cv)
    enc_half = enc_part.reshape(ctxs, -1, model_width)
    arrived = swap(pick(enc_half, 1 - me_ctx, 0).astype(BF16), "ctx", 1)
    enc_half = (pick(enc_half, me_ctx, 0) + arrived.astype(F32)).astype(BF16)
    enc_share = enc_half.shape[0] // tensors
    enc_mine = lax.dynamic_slice_in_dim(enc_half, me_tensor * enc_share, enc_share, 0).astype(F32)
    for j in range(1, tensors):
        away = lax.dynamic_slice_in_dim(enc_half, (me_tensor ^ j) * enc_share, enc_share, 0)
        enc_mine = enc_mine + swap(away, "tensor", j).astype(F32)
    grad_encoder = gather_rows(enc_mine.astype(BF16)).astype(F32)
    grad_hidden_one = grad_two + nt(dcq, weight_cq)

    grad_one, gain1, shift1 = norm_back(sum_one, norm1_gain, grad_hidden_one)
    obias = jnp.sum(grad_one, axis=0)
    one_grad_low = grad_one.astype(BF16)
    grad_smix = to_heads(nn(one_grad_low, weight_o).astype(BF16))
    grad_smix = jnp.pad(grad_smix, ((0, 0), (0, pad)))
    (grad_o,) = collect([(one_grad_low, mix_rows)], shard_first)
    dq, dk, dv, dtrunk = self_backward(
        counts, qkv, trunk, self_bias, grad_smix, mix, self_logs, heads, seg, scale
    )
    arrived = lax.ppermute(dtrunk.astype(BF16), "ctx", [(1, 0)]).astype(F32)
    dkv = jnp.concatenate([dk, dv], axis=1) + jnp.where(me_ctx == 0, dtrunk + arrived, 0.0)
    dqkv = jnp.concatenate([dq, dkv.astype(BF16)], axis=1)
    part = nt(dqkv, qkv_weights)
    part_low = part.astype(BF16)
    input_mine = grad_one + row_part(part, me_tensor)
    for j in range(1, tensors):
        input_mine = input_mine + swap(row_part(part_low, me_tensor ^ j), "tensor", j).astype(F32)
    grad_input = gather_rows(input_mine.astype(BF16)).astype(F32)
    packed = jnp.concatenate(
        [dqkv[:, i * padded : i * padded + head_columns] for i in range(3)], axis=1
    )
    grad_q, grad_k, grad_v = finish_rows(
        reduce_rows([(input_low, packed)], ctx_first), [head_columns] * 3
    )
    qkv_sums = jnp.sum(packed.astype(F32), axis=0)

    every = jnp.concatenate(
        [obias, cobias, downbias, gain1, shift1, gain2, shift2, gain3, shift3]
    )
    rel = jnp.concatenate(
        [cqbias.reshape(tensors, -1), cvbias.reshape(tensors, -1), upbias.reshape(tensors, -1)],
        axis=1,
    )
    sums = jnp.concatenate([every, rel[0]])
    for j in range(1, tensors):
        sums = sums + swap(jnp.concatenate([every, rel[j]]), "tensor", j)
    sums = jnp.concatenate([sums, qkv_sums])
    for axis, bit in row_dims:
        sums = sums + swap(sums, axis, bit)

    def cut(index):
        return sums[index * model_width : (index + 1) * model_width]

    tail = sums[9 * model_width :]
    sizes_tail = [head_columns, head_columns, ffn_upbias.shape[0]] + [head_columns] * 3
    tails, start = [], 0
    for size in sizes_tail:
        tails.append(tail[start : start + size])
        start += size
    cq_sum, cv_sum, up_sum, q_sum, _, v_sum = tails

    return (
        result_all[None],
        grad_input[None],
        grad_encoder[None],
        grad_q,
        grad_k,
        grad_v,
        grad_o.T,
        grad_cq,
        grad_ck,
        grad_cv,
        grad_co.T,
        grad_up,
        grad_down.T,
        q_sum,
        v_sum,
        cut(0),
        cq_sum,
        cv_sum,
        cut(1),
        up_sum,
        cut(2),
        cut(3),
        cut(4),
        cut(5),
        cut(6),
        cut(7),
        cut(8),
    )


def solution(mesh):
    sizes = {axis: mesh.shape[axis] for axis in ("shard", "ctx", "tensor")}
    rows = P("shard", "ctx", None)
    tall, wide = P("shard", "tensor"), P("tensor", "shard")
    mats = (tall, tall, tall, wide, tall, tall, tall, wide, tall, wide)
    part = P("tensor")
    vectors = (part, part, P(), part, part, P(), part) + (P(),) * 7
    tree = P("shard", None)
    return jax.shard_map(
        functools.partial(local, sizes),
        mesh=mesh,
        in_specs=(rows, rows, P("shard"), tree, tree) + mats + vectors + (rows,),
        out_specs=(rows, rows, rows) + mats + vectors,
        check_vma=False,
    )
```

time: 1330 us -> 681 us (0.51)
  waiting for transfers between devices: 849 us -> 239 us
  blocking collectives: 117 us -> 0 us
  starting transfers between devices: 2.5 us -> 115 us
  matrix products: 172 us -> 66.8 us
  Pallas kernels: 0 us -> 61.1 us
  local copies, waits for them, and re-layouts: 61 us -> 107 us
  other arithmetic: 97.7 us -> 77.7 us
  between operations: 18.5 us -> 4.13 us
    psum x8 -> x0, waiting for transfers between devices: 645 us -> none  [the longest x3 331 us: reduce_input(): return lax.psum(term_part, 'tensor')]
    ppermute x0 -> x92, waiting for transfers between devices: none -> 239 us  [the longest x90 237 us: swap(): return lax.ppermute(a, axis, [(i, i ^ bit) for i in range(sizes[axis])])]
    unnamed x31 -> x0, waiting for transfers between devices: 125 us -> none
    ppermute x0 -> x92, starting transfers between devices: none -> 115 us  [the longest x90 110 us: swap(): return lax.ppermute(a, axis, [(i, i ^ bit) for i in range(sizes[axis])])]
    dot_general x63 -> x38, matrix products: 172 us -> 66.8 us  [dot_of(): lax.dot_general(a, b, (((a_dim,), (b_dim,)), ((), ())), preferred_element...]
    all_gather x12 -> x0, blocking collectives: 92.7 us -> none  [the longest x1 12.1 us: local(): lax.all_gather(value_self.reshape(number_of_trees, local_rows, head_colum...]
    reduce_scatter x7 -> x0, waiting for transfers between devices: 79.6 us -> none  [the longest x1 29 us: local(): lax.psum_scatter(up_grad.astype(jnp.bfloat16), 'shard', scatter_dimension...]
    pallas_call x0 -> x4, Pallas kernels: none -> 61.1 us  [the longest x1 17.4 us: cross_forward(): pl.pallas_call(cross_forward_kernel, grid=(groups,), in_specs=[part, side...]
  transfers between devices with their start and end apart: 24 -> 92, of which waited for: 16 -> 38; matrix products, arithmetic and copies ran while one was open for 14% -> 27% of each run, Pallas kernels for 0% -> 7%
where the time goes in v1:
time: 681 us; the launch traced here: 671 us
  waiting for transfers between devices  239 us (35%)
  starting transfers between devices  115 us (17%)
  local copies, waits for them, and re-layouts  107 us (16%)
  other arithmetic  77.7 us (11%)
  matrix products  66.8 us (10%)
  Pallas kernels  61.1 us (9%)
    ppermute x90, waiting for transfers between devices, swap(): return lax.ppermute(a, axis, [(i, i ^ bit) for i in range(sizes[axis])])  237 us
    ppermute x90, starting transfers between devices, swap(): return lax.ppermute(a, axis, [(i, i ^ bit) for i in range(sizes[axis])])  110 us
    dot_general x38, matrix products, dot_of(): lax.dot_general(a, b, (((a_dim,), (b_dim,)), ((), ())), preferred_element...  66.8 us
    unnamed x238, local copies, waits for them, and re-layouts  30.5 us
    select_n x20, other arithmetic, grow(): jnp.where(high, other, a)  19.8 us
    pallas_call x1, Pallas kernels, cross_forward(): pl.pallas_call(cross_forward_kernel, grid=(groups,), in_specs=[part, side...  17.4 us
    pallas_call x1, Pallas kernels, cross_backward(): pl.pallas_call(functools.partial(cross_backward_kernel, scale=scale), gri...  15.5 us
    pallas_call x1, Pallas kernels, self_backward(): pl.pallas_call(functools.partial(self_backward_kernel, heads=heads, seg=s...  14.5 us
  transfers between devices with their start and end apart: 92, of which 38 were waited for; matrix products, arithmetic and copies ran while one was open for 27% of the time, Pallas kernels for 7%

profile of v1, /device:TPU:8, one launch (start us, length us, event | category | flops | bytes accessed | tf_op | source)
XLA Modules:
  0.0 670.7 jit_solution(15637918993572148661)
XLA Ops:
  1.7 3.0 collective-permute-start.29
  12.9 2.2 copy.103
  33.3 2.9 collective-permute-start.18
  47.3 4.6 collective-permute-done.17
  53.2 3.3 collective-permute-done.16
  57.2 5.2 collective-permute-done.8
  64.1 3.9 collective-permute-done.7
  72.3 3.4 collective-permute-done.6
  79.1 3.9 collective-permute-start.24
  111.3 3.5 concatenate.193
  114.8 2.7 fusion.24.q_ref.k_ref.v_ref
  118.7 3.4 collective-permute-start.2
  127.5 3.2 copy.114
  130.7 2.8 reshape_reshape.4
  143.9 2.5 collective-permute-done.2
  148.7 13.6 %shard_map.493 = (bf16[1024,256]{1,0:T(8,128)(2,1)}, f32[8,1024]{1,0:T(8,128)}) custom-call(s32[4]{0:T(128)} %broadcast_select_fusion.41.count_ref, bf16[1024,768]{1,0:T(8,128)(2,1)} %copy-done.30, bf16[1024,768]{1,0:T(8,128)(2,1)} %copy-done.30, bf16[1024,768]{1,0:T(8,128)(2,1)} %copy-done.30, bf16[1024,512]{1,0:T(8,128)(2,1)} %broadcast_select_fusion.12.trunk_ref, ...), custom_call_target="tpu_custom_call" | custom-call | flops 4026531840 | bytes 4194304 | tf_op jit(solution)/shard_map/pallas_call | solution.py:155
  163.4 2.9 collective-permute-start.3
  173.1 3.7 collective-permute-done.5
  189.6 2.5 convolution_convert_fusion.2.k_ref
  192.2 2.6 add_convert_fusion.2.v_ref
  194.7 17.4 %shard_map.494 = (bf16[256,768]{1,0:T(8,128)(2,1)}, f32[48,256]{1,0:T(8,128)}) custom-call(bf16[256,768]{1,0:T(8,128)(2,1)} %fusion.64.q_ref, bf16[1024,768]{1,0:T(8,128)(2,1)} %convolution_convert_fusion.2.k_ref, bf16[1024,768]{1,0:T(8,128)(2,1)} %add_convert_fusion.2.v_ref, bf16[1024,128]{1,0:T(8,128)(2,1)} %select_convert_fusion.bias_ref), custom_call_target="tpu_custom_call" | custom-call | flops 3221225472 | bytes 3932160 | tf_op jit(solution)/shard_map/pallas_call | solution.py:375
  214.1 2.5 pad_maximum_fusion.1
  216.7 2.5 broadcast_select_fusion.1
  221.3 9.5 %multiply_convert_fusion = (bf16[256,3072]{1,0:T(8,128)(2,1)S(1)}, f32[256,3072]{1,0:T(8,128)S(1)}, f32[256,3072]{1,0:T(8,128)S(1)}) fusion(f32[3072]{0:T(1024)S(1)} %copy-done.85, bf16[256,768]{1,0:T(8,128)(2,1)S(1)} %fusion.72, bf16[768,3840]{1,0:T(8,128)(2,1)S(1)} %bitcast.278), kind=kOutput, calls=%fused_computation.17 | convolution fusion | flops 1259864064 | bytes 12988416 | tf_op jit(solution)/shard_map/dot_general | solution.py:21
  234.9 3.1 fusion.105
  238.0 2.2 multiply_reduce_fusion
  242.4 15.5 %shard_map.495 = (bf16[256,768]{1,0:T(8,128)(2,1)}, bf16[1024,768]{1,0:T(8,128)(2,1)}, bf16[1024,768]{1,0:T(8,128)(2,1)}) custom-call(bf16[256,768]{1,0:T(8,128)(2,1)} %fusion.64.q_ref, bf16[1024,768]{1,0:T(8,128)(2,1)} %convolution_convert_fusion.2.k_ref, bf16[1024,768]{1,0:T(8,128)(2,1)} %add_convert_fusion.2.v_ref, ...), custom_call_target="tpu_custom_call" | custom-call | flops 8053063680 | bytes 7864320 | tf_op jit(solution)/shard_map/pallas_call | solution.py:428
  259.6 3.1 multiply_reduce_fusion.1
  266.8 2.3 convert_reduce_fusion
  269.1 3.1 convolution_convert_fusion.3
  283.2 4.4 fusion.50
  315.2 2.2 convolution_convert_fusion
  318.1 2.3 convolution_convert_fusion.1
  328.9 3.0 collective-permute-start.37
  333.4 2.5 collective-permute-done.37
  336.1 12.5 %collective-permute-done.38 = bf16[256,192]{1,0:T(8,128)(2,1)S(1)} collective-permute-done((bf16[256,192]{1,0:T(8,128)(2,1)S(1)}, bf16[256,192]{1,0:T(8,128)(2,1)S(1)}, u32[]{:S(2)}, u32[]{:S(2)}) %collective-permute-start.38) | collective-permute-done | bytes 98336 | tf_op jit(solution)/shard_map/ppermute | solution.py:535
  348.6 5.2 collective-permute-done.39
  355.0 14.5 %shard_map.496 = (bf16[1024,256]{1,0:T(8,128)(2,1)}, f32[1024,256]{1,0:T(8,128)}, f32[1024,256]{1,0:T(8,128)}, f32[1024,512]{1,0:T(8,128)}) custom-call(s32[4]{0:T(128)} %broadcast_select_fusion.41.count_ref, bf16[1024,768]{1,0:T(8,128)(2,1)} %copy-done.30, bf16[1024,768]{1,0:T(8,128)(2,1)} %copy-done.30, bf16[1024,768]{1,0:T(8,128)(2,1)} %copy-done.30, ...), custom_call_target="tpu_custom_call" | custom-call | flops 10066329600 | bytes 9437184 | tf_op jit(solution)/shard_map/pallas_call | solution.py:324
  369.5 2.7 convert_element_type.455
  372.2 22.8 %collective-permute-start.47 = (bf16[512,768]{1,0:T(8,128)(2,1)S(1)}, bf16[512,768]{1,0:T(8,128)(2,1)S(1)}, u32[]{:S(2)}, u32[]{:S(2)}) collective-permute-start(bf16[512,768]{1,0:T(8,128)(2,1)S(1)} %fusion.69), channel_id=1, source_target_pairs={{0,4},{4,0},{1,5},{5,1},{2,6},{6,2},{3,7},{7,3},{8,12},{12,8},{9,1... | collective-permute-start | bytes 2359304 | tf_op jit(solution)/shard_map/ppermute | solution.py:535
  399.4 3.7 collective-permute-start.59
  405.1 36.8 %collective-permute-done.59 = bf16[2,96,768]{2,1,0:T(8,128)(2,1)S(1)} collective-permute-done((bf16[2,96,768]{2,1,0:T(8,128)(2,1)S(1)}, bf16[2,96,768]{2,1,0:T(8,128)(2,1)S(1)}, u32[]{:S(2)}, u32[]{:S(2)}) %collective-permute-start.59) | collective-permute-done | bytes 294944 | tf_op jit(solution)/shard_map/ppermute | solution.py:535
  443.8 4.0 collective-permute-done.60
  456.9 3.3 collective-permute-done.48
  460.2 7.8 %collective-permute-done.49 = bf16[128,768]{1,0:T(8,128)(2,1)S(1)} collective-permute-done((bf16[128,768]{1,0:T(8,128)(2,1)S(1)}, bf16[128,768]{1,0:T(8,128)(2,1)S(1)}, u32[]{:S(2)}, u32[]{:S(2)}) %collective-permute-start.49) | collective-permute-done | bytes 196640 | tf_op jit(solution)/shard_map/ppermute | solution.py:535
  468.0 3.9 collective-permute-done.50
  472.1 2.3 collective-permute-start.52
  478.1 2.5 fusion.17
  480.7 3.1 fusion.131
  494.7 2.7 collective-permute-done.91
  502.1 4.9 collective-permute-done.55
  507.4 10.2 %collective-permute-done.42 = bf16[256,768]{1,0:T(8,128)(2,1)} collective-permute-done((bf16[256,768]{1,0:T(8,128)(2,1)}, bf16[256,768]{1,0:T(8,128)(2,1)}, u32[]{:S(2)}, u32[]{:S(2)}) %collective-permute-start.42) | collective-permute-done | bytes 393248 | tf_op jit(solution)/shard_map/ppermute | solution.py:535
  517.6 8.8 %collective-permute-done.43 = bf16[256,768]{1,0:T(8,128)(2,1)} collective-permute-done((bf16[256,768]{1,0:T(8,128)(2,1)}, bf16[256,768]{1,0:T(8,128)(2,1)}, u32[]{:S(2)}, u32[]{:S(2)}) %collective-permute-start.43) | collective-permute-done | bytes 393248 | tf_op jit(solution)/shard_map/ppermute | solution.py:535
  528.2 2.3 collective-permute-start.45
  532.4 10.6 %collective-permute-done.44 = bf16[256,768]{1,0:T(8,128)(2,1)S(1)} collective-permute-done((bf16[256,768]{1,0:T(8,128)(2,1)S(1)}, bf16[256,768]{1,0:T(8,128)(2,1)S(1)}, u32[]{:S(2)}, u32[]{:S(2)}) %collective-permute-start.44) | collective-permute-done | bytes 393248 | tf_op jit(solution)/shard_map/ppermute | solution.py:535
  543.0 13.9 %collective-permute-done.45 = bf16[256,768]{1,0:T(8,128)(2,1)S(1)} collective-permute-done((bf16[256,768]{1,0:T(8,128)(2,1)S(1)}, bf16[256,768]{1,0:T(8,128)(2,1)S(1)}, u32[]{:S(2)}, u32[]{:S(2)}) %collective-permute-start.45) | collective-permute-done | bytes 393248 | tf_op jit(solution)/shard_map/ppermute | solution.py:535
  557.0 7.9 %collective-permute-done.46 = bf16[256,768]{1,0:T(8,128)(2,1)S(1)} collective-permute-done((bf16[256,768]{1,0:T(8,128)(2,1)S(1)}, bf16[256,768]{1,0:T(8,128)(2,1)S(1)}, u32[]{:S(2)}, u32[]{:S(2)}) %collective-permute-start.46) | collective-permute-done | bytes 393248 | tf_op jit(solution)/shard_map/ppermute | solution.py:535
  568.8 2.5 add_convert_fusion
  576.8 23.6 %collective-permute-done.80 = bf16[2,96,3072]{2,1,0:T(8,128)(2,1)S(1)} collective-permute-done((bf16[2,96,3072]{2,1,0:T(8,128)(2,1)S(1)}, bf16[2,96,3072]{2,1,0:T(8,128)(2,1)S(1)}, u32[]{:S(2)}, u32[]{:S(2)}) %collective-permute-start.80) | collective-permute-done | bytes 1179680 | tf_op jit(solution)/shard_map/ppermute | solution.py:535
  602.6 23.0 %collective-permute-done.66 = bf16[2,96,3072]{2,1,0:T(8,128)(2,1)S(1)} collective-permute-done((bf16[2,96,3072]{2,1,0:T(8,128)(2,1)S(1)}, bf16[2,96,3072]{2,1,0:T(8,128)(2,1)S(1)}, u32[]{:S(2)}, u32[]{:S(2)}) %collective-permute-start.66) | collective-permute-done | bytes 1179680 | tf_op jit(solution)/shard_map/ppermute | solution.py:535
  629.9 5.3 collective-permute-done.74
  643.7 9.8 %collective-permute-done.76 = bf16[96,768]{1,0:T(8,128)(2,1)S(1)} collective-permute-done((bf16[96,768]{1,0:T(8,128)(2,1)S(1)}, bf16[96,768]{1,0:T(8,128)(2,1)S(1)}, u32[]{:S(2)}, u32[]{:S(2)}) %collective-permute-start.76) | collective-permute-done | bytes 147488 | tf_op jit(solution)/shard_map/ppermute | solution.py:535
  653.5 4.7 collective-permute-done.77
  658.3 3.4 collective-permute-start.78
  (620 shorter events, 256.1 us)
Async XLA Ops:
  1.7 77.5 %collective-permute-start.28 = (bf16[96,768]{1,0:T(8,128)(2,1)S(1)}, bf16[96,768]{1,0:T(8,128)(2,1)}, u32[]{:S(2)}, u32[]{:S(2)}) collective-permute-start(bf16[96,768]{1,0:T(8,128)(2,1)S(1)} %dynamic-slice_bitcast_fusion.9), channel_id=1, source_target_pairs={{0,1},{1,0},{2,3},{3,2},{4,5},{5,4},{6,7},{7,6},{8,9},{9,8},{10,11... | collective-permute-start | bytes 442376 | tf_op jit(solution)/shard_map/ppermute | solution.py:535
  1.7 81.3 %collective-permute-start.29 = (bf16[96,768]{1,0:T(8,128)(2,1)S(1)}, bf16[96,768]{1,0:T(8,128)(2,1)}, u32[]{:S(2)}, u32[]{:S(2)}) collective-permute-start(bf16[96,768]{1,0:T(8,128)(2,1)S(1)} %dynamic-slice_bitcast_fusion.9), channel_id=1, source_target_pairs={{0,2},{1,3},{2,0},{3,1},{4,6},{5,7},{6,4},{7,5},{8,10},{9,11},{10,... | collective-permute-start | bytes 442376 | tf_op jit(solution)/shard_map/ppermute | solution.py:535
  6.1 24.6 %collective-permute-start.12 = (f32[1152]{0:T(1024)}, f32[1152]{0:T(1024)}, u32[]{:S(2)}, u32[]{:S(2)}) collective-permute-start(f32[1152]{0:T(1024)} %concatenate.203), channel_id=1, source_target_pairs={{0,1},{1,0},{2,3},{3,2},{4,5},{5,4},{6,7},{7,6},{8,9},{9,8},{10,11... | collective-permute-start | bytes 13832 | tf_op jit(solution)/shard_map/ppermute | solution.py:535
  7.7 23.5 %collective-permute-start.13 = (f32[1152]{0:T(1024)}, f32[1152]{0:T(1024)}, u32[]{:S(2)}, u32[]{:S(2)}) collective-permute-start(f32[1152]{0:T(1024)} %concatenate.203), channel_id=1, source_target_pairs={{0,2},{1,3},{2,0},{3,1},{4,6},{5,7},{6,4},{7,5},{8,10},{9,11},{10,... | collective-permute-start | bytes 13832 | tf_op jit(solution)/shard_map/ppermute | solution.py:535
  8.1 25.2 %collective-permute-start.14 = (f32[1152]{0:T(1024)}, f32[1152]{0:T(1024)}, u32[]{:S(2)}, u32[]{:S(2)}) collective-permute-start(f32[1152]{0:T(1024)} %concatenate.203), channel_id=1, source_target_pairs={{0,3},{1,2},{2,1},{3,0},{4,7},{5,6},{6,5},{7,4},{8,11},{9,10},{10,... | collective-permute-start | bytes 13832 | tf_op jit(solution)/shard_map/ppermute | solution.py:535
  30.7 53.8 %collective-permute-start.30 = (bf16[96,768]{1,0:T(8,128)(2,1)S(1)}, bf16[96,768]{1,0:T(8,128)(2,1)}, u32[]{:S(2)}, u32[]{:S(2)}) collective-permute-start(bf16[96,768]{1,0:T(8,128)(2,1)S(1)} %dynamic-slice_bitcast_fusion.9), channel_id=1, source_target_pairs={{0,3},{1,2},{2,1},{3,0},{4,7},{5,6},{6,5},{7,4},{8,11},{9,10},{10,... | collective-permute-start | bytes 442376 | tf_op jit(solution)/shard_map/ppermute | solution.py:535
  31.2 56.8 %collective-permute-start.22 = (bf16[96,960]{1,0:T(8,128)(2,1)S(1)}, bf16[96,960]{1,0:T(8,128)(2,1)}, u32[]{:S(2)}, u32[]{:S(2)}) collective-permute-start(bf16[96,960]{1,0:T(8,128)(2,1)S(1)} %fusion.81), channel_id=1, source_target_pairs={{0,1},{1,0},{2,3},{3,2},{4,5},{5,4},{6,7},{7,6},{8,9},{9,8},{10,11... | collective-permute-start | bytes 552968 | tf_op jit(solution)/shard_map/ppermute | solution.py:535
  75.7 16.0 %collective-permute-start.23 = (bf16[96,960]{1,0:T(8,128)(2,1)S(1)}, bf16[96,960]{1,0:T(8,128)(2,1)}, u32[]{:S(2)}, u32[]{:S(2)}) collective-permute-start(bf16[96,960]{1,0:T(8,128)(2,1)S(1)} %fusion.81), channel_id=1, source_target_pairs={{0,2},{1,3},{2,0},{3,1},{4,6},{5,7},{6,4},{7,5},{8,10},{9,11},{10,... | collective-permute-start | bytes 552968 | tf_op jit(solution)/shard_map/ppermute | solution.py:535
  79.1 16.1 %collective-permute-start.24 = (bf16[96,960]{1,0:T(8,128)(2,1)S(1)}, bf16[96,960]{1,0:T(8,128)(2,1)S(1)}, u32[]{:S(2)}, u32[]{:S(2)}) collective-permute-start(bf16[96,960]{1,0:T(8,128)(2,1)S(1)} %fusion.81), channel_id=1, source_target_pairs={{0,3},{1,2},{2,1},{3,0},{4,7},{5,6},{6,5},{7,4},{8,11},{9,10},{10,... | collective-permute-start | bytes 552968 | tf_op jit(solution)/shard_map/ppermute | solution.py:535
  83.0 42.4 %collective-permute-start.15 = (bf16[1,512,768]{2,1,0:T(8,128)(2,1)}, bf16[1,512,768]{2,1,0:T(8,128)(2,1)}, u32[]{:S(2)}, u32[]{:S(2)}) collective-permute-start(bf16[1,512,768]{2,1,0:T(8,128)(2,1)} %convert_element_type.441), channel_id=1, source_target_pairs={{0,4},{4,0},{1,5},{5,1},{2,6},{6,2},{3,7},{7,3},{8,12},{12,8},{9,1... | collective-permute-start | bytes 2359304 | tf_op jit(solution)/shard_map/ppermute | solution.py:535
  84.6 14.4 %collective-permute-start = (bf16[1,1,192,576]{3,2,1,0:T(8,128)(2,1)}, bf16[1,1,192,576]{3,2,1,0:T(8,128)(2,1)}, u32[]{:S(2)}, u32[]{:S(2)}) collective-permute-start(bf16[1,1,192,576]{3,2,1,0:T(8,128)(2,1)} %maximum_bitcast_fusion.1), channel_id=1, source_target_pairs={{0,16},{8,24},{16,0},{24,8},{1,17},{9,25},{17,1},{25,9},{2,18},{10... | collective-permute-start | bytes 663560 | tf_op jit(solution)/shard_map/ppermute | solution.py:535
  88.0 13.8 %collective-permute-start.19 = (bf16[1,1,1,96,1536]{4,3,2,1,0:T(8,128)(2,1)}, bf16[1,1,1,96,1536]{4,3,2,1,0:T(8,128)(2,1)}, u32[]{:S(2)}, u32[]{:S(2)}) collective-permute-start(bf16[1,1,1,96,1536]{4,3,2,1,0:T(8,128)(2,1)} %bitcast.308), channel_id=1, source_target_pairs={{0,16},{8,24},{16,0},{24,8},{1,17},{9,25},{17,1},{25,9},{2,18},{10... | collective-permute-start | bytes 884744 | tf_op jit(solution)/shard_map/ppermute | solution.py:535
  91.7 12.5 %collective-permute-start.9 = (bf16[1,1,1,96,1536]{4,3,2,1,0:T(8,128)(2,1)}, bf16[1,1,1,96,1536]{4,3,2,1,0:T(8,128)(2,1)}, u32[]{:S(2)}, u32[]{:S(2)}) collective-permute-start(bf16[1,1,1,96,1536]{4,3,2,1,0:T(8,128)(2,1)} %bitcast.309), channel_id=1, source_target_pairs={{0,4},{4,0},{1,5},{5,1},{2,6},{6,2},{3,7},{7,3},{8,12},{12,8},{9,1... | collective-permute-start | bytes 884744 | tf_op jit(solution)/shard_map/ppermute | solution.py:535
  95.3 23.4 %collective-permute-start.31 = (bf16[1,1,1,96,3072]{4,3,2,1,0:T(8,128)(2,1)}, bf16[1,1,1,96,3072]{4,3,2,1,0:T(8,128)(2,1)}, u32[]{:S(2)}, u32[]{:S(2)}) collective-permute-start(bf16[1,1,1,96,3072]{4,3,2,1,0:T(8,128)(2,1)} %maximum_bitcast_fusion), channel_id=1, source_target_pairs={{0,4},{4,0},{1,5},{5,1},{2,6},{6,2},{3,7},{7,3},{8,12},{12,8},{9,1... | collective-permute-start | bytes 1769480 | tf_op jit(solution)/shard_map/ppermute | solution.py:535
  98.9 36.0 %collective-permute-start.25 = (bf16[1,1,1,96,3840]{4,3,2,1,0:T(8,128)(2,1)}, bf16[1,1,1,96,3840]{4,3,2,1,0:T(8,128)(2,1)}, u32[]{:S(2)}, u32[]{:S(2)}) collective-permute-start(bf16[1,1,1,96,3840]{4,3,2,1,0:T(8,128)(2,1)} %bitcast.290), channel_id=1, source_target_pairs={{0,16},{8,24},{16,0},{24,8},{1,17},{9,25},{17,1},{25,9},{2,18},{10... | collective-permute-start | bytes 2211848 | tf_op jit(solution)/shard_map/ppermute | solution.py:535
  104.2 33.6 %collective-permute-start.20 = (bf16[2,1,1,96,1536]{4,3,2,1,0:T(8,128)(2,1)}, bf16[2,1,1,96,1536]{4,3,2,1,0:T(8,128)(2,1)}, u32[]{:S(2)}, u32[]{:S(2)}) collective-permute-start(bf16[2,1,1,96,1536]{4,3,2,1,0:T(8,128)(2,1)} %pad_maximum_fusion.18), channel_id=1, source_target_pairs={{0,4},{4,0},{1,5},{5,1},{2,6},{6,2},{3,7},{7,3},{8,12},{12,8},{9,1... | collective-permute-start | bytes 1769480 | tf_op jit(solution)/shard_map/ppermute | solution.py:535
  108.3 32.7 %collective-permute-start.10 = (bf16[1,1,2,96,1536]{4,3,2,1,0:T(8,128)(2,1)}, bf16[1,1,2,96,1536]{4,3,2,1,0:T(8,128)(2,1)}, u32[]{:S(2)}, u32[]{:S(2)}) collective-permute-start(bf16[1,1,2,96,1536]{4,3,2,1,0:T(8,128)(2,1)} %pad_maximum_fusion.17), channel_id=1, source_target_pairs={{0,16},{8,24},{16,0},{24,8},{1,17},{9,25},{17,1},{25,9},{2,18},{10... | collective-permute-start | bytes 1769480 | tf_op jit(solution)/shard_map/ppermute | solution.py:535
  118.7 27.7 %collective-permute-start.2 = (bf16[1024,512]{1,0:T(8,128)(2,1)}, bf16[1024,512]{1,0:T(8,128)(2,1)}, u32[]{:S(2)}, u32[]{:S(2)}) collective-permute-start(bf16[1024,512]{1,0:T(8,128)(2,1)} %slice.430), channel_id=1, source_target_pairs={{0,4},{1,5},{2,6},{3,7},{8,12},{9,13},{10,14},{11,15},{16,20},{17,... | collective-permute-start | bytes 3145736 | tf_op jit(solution)/shard_map/ppermute | solution.py:698
  125.5 40.9 %collective-permute-start.32 = (bf16[1,1,2,96,3072]{4,3,2,1,0:T(8,128)(2,1)}, bf16[1,1,2,96,3072]{4,3,2,1,0:T(8,128)(2,1)}, u32[]{:S(2)}, u32[]{:S(2)}) collective-permute-start(bf16[1,1,2,96,3072]{4,3,2,1,0:T(8,128)(2,1)} %pad_maximum_fusion.14), channel_id=1, source_target_pairs={{0,16},{8,24},{16,0},{24,8},{1,17},{9,25},{17,1},{25,9},{2,18},{10... | collective-permute-start | bytes 3538952 | tf_op jit(solution)/shard_map/ppermute | solution.py:535
  137.7 44.2 %collective-permute-start.26 = (bf16[2,1,1,96,3840]{4,3,2,1,0:T(8,128)(2,1)}, bf16[2,1,1,96,3840]{4,3,2,1,0:T(8,128)(2,1)}, u32[]{:S(2)}, u32[]{:S(2)}) collective-permute-start(bf16[2,1,1,96,3840]{4,3,2,1,0:T(8,128)(2,1)} %pad_maximum_fusion.10), channel_id=1, source_target_pairs={{0,4},{4,0},{1,5},{5,1},{2,6},{6,2},{3,7},{7,3},{8,12},{12,8},{9,1... | collective-permute-start | bytes 4423688 | tf_op jit(solution)/shard_map/ppermute | solution.py:535
  141.0 39.1 %collective-permute-start.21 = (bf16[2,1,2,96,1536]{4,3,2,1,0:T(8,128)(2,1)}, bf16[2,1,2,96,1536]{4,3,2,1,0:T(8,128)(2,1)}, u32[]{:S(2)}, u32[]{:S(2)}) collective-permute-start(bf16[2,1,2,96,1536]{4,3,2,1,0:T(8,128)(2,1)} %pad_maximum_fusion.13), channel_id=1, source_target_pairs={{0,8},{8,0},{16,24},{24,16},{1,9},{9,1},{17,25},{25,17},{2,10},{10... | collective-permute-start | bytes 3538952 | tf_op jit(solution)/shard_map/ppermute | solution.py:535
  143.5 26.0 %collective-permute-start.11 = (bf16[2,1,2,96,1536]{4,3,2,1,0:T(8,128)(2,1)}, bf16[2,1,2,96,1536]{4,3,2,1,0:T(8,128)(2,1)S(1)}, u32[]{:S(2)}, u32[]{:S(2)}) collective-permute-start(bf16[2,1,2,96,1536]{4,3,2,1,0:T(8,128)(2,1)} %pad_maximum_fusion.12), channel_id=1, source_target_pairs={{0,8},{8,0},{16,24},{24,16},{1,9},{9,1},{17,25},{25,17},{2,10},{10... | collective-permute-start | bytes 3538952 | tf_op jit(solution)/shard_map/ppermute | solution.py:535
  171.5 40.6 %collective-permute-start.33 = (bf16[2,1,2,96,3072]{4,3,2,1,0:T(8,128)(2,1)}, bf16[2,1,2,96,3072]{4,3,2,1,0:T(8,128)(2,1)}, u32[]{:S(2)}, u32[]{:S(2)}) collective-permute-start(bf16[2,1,2,96,3072]{4,3,2,1,0:T(8,128)(2,1)} %pad_maximum_fusion.5), channel_id=1, source_target_pairs={{0,8},{8,0},{16,24},{24,16},{1,9},{9,1},{17,25},{25,17},{2,10},{10... | collective-permute-start | bytes 7077896 | tf_op jit(solution)/shard_map/ppermute | solution.py:535
  185.6 31.1 %collective-permute-start.27 = (bf16[2,1,2,96,3840]{4,3,2,1,0:T(8,128)(2,1)}, bf16[2,1,2,96,3840]{4,3,2,1,0:T(8,128)(2,1)}, u32[]{:S(2)}, u32[]{:S(2)}) collective-permute-start(bf16[2,1,2,96,3840]{4,3,2,1,0:T(8,128)(2,1)} %pad_maximum_fusion.2), channel_id=1, source_target_pairs={{0,8},{8,0},{16,24},{24,16},{1,9},{9,1},{17,25},{25,17},{2,10},{10... | collective-permute-start | bytes 8847368 | tf_op jit(solution)/shard_map/ppermute | solution.py:535
  287.6 84.6 %collective-permute-start.34 = (bf16[256,768]{1,0:T(8,128)(2,1)}, bf16[256,768]{1,0:T(8,128)(2,1)}, u32[]{:S(2)}, u32[]{:S(2)}) collective-permute-start(bf16[256,768]{1,0:T(8,128)(2,1)} %get-tuple-element.226), channel_id=1, source_target_pairs={{0,1},{1,0},{2,3},{3,2},{4,5},{5,4},{6,7},{7,6},{8,9},{9,8},{10,11... | collective-permute-start | bytes 1179656 | tf_op jit(solution)/shard_map/ppermute | solution.py:535
  288.2 106.7 %collective-permute-start.35 = (bf16[256,768]{1,0:T(8,128)(2,1)}, bf16[256,768]{1,0:T(8,128)(2,1)}, u32[]{:S(2)}, u32[]{:S(2)}) collective-permute-start(bf16[256,768]{1,0:T(8,128)(2,1)} %get-tuple-element.226), channel_id=1, source_target_pairs={{0,2},{1,3},{2,0},{3,1},{4,6},{5,7},{6,4},{7,5},{8,10},{9,11},{10,... | collective-permute-start | bytes 1179656 | tf_op jit(solution)/shard_map/ppermute | solution.py:535
  306.1 22.7 %collective-permute-start.86 = (f32[8064]{0:T(1024)}, f32[8064]{0:T(1024)S(1)}, u32[]{:S(2)}, u32[]{:S(2)}) collective-permute-start(f32[8064]{0:T(1024)} %constant_dynamic-update-slice_fusion.1), channel_id=1, source_target_pairs={{0,1},{1,0},{2,3},{3,2},{4,5},{5,4},{6,7},{7,6},{8,9},{9,8},{10,11... | collective-permute-start | bytes 96776 | tf_op jit(solution)/shard_map/ppermute | solution.py:535
  309.5 22.4 %collective-permute-start.87 = (f32[8064]{0:T(1024)}, f32[8064]{0:T(1024)S(1)}, u32[]{:S(2)}, u32[]{:S(2)}) collective-permute-start(f32[8064]{0:T(1024)} %constant_dynamic-update-slice_fusion.2), channel_id=1, source_target_pairs={{0,2},{1,3},{2,0},{3,1},{4,6},{5,7},{6,4},{7,5},{8,10},{9,11},{10,... | collective-permute-start | bytes 96776 | tf_op jit(solution)/shard_map/ppermute | solution.py:535
  311.2 20.6 %collective-permute-start.88 = (f32[8064]{0:T(1024)}, f32[8064]{0:T(1024)S(1)}, u32[]{:S(2)}, u32[]{:S(2)}) collective-permute-start(f32[8064]{0:T(1024)} %constant_dynamic-update-slice_fusion.3), channel_id=1, source_target_pairs={{0,3},{1,2},{2,1},{3,0},{4,7},{5,6},{6,5},{7,4},{8,11},{9,10},{10,... | collective-permute-start | bytes 96776 | tf_op jit(solution)/shard_map/ppermute | solution.py:535
  331.8 16.7 %collective-permute-start.38 = (bf16[256,192]{1,0:T(8,128)(2,1)S(1)}, bf16[256,192]{1,0:T(8,128)(2,1)S(1)}, u32[]{:S(2)}, u32[]{:S(2)}) collective-permute-start(bf16[256,192]{1,0:T(8,128)(2,1)S(1)} %get-tuple-element.289), channel_id=1, source_target_pairs={{0,2},{1,3},{2,0},{3,1},{4,6},{5,7},{6,4},{7,5},{8,10},{9,11},{10,... | collective-permute-start | bytes 294920 | tf_op jit(solution)/shard_map/ppermute | solution.py:535
  331.9 22.0 %collective-permute-start.39 = (bf16[256,192]{1,0:T(8,128)(2,1)S(1)}, bf16[256,192]{1,0:T(8,128)(2,1)S(1)}, u32[]{:S(2)}, u32[]{:S(2)}) collective-permute-start(bf16[256,192]{1,0:T(8,128)(2,1)S(1)} %get-tuple-element.288), channel_id=1, source_target_pairs={{0,3},{1,2},{2,1},{3,0},{4,7},{5,6},{6,5},{7,4},{8,11},{9,10},{10,... | collective-permute-start | bytes 294920 | tf_op jit(solution)/shard_map/ppermute | solution.py:535
  335.9 60.5 %collective-permute-start.36 = (bf16[256,768]{1,0:T(8,128)(2,1)}, bf16[256,768]{1,0:T(8,128)(2,1)S(1)}, u32[]{:S(2)}, u32[]{:S(2)}) collective-permute-start(bf16[256,768]{1,0:T(8,128)(2,1)} %get-tuple-element.226), channel_id=1, source_target_pairs={{0,3},{1,2},{2,1},{3,0},{4,7},{5,6},{6,5},{7,4},{8,11},{9,10},{10,... | collective-permute-start | bytes 1179656 | tf_op jit(solution)/shard_map/ppermute | solution.py:535
  348.6 219.6 %collective-permute-start.79 = (bf16[384,3072]{1,0:T(8,128)(2,1)}, bf16[384,3072]{1,0:T(8,128)(2,1)}, u32[]{:S(2)}, u32[]{:S(2)}) collective-permute-start(bf16[384,3072]{1,0:T(8,128)(2,1)} %convolution_convert_fusion), channel_id=1, source_target_pairs={{0,8},{8,0},{16,24},{24,16},{1,9},{9,1},{17,25},{25,17},{2,10},{10... | collective-permute-start | bytes 7077896 | tf_op jit(solution)/shard_map/ppermute | solution.py:535
  353.8 44.1 %collective-permute-start.58 = (bf16[384,768]{1,0:T(8,128)(2,1)}, bf16[384,768]{1,0:T(8,128)(2,1)}, u32[]{:S(2)}, u32[]{:S(2)}) collective-permute-start(bf16[384,768]{1,0:T(8,128)(2,1)} %convolution_convert_fusion.7), channel_id=1, source_target_pairs={{0,8},{8,0},{16,24},{24,16},{1,9},{9,1},{17,25},{25,17},{2,10},{10... | collective-permute-start | bytes 1769480 | tf_op jit(solution)/shard_map/ppermute | solution.py:535
  372.2 71.4 %collective-permute-start.47 = (bf16[512,768]{1,0:T(8,128)(2,1)S(1)}, bf16[512,768]{1,0:T(8,128)(2,1)S(1)}, u32[]{:S(2)}, u32[]{:S(2)}) collective-permute-start(bf16[512,768]{1,0:T(8,128)(2,1)S(1)} %fusion.69), channel_id=1, source_target_pairs={{0,4},{4,0},{1,5},{5,1},{2,6},{6,2},{3,7},{7,3},{8,12},{12,8},{9,1... | collective-permute-start | bytes 2359304 | tf_op jit(solution)/shard_map/ppermute | solution.py:535
  395.0 83.1 %collective-permute-start.40 = (bf16[1024,512]{1,0:T(8,128)(2,1)}, bf16[1024,512]{1,0:T(8,128)(2,1)}, u32[]{:S(2)}, u32[]{:S(2)}) collective-permute-start(bf16[1024,512]{1,0:T(8,128)(2,1)} %convert_element_type.455), channel_id=1, source_target_pairs={{4,0},{5,1},{6,2},{7,3},{12,8},{13,9},{14,10},{15,11},{20,16},{21,... | collective-permute-start | bytes 3145736 | tf_op jit(solution)/shard_map/ppermute | solution.py:777
  399.4 42.5 %collective-permute-start.59 = (bf16[2,96,768]{2,1,0:T(8,128)(2,1)S(1)}, bf16[2,96,768]{2,1,0:T(8,128)(2,1)S(1)}, u32[]{:S(2)}, u32[]{:S(2)}) collective-permute-start(bf16[2,96,768]{2,1,0:T(8,128)(2,1)S(1)} %dynamic-slice_bitcast_fusion.6), channel_id=1, source_target_pairs={{0,4},{4,0},{1,5},{5,1},{2,6},{6,2},{3,7},{7,3},{8,12},{12,8},{9,1... | collective-permute-start | bytes 884744 | tf_op jit(solution)/shard_map/ppermute | solution.py:535
  453.6 14.4 %collective-permute-start.49 = (bf16[128,768]{1,0:T(8,128)(2,1)S(1)}, bf16[128,768]{1,0:T(8,128)(2,1)S(1)}, u32[]{:S(2)}, u32[]{:S(2)}) collective-permute-start(bf16[128,768]{1,0:T(8,128)(2,1)S(1)} %get-tuple-element.233), channel_id=1, source_target_pairs={{0,2},{1,3},{2,0},{3,1},{4,6},{5,7},{6,4},{7,5},{8,10},{9,11},{10,... | collective-permute-start | bytes 589832 | tf_op jit(solution)/shard_map/ppermute | solution.py:535
  454.9 17.0 %collective-permute-start.50 = (bf16[128,768]{1,0:T(8,128)(2,1)S(1)}, bf16[128,768]{1,0:T(8,128)(2,1)S(1)}, u32[]{:S(2)}, u32[]{:S(2)}) collective-permute-start(bf16[128,768]{1,0:T(8,128)(2,1)S(1)} %get-tuple-element.232), channel_id=1, source_target_pairs={{0,3},{1,2},{2,1},{3,0},{4,7},{5,6},{6,5},{7,4},{8,11},{9,10},{10,... | collective-permute-start | bytes 589832 | tf_op jit(solution)/shard_map/ppermute | solution.py:535
  460.2 14.2 %collective-permute-start.64 = (bf16[1,96,192]{2,1,0:T(8,128)(2,1)S(1)}, bf16[1,96,192]{2,1,0:T(8,128)(2,1)S(1)}, u32[]{:S(2)}, u32[]{:S(2)}) collective-permute-start(bf16[1,96,192]{2,1,0:T(8,128)(2,1)S(1)} %fusion.88), channel_id=1, source_target_pairs={{0,4},{4,0},{1,5},{5,1},{2,6},{6,2},{3,7},{7,3},{8,12},{12,8},{9,1... | collective-permute-start | bytes 110600 | tf_op jit(solution)/shard_map/ppermute | solution.py:535
  472.0 16.1 %collective-permute-start.51 = (bf16[128,768]{1,0:T(8,128)(2,1)S(1)}, bf16[128,768]{1,0:T(8,128)(2,1)}, u32[]{:S(2)}, u32[]{:S(2)}) collective-permute-start(bf16[128,768]{1,0:T(8,128)(2,1)S(1)} %add_convert_fusion.6), channel_id=1, source_target_pairs={{0,1},{1,0},{2,3},{3,2},{4,5},{5,4},{6,7},{7,6},{8,9},{9,8},{10,11... | collective-permute-start | bytes 589832 | tf_op jit(solution)/shard_map/ppermute | solution.py:535
  472.1 16.0 %collective-permute-start.52 = (bf16[128,768]{1,0:T(8,128)(2,1)S(1)}, bf16[128,768]{1,0:T(8,128)(2,1)}, u32[]{:S(2)}, u32[]{:S(2)}) collective-permute-start(bf16[128,768]{1,0:T(8,128)(2,1)S(1)} %add_convert_fusion.6), channel_id=1, source_target_pairs={{0,2},{1,3},{2,0},{3,1},{4,6},{5,7},{6,4},{7,5},{8,10},{9,11},{10,... | collective-permute-start | bytes 589832 | tf_op jit(solution)/shard_map/ppermute | solution.py:535
  474.4 16.5 %collective-permute-start.53 = (bf16[128,768]{1,0:T(8,128)(2,1)S(1)}, bf16[128,768]{1,0:T(8,128)(2,1)}, u32[]{:S(2)}, u32[]{:S(2)}) collective-permute-start(bf16[128,768]{1,0:T(8,128)(2,1)S(1)} %add_convert_fusion.6), channel_id=1, source_target_pairs={{0,3},{1,2},{2,1},{3,0},{4,7},{5,6},{6,5},{7,4},{8,11},{9,10},{10,... | collective-permute-start | bytes 589832 | tf_op jit(solution)/shard_map/ppermute | solution.py:535
  488.1 19.0 %collective-permute-start.41 = (bf16[256,768]{1,0:T(8,128)(2,1)}, bf16[256,768]{1,0:T(8,128)(2,1)}, u32[]{:S(2)}, u32[]{:S(2)}) collective-permute-start(bf16[256,768]{1,0:T(8,128)(2,1)} %get-tuple-element.202), channel_id=1, source_target_pairs={{0,1},{1,0},{2,3},{3,2},{4,5},{5,4},{6,7},{7,6},{8,9},{9,8},{10,11... | collective-permute-start | bytes 1179656 | tf_op jit(solution)/shard_map/ppermute | solution.py:535
  490.9 26.7 %collective-permute-start.42 = (bf16[256,768]{1,0:T(8,128)(2,1)}, bf16[256,768]{1,0:T(8,128)(2,1)}, u32[]{:S(2)}, u32[]{:S(2)}) collective-permute-start(bf16[256,768]{1,0:T(8,128)(2,1)} %get-tuple-element.204), channel_id=1, source_target_pairs={{0,2},{1,3},{2,0},{3,1},{4,6},{5,7},{6,4},{7,5},{8,10},{9,11},{10,... | collective-permute-start | bytes 1179656 | tf_op jit(solution)/shard_map/ppermute | solution.py:535
  497.4 29.0 %collective-permute-start.43 = (bf16[256,768]{1,0:T(8,128)(2,1)}, bf16[256,768]{1,0:T(8,128)(2,1)}, u32[]{:S(2)}, u32[]{:S(2)}) collective-permute-start(bf16[256,768]{1,0:T(8,128)(2,1)} %get-tuple-element.203), channel_id=1, source_target_pairs={{0,3},{1,2},{2,1},{3,0},{4,7},{5,6},{6,5},{7,4},{8,11},{9,10},{10,... | collective-permute-start | bytes 1179656 | tf_op jit(solution)/shard_map/ppermute | solution.py:535
  507.0 64.5 %collective-permute-start.72 = (bf16[384,3072]{1,0:T(8,128)(2,1)}, bf16[384,3072]{1,0:T(8,128)(2,1)S(1)}, u32[]{:S(2)}, u32[]{:S(2)}) collective-permute-start(bf16[384,3072]{1,0:T(8,128)(2,1)} %convolution_convert_fusion.1), channel_id=1, source_target_pairs={{0,8},{8,0},{16,24},{24,16},{1,9},{9,1},{17,25},{25,17},{2,10},{10... | collective-permute-start | bytes 7077896 | tf_op jit(solution)/shard_map/ppermute | solution.py:535
  507.1 23.5 %collective-permute-start.56 = (bf16[96,576]{1,0:T(8,128)(2,1)S(1)}, bf16[96,576]{1,0:T(8,128)(2,1)S(1)}, u32[]{:S(2)}, u32[]{:S(2)}) collective-permute-start(bf16[96,576]{1,0:T(8,128)(2,1)S(1)} %dynamic-slice_bitcast_fusion.14), channel_id=1, source_target_pairs={{0,4},{4,0},{1,5},{5,1},{2,6},{6,2},{3,7},{7,3},{8,12},{12,8},{9,1... | collective-permute-start | bytes 331784 | tf_op jit(solution)/shard_map/ppermute | solution.py:535
  528.2 14.9 %collective-permute-start.44 = (bf16[256,768]{1,0:T(8,128)(2,1)S(1)}, bf16[256,768]{1,0:T(8,128)(2,1)S(1)}, u32[]{:S(2)}, u32[]{:S(2)}) collective-permute-start(bf16[256,768]{1,0:T(8,128)(2,1)S(1)} %add_convert_fusion.4), channel_id=1, source_target_pairs={{0,1},{1,0},{2,3},{3,2},{4,5},{5,4},{6,7},{7,6},{8,9},{9,8},{10,11... | collective-permute-start | bytes 1179656 | tf_op jit(solution)/shard_map/ppermute | solution.py:535
  528.2 28.7 %collective-permute-start.45 = (bf16[256,768]{1,0:T(8,128)(2,1)S(1)}, bf16[256,768]{1,0:T(8,128)(2,1)S(1)}, u32[]{:S(2)}, u32[]{:S(2)}) collective-permute-start(bf16[256,768]{1,0:T(8,128)(2,1)S(1)} %add_convert_fusion.4), channel_id=1, source_target_pairs={{0,2},{1,3},{2,0},{3,1},{4,6},{5,7},{6,4},{7,5},{8,10},{9,11},{10,... | collective-permute-start | bytes 1179656 | tf_op jit(solution)/shard_map/ppermute | solution.py:535
  530.5 34.4 %collective-permute-start.46 = (bf16[256,768]{1,0:T(8,128)(2,1)S(1)}, bf16[256,768]{1,0:T(8,128)(2,1)S(1)}, u32[]{:S(2)}, u32[]{:S(2)}) collective-permute-start(bf16[256,768]{1,0:T(8,128)(2,1)S(1)} %add_convert_fusion.4), channel_id=1, source_target_pairs={{0,3},{1,2},{2,1},{3,0},{4,7},{5,6},{6,5},{7,4},{8,11},{9,10},{10,... | collective-permute-start | bytes 1179656 | tf_op jit(solution)/shard_map/ppermute | solution.py:535
  543.0 30.6 %collective-permute-start.65 = (bf16[384,3072]{1,0:T(8,128)(2,1)S(1)}, bf16[384,3072]{1,0:T(8,128)(2,1)S(1)}, u32[]{:S(2)}, u32[]{:S(2)}) collective-permute-start(bf16[384,3072]{1,0:T(8,128)(2,1)S(1)} %copy-done.40), channel_id=1, source_target_pairs={{0,8},{8,0},{16,24},{24,16},{1,9},{9,1},{17,25},{25,17},{2,10},{10... | collective-permute-start | bytes 7077896 | tf_op jit(solution)/shard_map/ppermute | solution.py:535
  571.3 29.0 %collective-permute-start.80 = (bf16[2,96,3072]{2,1,0:T(8,128)(2,1)S(1)}, bf16[2,96,3072]{2,1,0:T(8,128)(2,1)S(1)}, u32[]{:S(2)}, u32[]{:S(2)}) collective-permute-start(bf16[2,96,3072]{2,1,0:T(8,128)(2,1)S(1)} %dynamic-slice_bitcast_fusion), channel_id=1, source_target_pairs={{0,16},{8,24},{16,0},{24,8},{1,17},{9,25},{17,1},{25,9},{2,18},{10... | collective-permute-start | bytes 3538952 | tf_op jit(solution)/shard_map/ppermute | solution.py:535
  573.6 27.9 %collective-permute-start.73 = (bf16[2,96,3072]{2,1,0:T(8,128)(2,1)S(1)}, bf16[2,96,3072]{2,1,0:T(8,128)(2,1)S(1)}, u32[]{:S(2)}, u32[]{:S(2)}) collective-permute-start(bf16[2,96,3072]{2,1,0:T(8,128)(2,1)S(1)} %dynamic-slice_bitcast_fusion.1), channel_id=1, source_target_pairs={{0,4},{4,0},{1,5},{5,1},{2,6},{6,2},{3,7},{7,3},{8,12},{12,8},{9,1... | collective-permute-start | bytes 3538952 | tf_op jit(solution)/shard_map/ppermute | solution.py:535
  575.9 49.7 %collective-permute-start.66 = (bf16[2,96,3072]{2,1,0:T(8,128)(2,1)S(1)}, bf16[2,96,3072]{2,1,0:T(8,128)(2,1)S(1)}, u32[]{:S(2)}, u32[]{:S(2)}) collective-permute-start(bf16[2,96,3072]{2,1,0:T(8,128)(2,1)S(1)} %dynamic-slice_bitcast_fusion.2), channel_id=1, source_target_pairs={{0,16},{8,24},{16,0},{24,8},{1,17},{9,25},{17,1},{25,9},{2,18},{10... | collective-permute-start | bytes 3538952 | tf_op jit(solution)/shard_map/ppermute | solution.py:535
  600.8 25.4 %collective-permute-start.81 = (bf16[96,3072]{1,0:T(8,128)(2,1)S(1)}, bf16[96,3072]{1,0:T(8,128)(2,1)S(1)}, u32[]{:S(2)}, u32[]{:S(2)}) collective-permute-start(bf16[96,3072]{1,0:T(8,128)(2,1)S(1)} %dynamic-slice_bitcast_fusion.3), channel_id=1, source_target_pairs={{0,4},{4,0},{1,5},{5,1},{2,6},{6,2},{3,7},{7,3},{8,12},{12,8},{9,1... | collective-permute-start | bytes 1769480 | tf_op jit(solution)/shard_map/ppermute | solution.py:535
  601.9 33.3 %collective-permute-start.74 = (bf16[96,3072]{1,0:T(8,128)(2,1)S(1)}, bf16[96,3072]{1,0:T(8,128)(2,1)S(1)}, u32[]{:S(2)}, u32[]{:S(2)}) collective-permute-start(bf16[96,3072]{1,0:T(8,128)(2,1)S(1)} %dynamic-slice_bitcast_fusion.4), channel_id=1, source_target_pairs={{0,16},{8,24},{16,0},{24,8},{1,17},{9,25},{17,1},{25,9},{2,18},{10... | collective-permute-start | bytes 1769480 | tf_op jit(solution)/shard_map/ppermute | solution.py:535
  626.4 13.3 %collective-permute-start.83 = (bf16[96,768]{1,0:T(8,128)(2,1)S(1)}, bf16[96,768]{1,0:T(8,128)(2,1)S(1)}, u32[]{:S(2)}, u32[]{:S(2)}) collective-permute-start(bf16[96,768]{1,0:T(8,128)(2,1)S(1)} %get-tuple-element.236), channel_id=1, source_target_pairs={{0,2},{1,3},{2,0},{3,1},{4,6},{5,7},{6,4},{7,5},{8,10},{9,11},{10,... | collective-permute-start | bytes 442376 | tf_op jit(solution)/shard_map/ppermute | solution.py:535
  628.4 14.4 %collective-permute-start.84 = (bf16[96,768]{1,0:T(8,128)(2,1)S(1)}, bf16[96,768]{1,0:T(8,128)(2,1)S(1)}, u32[]{:S(2)}, u32[]{:S(2)}) collective-permute-start(bf16[96,768]{1,0:T(8,128)(2,1)S(1)} %get-tuple-element.235), channel_id=1, source_target_pairs={{0,3},{1,2},{2,1},{3,0},{4,7},{5,6},{6,5},{7,4},{8,11},{9,10},{10,... | collective-permute-start | bytes 442376 | tf_op jit(solution)/shard_map/ppermute | solution.py:535
  636.0 17.5 %collective-permute-start.76 = (bf16[96,768]{1,0:T(8,128)(2,1)S(1)}, bf16[96,768]{1,0:T(8,128)(2,1)S(1)}, u32[]{:S(2)}, u32[]{:S(2)}) collective-permute-start(bf16[96,768]{1,0:T(8,128)(2,1)S(1)} %get-tuple-element.239), channel_id=1, source_target_pairs={{0,2},{1,3},{2,0},{3,1},{4,6},{5,7},{6,4},{7,5},{8,10},{9,11},{10,... | collective-permute-start | bytes 442376 | tf_op jit(solution)/shard_map/ppermute | solution.py:535
  637.9 20.3 %collective-permute-start.77 = (bf16[96,768]{1,0:T(8,128)(2,1)S(1)}, bf16[96,768]{1,0:T(8,128)(2,1)S(1)}, u32[]{:S(2)}, u32[]{:S(2)}) collective-permute-start(bf16[96,768]{1,0:T(8,128)(2,1)S(1)} %get-tuple-element.238), channel_id=1, source_target_pairs={{0,3},{1,2},{2,1},{3,0},{4,7},{5,6},{6,5},{7,4},{8,11},{9,10},{10,... | collective-permute-start | bytes 442376 | tf_op jit(solution)/shard_map/ppermute | solution.py:535
  639.7 22.0 %collective-permute-start.68 = (bf16[96,768]{1,0:T(8,128)(2,1)S(1)}, bf16[96,768]{1,0:T(8,128)(2,1)S(1)}, u32[]{:S(2)}, u32[]{:S(2)}) collective-permute-start(bf16[96,768]{1,0:T(8,128)(2,1)S(1)} %pad_maximum_fusion.26), channel_id=1, source_target_pairs={{0,1},{1,0},{2,3},{3,2},{4,5},{5,4},{6,7},{7,6},{8,9},{9,8},{10,11... | collective-permute-start | bytes 442376 | tf_op jit(solution)/shard_map/ppermute | solution.py:535
  642.9 18.8 %collective-permute-start.69 = (bf16[96,768]{1,0:T(8,128)(2,1)S(1)}, bf16[96,768]{1,0:T(8,128)(2,1)S(1)}, u32[]{:S(2)}, u32[]{:S(2)}) collective-permute-start(bf16[96,768]{1,0:T(8,128)(2,1)S(1)} %pad_maximum_fusion.27), channel_id=1, source_target_pairs={{0,2},{1,3},{2,0},{3,1},{4,6},{5,7},{6,4},{7,5},{8,10},{9,11},{10,... | collective-permute-start | bytes 442376 | tf_op jit(solution)/shard_map/ppermute | solution.py:535
  643.0 20.1 %collective-permute-start.70 = (bf16[96,768]{1,0:T(8,128)(2,1)S(1)}, bf16[96,768]{1,0:T(8,128)(2,1)S(1)}, u32[]{:S(2)}, u32[]{:S(2)}) collective-permute-start(bf16[96,768]{1,0:T(8,128)(2,1)S(1)} %pad_maximum_fusion.28), channel_id=1, source_target_pairs={{0,3},{1,2},{2,1},{3,0},{4,7},{5,6},{6,5},{7,4},{8,11},{9,10},{10,... | collective-permute-start | bytes 442376 | tf_op jit(solution)/shard_map/ppermute | solution.py:535
  (140 other events, 862.6 us)

commit v2 on v1

v2 whole, which is shorter than its diff:
```python
import functools

import jax
import jax.numpy as jnp
from jax import lax
from jax.experimental import pallas as pl
from jax.experimental.pallas import tpu as pltpu
from jax.sharding import PartitionSpec as P

HEAD_DIM = 64
LANES = 128
TILE = 256
NEG = -1e30
EPS = 1e-05
F32 = jnp.float32
BF16 = jnp.bfloat16
VMEM_LIMIT = 56 * 1024 * 1024
WEIGHT = 0.01


def dot_of(a, b, a_dim, b_dim):
    return lax.dot_general(a, b, (((a_dim,), (b_dim,)), ((), ())), preferred_element_type=F32)


def nn(a, b):
    return dot_of(a, b, 1, 0)


def nt(a, b):
    return dot_of(a, b, 1, 1)


def tn(a, b):
    return dot_of(a, b, 0, 0)


def head_lanes(rows, half):
    lane = lax.broadcasted_iota(jnp.int32, (rows, LANES), 1)
    return (lane < HEAD_DIM) if half == 0 else (lane >= HEAD_DIM)


def flags_of(rows, seg):
    lane = lax.broadcasted_iota(jnp.int32, (rows, LANES), 1) % HEAD_DIM
    row = lax.broadcasted_iota(jnp.int32, (rows, LANES), 0)
    return jnp.where(lane == row // seg, 1.0, 0.0).astype(BF16)


def causal_keep(size, seg):
    key = lax.broadcasted_iota(jnp.int32, (size, size), 0)
    query = lax.broadcasted_iota(jnp.int32, (size, size), 1)
    return (key // seg != query // seg) | (key <= query)


def flip(a):
    return a.astype(F32).T.astype(a.dtype)


def lane_pad(a):
    gap = -a.shape[1] % LANES
    return jnp.concatenate([a, jnp.zeros((a.shape[0], gap), a.dtype)], axis=1) if gap else a


def fold_forward(state, queries, key_tile, value_tile, bias_tile, heads, keep):
    out = []
    for h in range(heads):
        g, half = divmod(h, 2)
        lanes = slice(g * LANES, (g + 1) * LANES)
        if half == 0:
            value_rows = flip(value_tile[:, lanes])
        keys = jnp.where(head_lanes(TILE, half), key_tile[:, lanes], bias_tile)
        scores = nt(keys, queries[h])
        if keep is not None:
            scores = jnp.where(keep, scores, NEG)
        peak, total, mix = state[3 * h : 3 * h + 3]
        new_peak = jnp.maximum(peak, jnp.max(scores, axis=0, keepdims=True))
        weights = jnp.exp(scores - new_peak)
        shrink = jnp.exp(peak - new_peak)
        total = total * shrink + jnp.sum(weights, axis=0, keepdims=True)
        mix = mix * shrink + nn(
            value_rows[half * HEAD_DIM : (half + 1) * HEAD_DIM], weights.astype(BF16)
        )
        out += [new_peak, total, mix]
    return tuple(out)


def fresh_state(heads, rows):
    state = []
    for _ in range(heads):
        state += [
            jnp.full((1, rows), NEG, F32),
            jnp.zeros((1, rows), F32),
            jnp.zeros((HEAD_DIM, rows), F32),
        ]
    return tuple(state)


def flagged_queries(q, heads, seg):
    rows = q.shape[0]
    flags = flags_of(rows, seg)
    return [
        jnp.where(head_lanes(rows, h % 2), q[:, (h // 2) * LANES : (h // 2 + 1) * LANES], flags)
        for h in range(heads)
    ]


def mixed(state, heads):
    parts = [state[3 * h + 2] / state[3 * h + 1] for h in range(heads)]
    if heads % 2:
        parts.append(jnp.zeros_like(parts[0]))
    return jnp.concatenate(
        [jnp.concatenate(parts[h : h + 2], axis=0).T for h in range(0, len(parts), 2)], axis=1
    ).astype(BF16)


def put_logs(state, heads, log_ref):
    log_ref[...] = jnp.zeros_like(log_ref)
    for h in range(heads):
        log_ref[h : h + 1, :] = state[3 * h] + jnp.log(state[3 * h + 1])


def ancestors(parent_ref, label, count):
    def step(_, carry):
        at, bits = carry
        found = at >= 0
        safe = jnp.maximum(at, 0)
        return jnp.where(found, parent_ref[safe], at), jnp.where(
            found, bits | (jnp.int32(1) << safe), bits
        )

    return lax.fori_loop(0, count, step, (parent_ref[label], jnp.int32(0)))[1]


def seg_terms(bits, labels, same, seg):
    lane = lax.broadcasted_iota(jnp.int32, (TILE, LANES), 1) % HEAD_DIM
    row = lax.broadcasted_iota(jnp.int32, (TILE, LANES), 0) // seg
    out = jnp.zeros((TILE, LANES), F32)
    for i, mask in enumerate(bits):
        for t, label in enumerate(labels):
            if same and i == t:
                continue
            term = jnp.where(((mask >> label) & 1) == 1, 0.0, NEG)
            out = jnp.where((lane == i) & (row == t), term, out)
    return out.astype(BF16)


def unpack_kv(tile):
    half = tile.shape[1] // 2
    return lane_pad(tile[:, :half]), lane_pad(tile[:, half:])


def fill_trunk(info_ref, own_ref, sent_ref, trunk_ref):
    def fill(ref):
        keys, values = unpack_kv(ref[...])
        trunk_ref[:, : keys.shape[1]] = keys
        trunk_ref[:, keys.shape[1] :] = values

    @pl.when((pl.program_id(0) == 0) & (info_ref[1] == 0))
    def _():
        fill(own_ref)

    @pl.when((pl.program_id(0) == 0) & (info_ref[1] != 0))
    def _():
        fill(sent_ref)


def tile_rows(c):
    return pl.ds(pl.multiple_of(c * TILE, TILE), TILE)


def block_masks(info_ref, parent_ref, label_ref, seg, rows):
    b = pl.program_id(0)
    per = TILE // seg
    first = info_ref[1] * rows + b * TILE
    own = [label_ref[first + i * seg] for i in range(per)]
    bits = [ancestors(parent_ref, label, parent_ref.shape[0]) for label in own]

    def terms(c):
        return seg_terms(bits, [label_ref[c * TILE + t * seg] for t in range(per)], False, seg)

    count = jnp.where(info_ref[1] == 0, b, rows // TILE)
    return seg_terms(bits, own, True, seg), terms, count


def put_slot(slot, value, refs):
    for j, ref in enumerate(refs):

        @pl.when(slot == j)
        def _(ref=ref):
            ref[...] = value.astype(ref.dtype)


def take_slot(slot, refs):
    value = refs[0][...]
    for j, ref in enumerate(refs[1:], 1):
        value = jnp.where(slot == j, ref[...], value)
    return value


def self_forward_kernel(
    info_ref, parent_ref, label_ref, q_ref, own_ref, sent_ref, *rest, heads, seg
):
    mix_refs, (log_ref, trunk_ref) = rest[:-2], rest[-2:]
    b = pl.program_id(0)
    fill_trunk(info_ref, own_ref, sent_ref, trunk_ref)
    width = trunk_ref.shape[1] // 2
    queries = flagged_queries(lane_pad(q_ref[...]), heads, seg)
    own_terms, terms, count = block_masks(
        info_ref, parent_ref, label_ref, seg, own_ref.shape[0]
    )
    keys, values = unpack_kv(own_ref[tile_rows(b), :])
    state = fold_forward(
        fresh_state(heads, TILE), queries, keys, values, own_terms, heads, causal_keep(TILE, seg)
    )

    def body(c, state):
        rows = tile_rows(c)
        return fold_forward(
            state,
            queries,
            trunk_ref[rows, :width],
            trunk_ref[rows, width:],
            terms(c),
            heads,
            None,
        )

    state = lax.fori_loop(0, count, body, state)
    put_logs(state, heads, log_ref)
    put_slot(b ^ info_ref[2], mixed(state, heads)[:, : mix_refs[0].shape[1]], mix_refs)


def params():
    return pltpu.CompilerParams(vmem_limit_bytes=VMEM_LIMIT)


def cost(flops, bytes_accessed, transcendentals=0):
    return pl.CostEstimate(
        flops=int(flops * WEIGHT),
        bytes_accessed=int(bytes_accessed * WEIGHT),
        transcendentals=int(transcendentals * WEIGHT),
    )


def whole(shape):
    return pl.BlockSpec(shape, lambda *_: (0,) * len(shape))


def shape_of(shape, dtype):
    return jax.ShapeDtypeStruct(shape, dtype)


def self_forward(scalars, q, own, sent, tensors, heads, seg):
    rows, columns = q.shape
    blocks = rows // TILE
    width = -(-columns // LANES) * LANES
    return pl.pallas_call(
        functools.partial(self_forward_kernel, heads=heads, seg=seg),
        grid_spec=pltpu.PrefetchScalarGridSpec(
            num_scalar_prefetch=3,
            grid=(blocks,),
            in_specs=[
                pl.BlockSpec((TILE, columns), lambda b, *_: (b, 0)),
                whole(own.shape),
                whole(own.shape),
            ],
            out_specs=[whole((TILE, columns))] * tensors
            + [pl.BlockSpec((8, TILE), lambda b, *_: (0, b))],
            scratch_shapes=[pltpu.VMEM((rows, 2 * width), BF16)],
        ),
        out_shape=[shape_of((TILE, columns), BF16)] * tensors + [shape_of((8, rows), F32)],
        compiler_params=params(),
        cost_estimate=cost(rows * rows * columns * 8, rows * columns * 16, rows * rows * heads),
        name="self_forward",
    )(*scalars, q, own, sent)


def fold_backward(
    queries, plain, grads, logs, deltas, key_tile, value_tile, bias_tile, heads, keep
):
    grad_keys, grad_values, grad_queries = [], [], []
    for h in range(heads):
        g, half = divmod(h, 2)
        lanes = slice(g * LANES, (g + 1) * LANES)
        if half == 0:
            key_rows = flip(key_tile[:, lanes])
        keys = jnp.where(head_lanes(TILE, half), key_tile[:, lanes], bias_tile)
        scores = nt(keys, queries[h])
        if keep is not None:
            scores = jnp.where(keep, scores, NEG)
        probs = jnp.exp(scores - logs[h])
        grad_probs = nt(value_tile[:, lanes], grads[h])
        grad_scores = (probs * (grad_probs - deltas[h])).astype(BF16)
        part_values = nn(probs.astype(BF16), grads[h])
        part_keys = nn(grad_scores, plain[h])
        if half == 0:
            grad_values.append(part_values)
            grad_keys.append(part_keys)
        else:
            grad_values[g] = grad_values[g] + part_values
            grad_keys[g] = grad_keys[g] + part_keys
        grad_queries.append(nn(key_rows[half * HEAD_DIM : (half + 1) * HEAD_DIM], grad_scores))
    return grad_keys, grad_values, tuple(grad_queries)


def backward_sides(q, grad, mix, heads, seg):
    rows = q.shape[0]
    queries = flagged_queries(q, heads, seg)
    plain, grads, deltas = [], [], []
    for h in range(heads):
        g, half = divmod(h, 2)
        lanes = slice(g * LANES, (g + 1) * LANES)
        mask = head_lanes(rows, half)
        plain.append(jnp.where(mask, q[:, lanes], jnp.zeros((), BF16)))
        grads.append(jnp.where(mask, grad[:, lanes], jnp.zeros((), BF16)))
        if half == 0:
            product = (grad[:, lanes].astype(F32) * mix[:, lanes].astype(F32)).T
        deltas.append(
            jnp.sum(product[half * HEAD_DIM : (half + 1) * HEAD_DIM], axis=0, keepdims=True)
        )
    return queries, plain, grads, deltas


def query_grads(grad_queries, scale):
    parts = list(grad_queries)
    if len(parts) % 2:
        parts.append(jnp.zeros_like(parts[0]))
    return (
        jnp.concatenate(
            [jnp.concatenate(parts[h : h + 2], axis=0).T for h in range(0, len(parts), 2)], axis=1
        )
        * scale
    ).astype(BF16)


def self_backward_kernel(
    info_ref, parent_ref, label_ref, q_ref, own_ref, sent_ref, *rest, heads, seg, scale, tensors
):
    grad_refs, mix_refs, rest = rest[:tensors], rest[tensors : 2 * tensors], rest[2 * tensors :]
    log_ref, dq_ref, down_ref, dtrunk_ref, sums_ref, trunk_ref, sum_ref, vector_ref = rest
    b = pl.program_id(0)
    slot = b ^ info_ref[2]
    fill_trunk(info_ref, own_ref, sent_ref, trunk_ref)
    width = trunk_ref.shape[1] // 2
    half_columns = own_ref.shape[1] // 2
    queries, plain, grads, deltas = backward_sides(
        lane_pad(q_ref[...]),
        lane_pad(take_slot(slot, grad_refs)),
        lane_pad(take_slot(slot, mix_refs)),
        heads,
        seg,
    )
    logs = [log_ref[h : h + 1, :] for h in range(heads)]
    own_terms, terms, count = block_masks(
        info_ref, parent_ref, label_ref, seg, own_ref.shape[0]
    )

    @pl.when(b == 0)
    def _():
        sum_ref[...] = jnp.zeros_like(sum_ref)
        vector_ref[...] = jnp.zeros_like(vector_ref)

    keys, values = unpack_kv(own_ref[tile_rows(b), :])
    grad_keys, grad_values, grad_queries = fold_backward(
        queries, plain, grads, logs, deltas, keys, values, own_terms, heads, causal_keep(TILE, seg)
    )
    down_ref[:, :half_columns] = jnp.concatenate(grad_keys, axis=1)[:, :half_columns]
    down_ref[:, half_columns:] = jnp.concatenate(grad_values, axis=1)[:, :half_columns]

    def body(c, grad_queries):
        rows = tile_rows(c)
        grad_keys, grad_values, more = fold_backward(
            queries,
            plain,
            grads,
            logs,
            deltas,
            trunk_ref[rows, :width],
            trunk_ref[rows, width:],
            terms(c),
            heads,
            None,
        )
        for g in range(len(grad_keys)):
            sum_ref[rows, g * LANES : (g + 1) * LANES] += grad_keys[g]
            sum_ref[rows, width + g * LANES : width + (g + 1) * LANES] += grad_values[g]
        return tuple(x + y for x, y in zip(grad_queries, more))

    grad_queries = lax.fori_loop(0, count, body, grad_queries)
    dq = query_grads(grad_queries, scale)[:, :half_columns]
    dq_ref[...] = dq
    vector_ref[0:1, :] += jnp.sum(dq.astype(F32), axis=0, keepdims=True)
    vector_ref[1:2, :] += jnp.sum(down_ref[:, half_columns:], axis=0, keepdims=True)

    @pl.when(b == pl.num_programs(0) - 1)
    def _():
        trunk_sum = jnp.sum(sum_ref[:, width : width + half_columns], axis=0, keepdims=True)
        sums_ref[...] = jnp.zeros_like(sums_ref)
        sums_ref[pl.ds(info_ref[2], 1), :half_columns] = vector_ref[0:1, :]
        sums_ref[pl.ds(tensors + info_ref[2], 1), :half_columns] = (
            vector_ref[1:2, :] + trunk_sum
        )
        dtrunk_ref[:, :half_columns] = sum_ref[:, :half_columns].astype(BF16)
        dtrunk_ref[:, half_columns:] = sum_ref[:, width : width + half_columns].astype(BF16)


def self_backward(scalars, q, own, sent, grads, mixes, logs, heads, seg, scale, model_width):
    rows, columns = q.shape
    blocks = rows // TILE
    width = -(-columns // LANES) * LANES
    tensors = len(grads)
    tile = pl.BlockSpec((TILE, columns), lambda b, *_: (b, 0))
    return pl.pallas_call(
        functools.partial(
            self_backward_kernel, heads=heads, seg=seg, scale=scale, tensors=tensors
        ),
        grid_spec=pltpu.PrefetchScalarGridSpec(
            num_scalar_prefetch=3,
            grid=(blocks,),
            in_specs=[tile, whole(own.shape), whole(own.shape)]
            + [whole((TILE, columns))] * (2 * tensors)
            + [pl.BlockSpec((8, TILE), lambda b, *_: (0, b))],
            out_specs=[
                tile,
                pl.BlockSpec((TILE, 2 * columns), lambda b, *_: (b, 0)),
                whole((rows, 2 * columns)),
                whole((2 * tensors, model_width)),
            ],
            scratch_shapes=[
                pltpu.VMEM((rows, 2 * width), BF16),
                pltpu.VMEM((rows, 2 * width), F32),
                pltpu.VMEM((8, columns), F32),
            ],
        ),
        out_shape=[
            shape_of((rows, columns), BF16),
            shape_of((rows, 2 * columns), F32),
            shape_of((rows, 2 * columns), BF16),
            shape_of((2 * tensors, model_width), F32),
        ],
        compiler_params=params(),
        cost_estimate=cost(rows * rows * columns * 20, rows * columns * 40, rows * rows * heads),
        name="self_backward",
    )(*scalars, q, own, sent, *grads, *mixes, logs)


def length_terms(info_ref, length_ref, c, half_rows):
    row = lax.broadcasted_iota(jnp.int32, (TILE, LANES), 0)
    lane = lax.broadcasted_iota(jnp.int32, (TILE, LANES), 1) % HEAD_DIM
    half, start = divmod(c * TILE, half_rows)
    place = row + ((half ^ info_ref[1]) * half_rows + start)
    return jnp.where((place >= length_ref[0]) & (lane == 0), NEG, 0.0).astype(BF16)


def cross_forward_kernel(info_ref, length_ref, q_ref, k_ref, v_ref, mix_ref, log_ref):
    rows, keys = q_ref.shape[0], k_ref.shape[0]
    queries = flagged_queries(q_ref[...], 2, rows)
    state = fresh_state(2, rows)
    for c in range(keys // TILE):
        part = slice(c * TILE, (c + 1) * TILE)
        terms = length_terms(info_ref, length_ref, c, keys // 2)
        state = fold_forward(state, queries, k_ref[part, :], v_ref[part, :], terms, 2, None)
    put_logs(state, 2, log_ref)
    mix_ref[...] = mixed(state, 2)


def cross_specs(rows, keys, groups):
    part = pl.BlockSpec((rows, LANES), lambda g, *_: (0, g))
    return (
        part,
        pl.BlockSpec((keys, LANES), lambda g, *_: (0, g)),
        pl.BlockSpec((keys, LANES), lambda g, *_: (0, groups + g)),
        pl.BlockSpec((8, rows), lambda g, *_: (g, 0)),
    )


def cross_forward(scalars, q, kv):
    rows, width = q.shape
    keys = kv.shape[0]
    groups = width // LANES
    part, key_side, value_side, log_side = cross_specs(rows, keys, groups)
    return pl.pallas_call(
        cross_forward_kernel,
        grid_spec=pltpu.PrefetchScalarGridSpec(
            num_scalar_prefetch=2,
            grid=(groups,),
            in_specs=[part, key_side, value_side],
            out_specs=[part, log_side],
        ),
        out_shape=[shape_of((rows, width), BF16), shape_of((8 * groups, rows), F32)],
        compiler_params=params(),
        cost_estimate=cost(
            rows * keys * width * 8, (rows + keys) * width * 4, rows * keys * groups * 2
        ),
        name="cross_forward",
    )(*scalars, q, kv, kv)


def cross_backward_kernel(
    info_ref,
    length_ref,
    q_ref,
    k_ref,
    v_ref,
    grad_ref,
    mix_ref,
    log_ref,
    dq_ref,
    dk_ref,
    dv_ref,
    *,
    scale,
):
    rows, keys = q_ref.shape[0], k_ref.shape[0]
    queries, plain, grads, deltas = backward_sides(
        q_ref[...], grad_ref[...], mix_ref[...], 2, rows
    )
    logs = [log_ref[h : h + 1, :] for h in range(2)]
    total = (jnp.zeros((HEAD_DIM, rows), F32),) * 2
    for c in range(keys // TILE):
        part = slice(c * TILE, (c + 1) * TILE)
        terms = length_terms(info_ref, length_ref, c, keys // 2)
        grad_keys, grad_values, more = fold_backward(
            queries, plain, grads, logs, deltas, k_ref[part, :], v_ref[part, :], terms, 2, None
        )
        dk_ref[part, :] = grad_keys[0].astype(BF16)
        dv_ref[part, :] = grad_values[0].astype(BF16)
        total = tuple(x + y for x, y in zip(total, more))
    dq_ref[...] = query_grads(total, scale)


def cross_backward(scalars, q, kv, grad, mix, logs, scale):
    rows, width = q.shape
    keys = kv.shape[0]
    groups = width // LANES
    part, key_side, value_side, log_side = cross_specs(rows, keys, groups)
    return pl.pallas_call(
        functools.partial(cross_backward_kernel, scale=scale),
        grid_spec=pltpu.PrefetchScalarGridSpec(
            num_scalar_prefetch=2,
            grid=(groups,),
            in_specs=[part, key_side, value_side, part, part, log_side],
            out_specs=[part, key_side, key_side],
        ),
        out_shape=[
            shape_of((rows, width), BF16),
            shape_of((keys, width), BF16),
            shape_of((keys, width), BF16),
        ],
        compiler_params=params(),
        cost_estimate=cost(
            rows * keys * width * 20, (rows * 4 + keys * 4) * width * 2, rows * keys * groups * 2
        ),
        name="cross_backward",
    )(*scalars, q, kv, kv, grad, mix, logs)


def norm_parts(values):
    center = values - jnp.mean(values, axis=-1, keepdims=True)
    inverse = lax.rsqrt(jnp.mean(center * center, axis=-1, keepdims=True) + EPS)
    return center * inverse, inverse


def norm_back(pre_sum, gain, grad_out):
    normed, inverse = norm_parts(pre_sum)
    grad_normed = grad_out * gain
    grad_pre = inverse * (
        grad_normed
        - jnp.mean(grad_normed, axis=-1, keepdims=True)
        - normed * jnp.mean(grad_normed * normed, axis=-1, keepdims=True)
    )
    return (
        grad_pre,
        jnp.sum(grad_out * normed, axis=0, keepdims=True),
        jnp.sum(grad_out, axis=0, keepdims=True),
    )


def project_kernel(x_ref, w_ref, qb_ref, vb_ref, q_ref, kv_ref, low_ref, *, scale):
    columns = q_ref.shape[1]
    low = x_ref[0].astype(BF16)
    low_ref[...] = low
    out = nn(low, w_ref[...])
    q_ref[...] = ((out[:, :columns] + qb_ref[...]) * scale).astype(BF16)
    kv_ref[:, :columns] = out[:, columns : 2 * columns].astype(BF16)
    kv_ref[:, columns:] = (out[:, 2 * columns :] + vb_ref[...]).astype(BF16)


def project(x, w, qb, vb, scale):
    _, rows, width = x.shape
    columns = qb.shape[1]
    return pl.pallas_call(
        functools.partial(project_kernel, scale=scale),
        grid=(rows // TILE,),
        in_specs=[
            pl.BlockSpec((1, TILE, width), lambda b: (0, b, 0)),
            whole(w.shape),
            whole(qb.shape),
            whole(vb.shape),
        ],
        out_specs=[
            pl.BlockSpec((TILE, columns), lambda b: (b, 0)),
            pl.BlockSpec((TILE, 2 * columns), lambda b: (b, 0)),
            pl.BlockSpec((TILE, width), lambda b: (b, 0)),
        ],
        out_shape=[
            shape_of((rows, columns), BF16),
            shape_of((rows, 2 * columns), BF16),
            shape_of((rows, width), BF16),
        ],
        compiler_params=params(),
        cost_estimate=cost(rows * width * columns * 6, rows * width * 8),
        name="project",
    )(x, w, qb, vb)


def assemble_kernel(info_ref, near_ref, far_ref, ckv_ref, o_ref, cq_ref, bias_ref):
    tensors, _, columns = o_ref.shape
    width = tensors * columns
    rows = near_ref.shape[2] - bias_ref.shape[1]

    def put(ref):
        for z in range(tensors):
            part = slice(z * columns, (z + 1) * columns)
            late = slice(width + z * columns, width + (z + 1) * columns)
            ckv_ref[:, part] = ref[0, z, :rows, :columns]
            ckv_ref[:, late] = ref[0, z, :rows, columns : 2 * columns]
            o_ref[z] = ref[0, z, :rows, 2 * columns : 3 * columns]
            cq_ref[:, part] = ref[0, z, :rows, 3 * columns :]
        bias_ref[...] = ref[0, :, rows:, :]

    other = (pl.program_id(0) & 1) ^ (info_ref[0] & 1)

    @pl.when(other == 0)
    def _():
        put(near_ref)

    @pl.when(other != 0)
    def _():
        put(far_ref)


def assemble(info, near, far, shards, columns, bias_rows):
    _, tensors, rows, packed = near.shape
    rows -= bias_rows
    width = tensors * columns
    height = shards * rows
    side = pl.BlockSpec((1,) + near.shape[1:], lambda s, i: ((s >> 1) ^ (i[0] >> 1), 0, 0, 0))
    bias = (tensors, bias_rows, packed)
    return pl.pallas_call(
        assemble_kernel,
        grid_spec=pltpu.PrefetchScalarGridSpec(
            num_scalar_prefetch=1,
            grid=(shards,),
            in_specs=[side, side],
            out_specs=[
                pl.BlockSpec((rows, 2 * width), lambda s, i: (s, 0)),
                pl.BlockSpec((tensors, rows, columns), lambda s, i: (0, s, 0)),
                pl.BlockSpec((rows, width), lambda s, i: (s, 0)),
                whole(bias),
            ],
        ),
        out_shape=[
            shape_of((height, 2 * width), BF16),
            shape_of((tensors, height, columns), BF16),
            shape_of((height, width), BF16),
            shape_of(bias, BF16),
        ],
        compiler_params=params(),
        cost_estimate=cost(0, near.size * 8),
        name="assemble",
    )(info, near, far)


def bias_part(bias_ref, j, start, columns):
    width = bias_ref.shape[2]
    row, lane = divmod(start, width)
    tall = bias_ref[j].astype(F32)
    full = tall[:2] + tall[2:4]
    if lane + columns <= width:
        return full[row : row + 1, lane : lane + columns]
    return jnp.concatenate(
        [full[row : row + 1, lane:], full[row + 1 : row + 2, : lane + columns - width]], axis=1
    )


def tensor_row(bias_ref, start, columns):
    return jnp.concatenate(
        [bias_part(bias_ref, j, start, columns) for j in range(bias_ref.shape[0])], axis=1
    )


def after_self_kernel(
    info_ref, x_ref, o_ref, cq_ref, ob_ref, gain_ref, shift_ref, bias_ref, *rest, scale
):
    mix_refs, (sum_ref, low_ref, q_ref, joined_ref) = rest[:-4], rest[-4:]
    joined_ref[...] = jnp.concatenate([mix_ref[...] for mix_ref in mix_refs], axis=1)
    total = x_ref[0] + ob_ref[...]
    for j, mix_ref in enumerate(mix_refs):
        total = total + nt(mix_ref[...], o_ref[j])
    sum_ref[...] = total
    hidden = norm_parts(total)[0] * gain_ref[...] + shift_ref[...]
    low = hidden.astype(BF16)
    low_ref[...] = low
    bias = tensor_row(bias_ref, 0, mix_refs[0].shape[1])
    q_ref[...] = ((nn(low, cq_ref[...]) + bias) * scale).astype(BF16)


def after_self(info, x, o, cq, ob, gain, shift, bias, mixes, scale):
    width = x.shape[2]
    rows = mixes[0].shape[0]
    return pl.pallas_call(
        functools.partial(after_self_kernel, scale=scale),
        grid_spec=pltpu.PrefetchScalarGridSpec(
            num_scalar_prefetch=1,
            grid=(1,),
            in_specs=[pl.BlockSpec((1, rows, width), lambda s, i: (0, i[2], 0))]
            + [whole(a.shape) for a in (o, cq, ob, gain, shift, bias) + tuple(mixes)],
            out_specs=[whole((rows, width))] * 4,
        ),
        out_shape=[shape_of((rows, width), F32)] + [shape_of((rows, width), BF16)] * 3,
        compiler_params=params(),
        cost_estimate=cost(rows * width * width * 4, width * width * 4 + rows * width * 12),
        name="after_self",
    )(info, x, o, cq, ob, gain, shift, bias, *mixes)


def encode_kernel(info_ref, own_ref, sent_ref, w_ref, bias_ref, low_ref, kv_ref, *, columns):
    width = low_ref.shape[1]
    half = pl.num_programs(0) // 2

    @pl.when(pl.program_id(0) < half)
    def _():
        low_ref[...] = own_ref[0].astype(BF16)

    @pl.when(pl.program_id(0) >= half)
    def _():
        low_ref[...] = sent_ref[...]

    out = nn(low_ref[...], w_ref[...])
    kv_ref[:, :width] = out[:, :width].astype(BF16)
    kv_ref[:, width:] = (
        out[:, width:] + tensor_row(bias_ref, columns, columns)
    ).astype(BF16)


def encode(info, own, sent, w, bias, columns):
    _, rows, width = own.shape
    half = rows // TILE
    return pl.pallas_call(
        functools.partial(encode_kernel, columns=columns),
        grid_spec=pltpu.PrefetchScalarGridSpec(
            num_scalar_prefetch=1,
            grid=(2 * half,),
            in_specs=[
                pl.BlockSpec((1, TILE, width), lambda b, i: (0, jnp.minimum(b, half - 1), 0)),
                pl.BlockSpec((TILE, width), lambda b, i: (jnp.maximum(b - half, 0), 0)),
                whole(w.shape),
                whole(bias.shape),
            ],
            out_specs=[
                pl.BlockSpec((TILE, width), lambda b, i: (b, 0)),
                pl.BlockSpec((TILE, 2 * width), lambda b, i: (b, 0)),
            ],
        ),
        out_shape=[shape_of((2 * rows, width), BF16), shape_of((2 * rows, 2 * width), BF16)],
        compiler_params=params(),
        cost_estimate=cost(rows * width * width * 8, rows * width * 14),
        name="encode",
    )(info, own, sent, w, bias)


def gelu_parts(values):
    half = 0.5 * (1.0 + lax.erf(values * (0.5**0.5)))
    slope = half + values * (jnp.exp(-0.5 * values * values) * (0.5 / jnp.pi) ** 0.5)
    return values * half, slope


def feed_kernel(
    info_ref,
    sum_ref,
    vectors_ref,
    mix_ref,
    packed_ref,
    bias_ref,
    goal_ref,
    w_ref,
    result_ref,
    dw_ref,
    grad_ref,
    grad_low_ref,
    grad_mix_ref,
    sums_ref,
    two_ref,
    low_ref,
    low_t_ref,
    act_ref,
    slope_ref,
    acc_ref,
    three_low_ref,
    three_t_ref,
    co_ref,
):
    phase, z = pl.program_id(0), pl.program_id(1)
    tensors = pl.num_programs(1)
    rows, width = sum_ref.shape
    hidden_units = w_ref.shape[3]
    piece = width // w_ref.shape[1]
    up = w_ref[0, :, :piece].reshape(width, hidden_units)
    down = w_ref[0, :, piece : 2 * piece].reshape(width, hidden_units)
    gain1, shift1, cob, gain2, shift2, downb, gain3, shift3 = (
        vectors_ref[i : i + 1, :] for i in range(1, 9)
    )

    @pl.when((phase == 0) & (z == 0))
    def _():
        _, shards, chunk, _ = packed_ref.shape
        columns = co_ref.shape[2]
        for t in range(co_ref.shape[0]):
            for s in range(shards):
                for i in range(piece // chunk):
                    start = s * piece + i * chunk
                    co_ref[t, start : start + chunk, :] = packed_ref[
                        t, s, :, i * columns : (i + 1) * columns
                    ]
        hidden_one = norm_parts(sum_ref[...])[0] * gain1 + shift1
        sum_two = hidden_one + cob
        for j in range(co_ref.shape[0]):
            part = mix_ref[:, j * columns : (j + 1) * columns]
            sum_two = sum_two + nt(part, co_ref[info_ref[2] ^ j])
        two_ref[...] = sum_two
        hidden_two = norm_parts(sum_two)[0] * gain2 + shift2
        low_ref[...] = hidden_two.astype(BF16)
        low_t_ref[...] = hidden_two.T.astype(BF16)
        acc_ref[...] = hidden_two + downb
        sums_ref[...] = jnp.zeros_like(sums_ref)

    @pl.when(phase == 0)
    def _():
        bias = bias_part(bias_ref, z ^ info_ref[2], 2 * co_ref.shape[2], hidden_units)
        pre = nn(low_ref[...], up) + bias
        value, slope = gelu_parts(pre)
        act = value.astype(BF16)
        act_ref[z] = act
        slope_ref[z] = slope
        acc_ref[...] += nt(act, down)

    @pl.when((phase == 0) & (z == tensors - 1))
    def _():
        sum_three = acc_ref[...]
        result = norm_parts(sum_three)[0] * gain3 + shift3
        result_ref[...] = result.astype(BF16)
        grad_three, *both = norm_back(sum_three, gain3, goal_ref[0])
        sums_ref[0:1, :] = both[0]
        sums_ref[1:2, :] = both[1]
        sums_ref[2:3, :] = jnp.sum(grad_three, axis=0, keepdims=True)
        acc_ref[...] = grad_three
        three_low_ref[...] = grad_three.astype(BF16)
        three_t_ref[...] = grad_three.T.astype(BF16)

    @pl.when(phase == 1)
    def _():
        grad_pre = nn(three_low_ref[...], down) * slope_ref[z]
        sums_ref[pl.ds(8 + z, 1), :hidden_units] = jnp.sum(grad_pre, axis=0, keepdims=True)
        pre_low = grad_pre.astype(BF16)
        acc_ref[...] += nt(pre_low, up)
        shards = dw_ref.shape[1]
        dw_ref[0, :, 0] = (
            nn(low_t_ref[...], pre_low).astype(BF16).reshape(shards, piece, hidden_units)
        )
        dw_ref[0, :, 1] = (
            nn(three_t_ref[...], act_ref[z]).astype(BF16).reshape(shards, piece, hidden_units)
        )

    @pl.when((phase == 1) & (z == tensors - 1))
    def _():
        grad_two, *both = norm_back(two_ref[...], gain2, acc_ref[...])
        sums_ref[3:4, :] = both[0]
        sums_ref[4:5, :] = both[1]
        sums_ref[5:6, :] = jnp.sum(grad_two, axis=0, keepdims=True)
        grad_ref[...] = grad_two
        low = grad_two.astype(BF16)
        grad_low_ref[...] = low
        columns = co_ref.shape[2]
        for j in range(co_ref.shape[0]):
            part = nn(low, co_ref[info_ref[2] ^ j]).astype(BF16)
            grad_mix_ref[:, j * columns : (j + 1) * columns] = part


def feed(info, sum_one, vectors, mix, columns, chunk, bias, goal, w):
    rows, width = sum_one.shape
    tensors, shards, taller, hidden_units = w.shape
    piece = width // shards
    assert hidden_units == width
    grads = (tensors, shards, 2, piece, hidden_units)
    head = (sum_one, vectors, mix)
    last = 2 * piece // chunk
    return pl.pallas_call(
        feed_kernel,
        grid_spec=pltpu.PrefetchScalarGridSpec(
            num_scalar_prefetch=1,
            grid=(2, tensors),
            in_specs=[whole(a.shape) for a in head]
            + [
                pl.BlockSpec(
                    (tensors, shards, chunk, hidden_units), lambda p, z, i: (0, 0, last, 0)
                ),
                whole(bias.shape),
                pl.BlockSpec((1, rows, width), lambda p, z, i: (0, i[2], 0)),
                pl.BlockSpec((1, shards, taller, hidden_units), lambda p, z, i: (z, 0, 0, 0)),
            ],
            out_specs=[
                whole((rows, width)),
                pl.BlockSpec((1,) + grads[1:], lambda p, z, i: (p * z, 0, 0, 0, 0)),
                whole((rows, width)),
                whole((rows, width)),
                whole((rows, width)),
                whole((16, width)),
            ],
            scratch_shapes=[
                pltpu.VMEM((rows, width), F32),
                pltpu.VMEM((rows, width), BF16),
                pltpu.VMEM((width, rows), BF16),
                pltpu.VMEM((tensors, rows, hidden_units), BF16),
                pltpu.VMEM((tensors, rows, hidden_units), F32),
                pltpu.VMEM((rows, width), F32),
                pltpu.VMEM((rows, width), BF16),
                pltpu.VMEM((width, rows), BF16),
                pltpu.VMEM((tensors, width, columns), BF16),
            ],
        ),
        out_shape=[
            shape_of((rows, width), BF16),
            shape_of(grads, BF16),
            shape_of((rows, width), F32),
            shape_of((rows, width), BF16),
            shape_of((rows, width), BF16),
            shape_of((16, width), F32),
        ],
        compiler_params=params(),
        cost_estimate=cost(rows * w.size * 6, w.size * 6, rows * width * tensors * 2),
        name="feed",
    )(info, *head, w, bias, goal, w)


def before_self_kernel(
    info_ref, grad_ref, dq_ref, cq_ref, sum_ref, gain_ref, dv_ref, o_ref, *out_refs
):
    grad_one_ref, low_ref, sums_ref = out_refs[:3]
    mix_refs = out_refs[3:]
    tensors, _, columns = o_ref.shape
    grad_hidden = grad_ref[...] + nt(dq_ref[...], cq_ref[...])
    grad_one, gain, shift = norm_back(sum_ref[...], gain_ref[...], grad_hidden)
    grad_one_ref[...] = grad_one
    low = grad_one.astype(BF16)
    low_ref[...] = low
    for j, mix_ref in enumerate(mix_refs):
        mix_ref[...] = nn(low, o_ref[j]).astype(BF16)
    sums_ref[...] = jnp.zeros_like(sums_ref)
    sums_ref[0:1, :] = gain
    sums_ref[1:2, :] = shift
    sums_ref[2:3, :] = jnp.sum(grad_one, axis=0, keepdims=True)
    queries = jnp.sum(dq_ref[...].astype(F32), axis=0, keepdims=True)
    values = jnp.sum(dv_ref[...].astype(F32), axis=0, keepdims=True)
    for j in range(tensors):
        part = slice(j * columns, (j + 1) * columns)
        at = info_ref[2] ^ j
        sums_ref[pl.ds(8 + at, 1), :columns] = queries[:, part]
        sums_ref[pl.ds(8 + tensors + at, 1), :columns] = values[:, part]


def before_self(info, grad, dq, cq, sum_one, gain, dv, o):
    rows, width = grad.shape
    tensors, _, columns = o.shape
    args = (grad, dq, cq, sum_one, gain, dv, o)
    return pl.pallas_call(
        before_self_kernel,
        grid_spec=pltpu.PrefetchScalarGridSpec(
            num_scalar_prefetch=1,
            grid=(1,),
            in_specs=[whole(a.shape) for a in args],
            out_specs=[whole((rows, width))] * 2
            + [whole((8 + 2 * tensors, width))]
            + [whole((rows, columns))] * tensors,
        ),
        out_shape=[
            shape_of((rows, width), F32),
            shape_of((rows, width), BF16),
            shape_of((8 + 2 * tensors, width), F32),
        ]
        + [shape_of((rows, columns), BF16)] * tensors,
        compiler_params=params(),
        cost_estimate=cost(rows * width * width * 4, width * width * 6 + rows * width * 14),
        name="before_self",
    )(info, *args)


def encoder_grad_kernel(dk_ref, dv_ref, w_ref, keep_ref, send_ref):
    width = dk_ref.shape[1]
    part = nt(dk_ref[...], w_ref[:, :width]) + nt(dv_ref[...], w_ref[:, width:])
    half = pl.num_programs(0) // 2

    @pl.when(pl.program_id(0) < half)
    def _():
        send_ref[...] = part.astype(BF16)

    @pl.when(pl.program_id(0) >= half)
    def _():
        keep_ref[...] = part


def encoder_grad(dk, dv, w):
    keys, width = dk.shape
    half = keys // TILE // 2
    side = pl.BlockSpec((TILE, width), lambda b: (jnp.where(b < half, b + half, b - half), 0))
    return pl.pallas_call(
        encoder_grad_kernel,
        grid=(2 * half,),
        in_specs=[side, side, whole(w.shape)],
        out_specs=[
            pl.BlockSpec((TILE, width), lambda b: (jnp.maximum(b - half, 0), 0)),
            pl.BlockSpec((TILE, width), lambda b: (jnp.minimum(b, half - 1), 0)),
        ],
        out_shape=[shape_of((keys // 2, width), F32), shape_of((keys // 2, width), BF16)],
        compiler_params=params(),
        cost_estimate=cost(keys * width * width * 4, keys * width * 10),
        name="encoder_grad",
    )(dk, dv, w)


def square_grads_kernel(info_ref, *refs, ctxs, groups):
    count = sum(groups)
    left_refs, right_refs = refs[:count], refs[count : 2 * count]
    flipped = refs[-count:]
    outs = refs[2 * count : -count]
    i, other = pl.program_id(0), pl.program_id(1)
    _, _, tensors, share, packed = outs[0].shape
    piece = share * ctxs
    columns = packed // groups[0]

    @pl.when((i == 0) & (other == 0))
    def _():
        for left_ref, flipped_ref in zip(left_refs, flipped):
            flipped_ref[...] = flip(left_ref[...])

    s = ((i ^ (info_ref[0] >> 1)) << 1) + ((info_ref[0] & 1) ^ other)
    rows = pl.ds(pl.multiple_of(s * piece, piece), piece)
    grads = [
        nn(flipped_ref[rows, :], right_ref[...]).astype(BF16)
        for flipped_ref, right_ref in zip(flipped, right_refs)
    ]

    def put(refs):
        for z in range(tensors):
            part = slice(z * columns, (z + 1) * columns)
            start = 0
            for ref, size in zip(refs, groups):
                tile = jnp.concatenate(
                    [grad[:, part] for grad in grads[start : start + size]], axis=1
                )
                start += size
                for r in range(ctxs):
                    chosen = tile[:share]
                    for c in range(1, ctxs):
                        chosen = jnp.where(
                            (info_ref[1] ^ r) == c, tile[c * share : (c + 1) * share], chosen
                        )
                    ref[0, r, z] = chosen

    @pl.when(other == 0)
    def _():
        put(outs[: len(groups)])

    @pl.when(other != 0)
    def _():
        put(outs[len(groups) :])


def square_grads(info, pairs, groups, sizes):
    shards, ctxs, tensors = sizes
    width = pairs[0][0].shape[1]
    share = width // shards // ctxs
    args = [left for left, _ in pairs] + [right for _, right in pairs]
    sides = [
        (shards // 2, ctxs, tensors, share, size * width // tensors) for size in groups
    ] * 2
    return pl.pallas_call(
        functools.partial(square_grads_kernel, ctxs=ctxs, groups=groups),
        grid_spec=pltpu.PrefetchScalarGridSpec(
            num_scalar_prefetch=1,
            grid=(shards // 2, 2),
            in_specs=[whole(a.shape) for a in args],
            out_specs=[
                pl.BlockSpec((1,) + side[1:], lambda i, c, n: (i, 0, 0, 0, 0)) for side in sides
            ],
            scratch_shapes=[pltpu.VMEM((width, left.shape[0]), BF16) for left, _ in pairs],
        ),
        out_shape=[shape_of(side, BF16) for side in sides],
        compiler_params=params(),
        cost_estimate=cost(2 * width * sum(a.size for a in args), width * width * 8),
        name="square_grads",
    )(info, *args)


def input_grad_kernel(
    info_ref, dq_ref, down_ref, dtrunk_ref, came_ref, low_ref, w_ref, *rest, ctxs, tensors
):
    part_refs = rest[:tensors]
    near_ref, far_ref, dw_ref = rest[tensors:]
    b = pl.program_id(0)

    @pl.when(b == 0)
    def _():
        dw_ref[...] = jnp.zeros_like(dw_ref)

    trunk = dtrunk_ref[...].astype(F32) + came_ref[...].astype(F32)
    dkv = (down_ref[...] + jnp.where(info_ref[1] == 0, trunk, 0.0)).astype(BF16)
    grads = jnp.concatenate([dq_ref[...], dkv], axis=1)
    dw_ref[...] += tn(low_ref[...], grads)
    put_slot(b ^ info_ref[2], nt(grads, w_ref[...]), part_refs)

    @pl.when(b == pl.num_programs(0) - 1)
    def _():
        halves, _, share, _ = near_ref.shape
        for other, ref in ((0, near_ref), (1, far_ref)):
            for i in range(halves):
                s = ((i ^ (info_ref[0] >> 1)) << 1) + ((info_ref[0] & 1) ^ other)
                for r in range(ctxs):
                    start = (s * ctxs + (info_ref[1] ^ r)) * share
                    ref[i, r] = dw_ref[pl.ds(pl.multiple_of(start, share), share), :].astype(BF16)


def input_grad(info, dq, down, dtrunk, came, low, w, sizes):
    shards, ctxs, tensors = sizes
    rows, columns = dq.shape
    width = low.shape[1]
    share = width // shards // ctxs
    side = (shards // 2, ctxs, share, 3 * columns)

    def tile(n):
        return pl.BlockSpec((TILE, n), lambda b, i: (b, 0))

    return pl.pallas_call(
        functools.partial(input_grad_kernel, ctxs=ctxs, tensors=tensors),
        grid_spec=pltpu.PrefetchScalarGridSpec(
            num_scalar_prefetch=1,
            grid=(rows // TILE,),
            in_specs=[
                tile(columns),
                tile(2 * columns),
                tile(2 * columns),
                tile(2 * columns),
                tile(width),
                whole(w.shape),
            ],
            out_specs=[whole((TILE, width))] * tensors
            + [whole(side), whole(side)],
            scratch_shapes=[pltpu.VMEM((width, 3 * columns), F32)],
        ),
        out_shape=[shape_of((TILE, width), F32)]
        + [shape_of((TILE, width), BF16)] * (tensors - 1)
        + [shape_of(side, BF16)] * 2,
        compiler_params=params(),
        cost_estimate=cost(rows * width * columns * 12, rows * width * 14),
        name="input_grad",
    )(info, dq, down, dtrunk, came, low, w)


def lay_rows_kernel(info_ref, *refs):
    in_refs, out_ref = refs[:-1], refs[-1]
    out_ref[...] = take_slot(pl.program_id(0) ^ info_ref[2], in_refs).astype(F32)


def lay_rows(info, parts):
    rows, width = parts[0].shape
    return pl.pallas_call(
        lay_rows_kernel,
        grid_spec=pltpu.PrefetchScalarGridSpec(
            num_scalar_prefetch=1,
            grid=(len(parts),),
            in_specs=[whole((rows, width))] * len(parts),
            out_specs=pl.BlockSpec((rows, width), lambda b, i: (b, 0)),
        ),
        out_shape=shape_of((rows * len(parts), width), F32),
        compiler_params=params(),
        cost_estimate=cost(0, rows * width * len(parts) * 6),
        name="lay_rows",
    )(info, *parts)


def local(sizes, *args):
    (
        layer_input,
        encoder_out,
        enc_length,
        parent_ids,
        token_segment,
        self_query,
        self_key,
        self_value,
        self_output,
        cross_query,
        cross_key,
        cross_value,
        cross_output,
        ffn_up,
        ffn_down,
        self_qbias,
        self_vbias,
        self_obias,
        cross_qbias,
        cross_vbias,
        cross_obias,
        ffn_upbias,
        ffn_downbias,
        norm1_gain,
        norm1_shift,
        norm2_gain,
        norm2_shift,
        norm3_gain,
        norm3_shift,
        out_grad,
    ) = args
    shards, ctxs, tensors = sizes["shard"], sizes["ctx"], sizes["tensor"]
    me_ctx = lax.axis_index("ctx")
    info = jnp.stack([lax.axis_index("shard"), me_ctx, lax.axis_index("tensor")]).astype(jnp.int32)
    scale = HEAD_DIM ** (-0.5)
    local_rows, width = layer_input.shape[1:]
    piece, columns = self_query.shape
    heads = columns // HEAD_DIM
    seg = token_segment.shape[1] // parent_ids.shape[1]
    assert local_rows == tensors * TILE and ctxs == 2

    def swap(a, axis, bit):
        return lax.ppermute(a, axis, [(i, i ^ bit) for i in range(sizes[axis])])

    shard_bits = [("shard", 1 << k) for k in range(1, shards.bit_length() - 1)]

    def over_tensor(a):
        return [a] + [swap(a, "tensor", j) for j in range(1, tensors)]

    def grow(a, axis, bit, *others):
        return jnp.stack(tie([a, swap(a, axis, bit)], *others))

    def add(a, b):
        return (a.astype(F32) + b.astype(F32)).astype(BF16)

    def reduce_levels(near, far):
        came = swap(far, "shard", 1)
        lead = (2,) * len(shard_bits) + near.shape[1:]
        near, came = near.reshape(lead), came.reshape(lead)

        for axis, bit in list(reversed(shard_bits)) + [("ctx", 1)]:
            send = add(near[1], came[1])
            near, came = add(near[0], came[0]), swap(send, axis, bit)
        return add(near, came)

    def join_ctx(mine):
        other = swap(mine, "ctx", 1)
        first = me_ctx == 0
        return jnp.concatenate([jnp.where(first, mine, other), jnp.where(first, other, mine)])

    def row(vector):
        return vector.reshape(1, -1)

    def tie(a, *others):
        return lax.optimization_barrier((a,) + others)[0]

    vectors = jnp.stack(
        [
            self_obias,
            norm1_gain,
            norm1_shift,
            cross_obias,
            norm2_gain,
            norm2_shift,
            ffn_downbias,
            norm3_gain,
            norm3_shift,
        ]
    )

    pack = tensors if piece % (16 * tensors) == 0 else 1
    chunk = piece // pack
    packed_co = jnp.concatenate(
        [cross_output.T[i * chunk : (i + 1) * chunk] for i in range(pack)], axis=1
    )
    packed_co = jnp.pad(packed_co, ((0, 0), (0, width - packed_co.shape[1])))
    ffn_piece = jnp.concatenate([ffn_up, ffn_down.T, packed_co], axis=0)
    bias = jnp.concatenate([cross_qbias, cross_vbias, ffn_upbias])
    bias = jnp.pad(bias, (0, -bias.shape[0] % width)).reshape(-1, width)
    bias_high = lax.reduce_precision(bias, 8, 7)
    bias_rows = 16
    bias = jnp.concatenate([bias_high, bias - bias_high]).astype(BF16)
    bias = jnp.pad(bias, ((0, bias_rows - bias.shape[0]), (0, 0)))
    squares = over_tensor(
        jnp.concatenate(
            [
                jnp.concatenate([cross_key, cross_value, self_output.T, cross_query], axis=1),
                bias,
            ],
            axis=0,
        )
    )
    enc_sent = swap(encoder_out[0].astype(BF16), "ctx", 1)
    qkv_weights = lax.all_gather(
        jnp.concatenate([self_query, self_key, self_value], axis=1), "shard", axis=0, tiled=True
    )

    scalars = (info, parent_ids[0], token_segment[0])
    q, kv, input_low = project(layer_input, qkv_weights, row(self_qbias), row(self_vbias), scale)
    squares = jnp.stack(tie(squares, q))
    ffn_all = lax.all_gather(tie(ffn_piece, squares), ("tensor", "shard"), axis=0, tiled=True)
    kv_sent = lax.ppermute(tie(kv, squares), "ctx", [(0, 1)])
    for axis, bit in shard_bits[:-1]:
        squares = grow(squares, axis, bit, kv_sent)
    kv_sent = tie(kv_sent, squares)
    *mixes, self_logs = self_forward(scalars, q, kv, kv_sent, tensors, heads, seg)
    squares = grow(squares, *shard_bits[-1], self_logs)
    near = squares.reshape((shards // 2,) + squares.shape[-3:])
    far = swap(near, "shard", 1)
    all_heads = mixes[:1] + [swap(mixes[j], "tensor", j) for j in range(1, tensors)]
    weight_ckv, weight_o, weight_cq, bias = assemble(info, near, far, shards, columns, bias_rows)
    enc_low, ckv = encode(info, encoder_out, enc_sent, weight_ckv, bias, columns)
    all_heads = all_heads[:1] + list(tie(all_heads[1:], ckv))
    sum_one, one_low, cq, self_mix = after_self(
        info,
        layer_input,
        weight_o,
        weight_cq,
        vectors[0:1],
        vectors[1:2],
        vectors[2:3],
        bias,
        all_heads,
        scale,
    )

    cross_scalars = (info, enc_length)
    cross_mix, cross_logs = cross_forward(cross_scalars, cq, ckv)

    result, ffn_grads, grad_two, two_grad_low, grad_cmix, feed_sums = feed(
        info,
        sum_one,
        vectors,
        cross_mix,
        columns,
        chunk,
        bias,
        out_grad,
        ffn_all.reshape(tensors, shards, -1, width),
    )
    ffn_grads = lax.psum_scatter(
        ffn_grads.reshape(-1, ffn_grads.shape[-1]),
        ("tensor", "shard"),
        scatter_dimension=0,
        tiled=True,
    )
    result_parts = [result] + [swap(result, "tensor", j) for j in range(1, tensors - 1)]

    dcq, dck, dcv = cross_backward(cross_scalars, cq, ckv, grad_cmix, cross_mix, cross_logs, scale)
    grad_one, one_grad_low, self_sums, *grad_mixes = before_self(
        info, grad_two, dcq, weight_cq, sum_one, vectors[1:2], dcv, weight_o
    )
    head_grads = grad_mixes[:1] + [swap(grad_mixes[j], "tensor", j) for j in range(1, tensors)]
    mesh_sizes = (shards, ctxs, tensors)
    result_parts = result_parts[:1] + list(tie(result_parts[1:], one_grad_low))
    enc_keep, enc_send = encoder_grad(tie(dck, result_parts[1:]), dcv, weight_ckv)
    enc_send, head_grads = tie((enc_send, head_grads), enc_send)
    result_parts.append(swap(tie(result, head_grads), "tensor", tensors - 1))

    dq, down, dtrunk, late_sums = self_backward(
        scalars, q, kv, kv_sent, head_grads, mixes, self_logs, heads, seg, scale, width
    )
    trunk_came = lax.ppermute(dtrunk, "ctx", [(1, 0)])
    enc_came, result_parts = tie((swap(enc_send, "ctx", 1), result_parts), dtrunk)
    enc_mine = (enc_keep + enc_came.astype(F32)).astype(BF16)
    near_a, near_b, far_a, far_b = square_grads(
        info,
        [
            (tie(enc_low, enc_mine), dck),
            (enc_low, dcv),
            (one_grad_low, self_mix),
            (one_low, dcq),
            (two_grad_low, cross_mix),
        ],
        (2, 3),
        mesh_sizes,
    )
    result_all = lay_rows(info, tie(result_parts, near_a))

    def path(near, far, order):
        lead = (2,) * len(shard_bits) + near.shape[1:]
        dims = list(reversed(shard_bits)) + [("ctx", 1)]
        came = yield swap(far, "shard", 1)
        near, came = near.reshape(lead), came.reshape(lead)
        for axis, bit in order:
            dim = dims.index((axis, bit))
            dims.pop(dim)
            index = (slice(None),) * dim
            send = add(near[index + (1,)], came[index + (1,)])
            keep = add(near[index + (0,)], came[index + (0,)])
            near, came = keep, (yield swap(send, axis, bit))
        return add(near, came)

    high = list(reversed(shard_bits))
    paths = [path(near_a, far_a, [("ctx", 1)] + high), path(near_b, far_b, high + [("ctx", 1)])]
    waits = tie([next(p) for p in paths], result_all)
    waits = [p.send(w) for p, w in zip(paths, waits)]
    sums = jnp.concatenate([feed_sums, self_sums, late_sums], axis=0)
    for axis, bit in [("shard", 1)] + shard_bits:
        sums = sums + swap(sums, axis, bit)
    trunk_came = tie(trunk_came, far_a, far_b)
    *parts, near, far = input_grad(
        info, dq, down, dtrunk, trunk_came, input_low, qkv_weights, mesh_sizes
    )
    part_came = [swap(parts[j], "tensor", j) for j in range(1, tensors)]
    waits, ffn_grads = tie((waits, ffn_grads), parts[0])
    grad_encoder = lax.psum(tie(enc_mine, ffn_grads), "tensor").astype(F32)
    ffn_grads = ffn_grads.astype(F32) + swap(ffn_grads, "ctx", 1).astype(F32)
    for _ in range(len(high)):
        waits = [p.send(w) for p, w in zip(paths, waits)]
    blocks = []
    for p, w in zip(paths, waits):
        try:
            p.send(w)
        except StopIteration as end:
            blocks.append(end.value)
    qkv_grads = join_ctx(reduce_levels(near, far)).astype(F32)
    grad_q, grad_k, grad_v = (qkv_grads[:, i * columns : (i + 1) * columns] for i in range(3))
    sums = sums + swap(tie(sums, parts[0]), "ctx", 1)
    part_came = tie(part_came, sums, qkv_grads, ffn_grads, blocks)
    input_mine = grad_one + parts[0]
    for part in part_came:
        input_mine = input_mine + part.astype(F32)
    input_mine = input_mine.astype(BF16)
    input_all = over_tensor(input_mine)
    sums, blocks = tie((sums, blocks), input_mine)
    others = over_tensor(sums)
    square_sums = []
    for block in blocks:
        total = block[0].astype(F32)
        for j in range(1, tensors):
            total = total + swap(block[j], "tensor", j).astype(F32)
        square_sums.append(total.astype(BF16))
    sums = others[0]
    for other in tie(others[1:], input_all):
        sums = sums + other
    squares = join_ctx(jnp.concatenate(square_sums, axis=1)).astype(F32)
    grad_ck, grad_cv, grad_o, grad_cq, grad_co = (
        squares[:, i * columns : (i + 1) * columns] for i in range(5)
    )
    grad_input = lay_rows(info, input_all)
    me_tensor = info[2]

    def mine(start, size):
        return lax.dynamic_slice(sums, (start + me_tensor, 0), (1, size)).reshape(-1)

    base = 16 + 8
    later = base + 2 * tensors

    return (
        result_all[None],
        grad_input[None],
        grad_encoder[None],
        grad_q,
        grad_k,
        grad_v,
        grad_o.T,
        grad_cq,
        grad_ck,
        grad_cv,
        grad_co.T,
        ffn_grads[:piece],
        ffn_grads[piece:].T,
        mine(later, columns),
        mine(later + tensors, columns),
        sums[18],
        mine(base, columns),
        mine(base + tensors, columns),
        sums[5],
        mine(8, ffn_upbias.shape[0]),
        sums[2],
        sums[16],
        sums[17],
        sums[3],
        sums[4],
        sums[0],
        sums[1],
    )


def solution(mesh):
    sizes = {axis: mesh.shape[axis] for axis in ("shard", "ctx", "tensor")}
    rows = P("shard", "ctx", None)
    tall, wide = P("shard", "tensor"), P("tensor", "shard")
    mats = (tall, tall, tall, wide, tall, tall, tall, wide, tall, wide)
    part = P("tensor")
    vectors = (part, part, P(), part, part, P(), part) + (P(),) * 7
    tree = P("shard", None)
    return jax.shard_map(
        functools.partial(local, sizes),
        mesh=mesh,
        in_specs=(rows, rows, P("shard"), tree, tree) + mats + vectors + (rows,),
        out_specs=(rows, rows, rows) + mats + vectors,
        check_vma=False,
    )
```

time: 681 us -> 453 us (0.67); the launches traced: 671 us -> 451 us
  Pallas kernels: 61.1 us -> 157 us
  local copies, waits for them, and re-layouts: 107 us -> 13 us
  waiting for transfers between devices: 239 us -> 157 us
  matrix products: 66.8 us -> 0 us
  other arithmetic: 77.7 us -> 22.5 us
  starting transfers between devices: 115 us -> 76.6 us
  between operations: 4.13 us -> 15.2 us
  blocking collectives: 0 us -> 10.1 us
    ppermute x90 -> x46, waiting for transfers between devices: 237 us -> 142 us  [swap(): return lax.ppermute(a, axis, [(i, i ^ bit) for i in range(sizes[axis])])]
    pallas_call x1 -> x12, Pallas kernels: 17.4 us -> 109 us  [the longest x1 22.5 us: feed(): pl.pallas_call(feed_kernel, grid_spec=pltpu.PrefetchScalarGridSpec(num_sc...]
    dot_general x38 -> x0, matrix products: 66.8 us -> none  [dot_of(): lax.dot_general(a, b, (((a_dim,), (b_dim,)), ((), ())), preferred_element...]
    ppermute x90 -> x46, starting transfers between devices: 110 us -> 71.7 us  [swap(): return lax.ppermute(a, axis, [(i, i ^ bit) for i in range(sizes[axis])])]
    unnamed x238 -> x96, local copies, waits for them, and re-layouts: 30.5 us -> 6.56 us
    select_n x22 -> x2, other arithmetic: 21.4 us -> 0.11 us  [join_ctx(): jnp.where(first, mine, other)]
    concatenate x14 -> x2, local copies, waits for them, and re-layouts: 21.6 us -> 0.8 us  [the longest x1 0.8 us: local(): bias = jnp.concatenate([cross_qbias, cross_vbias, ffn_upbias])]
    slice x29 -> x3, local copies, waits for them, and re-layouts: 22.2 us -> 1.72 us  [the longest x1 0.86 us: local(): qkv_grads[:, i * columns:(i + 1) * columns]]
  transfers between devices with their start and end apart: 92 -> 51, of which waited for: 38 -> 24; matrix products, arithmetic and copies ran while one was open for 27% -> 6% of each run, Pallas kernels for 7% -> 29%
where the time goes in v2:
time: 453 us; the launch traced here: 451 us
  Pallas kernels  157 us (35%)
  waiting for transfers between devices  157 us (35%)
  starting transfers between devices  76.6 us (17%)
  other arithmetic  22.5 us (5%)
  between operations  15.2 us (3%)
  local copies, waits for them, and re-layouts  13 us (3%)
  blocking collectives  10.1 us (2%)
    ppermute x46, waiting for transfers between devices, swap(): return lax.ppermute(a, axis, [(i, i ^ bit) for i in range(sizes[axis])])  142 us
    ppermute x46, starting transfers between devices, swap(): return lax.ppermute(a, axis, [(i, i ^ bit) for i in range(sizes[axis])])  71.7 us
    pallas_call x1, Pallas kernels, feed(): pl.pallas_call(feed_kernel, grid_spec=pltpu.PrefetchScalarGridSpec(num_sc...  22.5 us
    pallas_call x1, Pallas kernels, cross_forward(): pl.pallas_call(cross_forward_kernel, grid_spec=pltpu.PrefetchScalarGridSp...  17.9 us
    pallas_call x1, Pallas kernels, cross_backward(): pl.pallas_call(functools.partial(cross_backward_kernel, scale=scale), gri...  16.3 us
    pallas_call x1, Pallas kernels, self_backward(): pl.pallas_call(functools.partial(self_backward_kernel, heads=heads, seg=s...  16.1 us
    pallas_call x1, Pallas kernels, self_forward(): pl.pallas_call(functools.partial(self_forward_kernel, heads=heads, seg=se...  14.8 us
    ppermute x1, waiting for transfers between devices, local(): kv_sent = lax.ppermute(tie(kv, squares), 'ctx', [(0, 1)])  14.6 us
  transfers between devices with their start and end apart: 51, of which 24 were waited for; matrix products, arithmetic and copies ran while one was open for 6% of the time, Pallas kernels for 29%

profile of v2, /device:TPU:8, one launch (start us, length us, event | category | flops | bytes accessed | tf_op | source)
XLA Modules:
  0.0 451.3 jit_solution(7761160295581002011)
XLA Ops:
  10.4 3.0 collective-permute-start.1
  14.9 10.1 %all_gather.6.w_ref = bf16[768,576]{1,0:T(8,128)(2,1)} all-gather(bf16[192,576]{1,0:T(8,128)(2,1)S(1)} %pad_maximum_fusion.3), channel_id=1, replica_groups=mesh['shard'=4,'ctx'=2,'tensor'=4] {'shard'}, dimensions={0}, use_global_device_ids=true | all-gather | bytes 1105920 | tf_op jit(solution)/shard_map/all_gather | solution.py:1305
  25.2 5.5 %project.1 = (bf16[1024,192]{1,0:T(8,128)(2,1)}, bf16[1024,384]{1,0:T(8,128)(2,1)}, bf16[1024,768]{1,0:T(8,128)(2,1)}) custom-call(f32[1,1024,768]{2,1,0:T(8,128)} %x_ref.3, bf16[768,576]{1,0:T(8,128)(2,1)} %all_gather.6.w_ref, f32[1,192]{1,0:T(1,128)} %bitcast.126, f32[1,192]{1,0:T(1,128)} %bitcast.127), custom_call_target="tpu_custom_call" | custom-call | flops 9059696 | bytes 62914 | tf_op jit(solution)/shard_map/project/pallas_call | solution.py:591
  31.6 3.4 collective-permute-done.1
  35.1 6.3 %collective-permute-done.2 = bf16[208,768]{1,0:T(8,128)(2,1)S(1)} collective-permute-done((bf16[208,768]{1,0:T(8,128)(2,1)S(1)}, bf16[208,768]{1,0:T(8,128)(2,1)S(1)}, u32[]{:S(2)}, u32[]{:S(2)}) %collective-permute-start.2) | collective-permute-done | bytes 319520 | tf_op jit(solution)/shard_map/ppermute | solution.py:1234
  41.6 1.6 collective-permute-start.3
  43.2 3.5 collective-permute-start.4
  47.3 14.6 %collective-permute-done.4.sent_ref = bf16[1024,384]{1,0:T(8,128)(2,1)S(1)} collective-permute-done((bf16[1024,384]{1,0:T(8,128)(2,1)S(1)}, bf16[1024,384]{1,0:T(8,128)(2,1)S(1)}, u32[]{:S(2)}, u32[]{:S(2)}) %collective-permute-start.4) | collective-permute-done | bytes 786464 | tf_op jit(solution)/shard_map/ppermute | solution.py:1313
  62.9 14.8 %self_forward.1 = (bf16[256,192]{1,0:T(8,128)(2,1)}, bf16[256,192]{1,0:T(8,128)(2,1)}, bf16[256,192]{1,0:T(8,128)(2,1)}, bf16[256,192]{1,0:T(8,128)(2,1)}, f32[8,1024]{1,0:T(8,128)}) custom-call(s32[3]{0:T(128)} %pad_add_fusion.info_ref, s32[16]{0:T(128)} %bitcast.124, s32[2048]{0:T(1024)} %bitcast.122, bf16[1024,192]{1,0:T(8,128)(2,1)} %get-tuple-element.127.q_ref, ...), custom_call_target="tpu_custom_call" | custom-call | flops 16106127 | bytes 31457 | tf_op jit(solution)/shard_map/self_forward/pallas_call | solution.py:256
  77.7 2.0 pad_maximum_fusion.near_ref
  81.0 12.4 %collective-permute-start.9 = (bf16[512,768]{1,0:T(8,128)(2,1)}, bf16[512,768]{1,0:T(8,128)(2,1)S(1)}, u32[]{:S(2)}, u32[]{:S(2)}) collective-permute-start(bf16[512,768]{1,0:T(8,128)(2,1)} %convert_bitcast_fusion), channel_id=1, source_target_pairs={{0,4},{4,0},{1,5},{5,1},{2,6},{6,2},{3,7},{7,3},{8,12},{12,8},{9,1... | collective-permute-start | bytes 2359304 | tf_op jit(solution)/shard_map/ppermute | solution.py:1234
  93.4 3.0 collective-permute-start.7
  99.0 6.9 %assemble.1 = (bf16[768,1536]{1,0:T(8,128)(2,1)}, bf16[4,768,192]{2,1,0:T(8,128)(2,1)}, bf16[768,768]{1,0:T(8,128)(2,1)}, bf16[4,16,768]{2,1,0:T(8,128)(2,1)}) custom-call(s32[3]{0:T(128)} %pad_add_fusion.info_ref, bf16[2,4,208,768]{3,2,1,0:T(8,128)(2,1)} %copy-done, bf16[2,4,208,768]{3,2,1,0:T(8,128)(2,1)} %collective-permute-done.5.far_ref), custom_call_target="tpu_custom_call" | custom-call | bytes 102236 | tf_op jit(solution)/shard_map/assemble/pallas_call | solution.py:649
  106.0 5.8 %collective-permute-done.9.sent_ref = bf16[512,768]{1,0:T(8,128)(2,1)S(1)} collective-permute-done((bf16[512,768]{1,0:T(8,128)(2,1)}, bf16[512,768]{1,0:T(8,128)(2,1)S(1)}, u32[]{:S(2)}, u32[]{:S(2)}) %collective-permute-start.9) | collective-permute-done | bytes 786464 | tf_op jit(solution)/shard_map/ppermute | solution.py:1234
  112.7 7.4 %encode.1 = (bf16[1024,768]{1,0:T(8,128)(2,1)}, bf16[1024,1536]{1,0:T(8,128)(2,1)}) custom-call(s32[3]{0:T(128)} %pad_add_fusion.info_ref, f32[1,512,768]{2,1,0:T(8,128)} %own_ref.1, bf16[512,768]{1,0:T(8,128)(2,1)} %copy-done.10, bf16[768,1536]{1,0:T(8,128)(2,1)} %get-tuple-element.145.w_ref, bf16[4,16,768]{2,1,0:T(8,128)(2,1)} %get-tuple-element.140.bias_ref), custom_call_target="tpu_custom_call" | custom-call | flops 24159192 | bytes 55050 | tf_op jit(solution)/shard_map/encode/pallas_call | solution.py:749
  120.1 3.6 collective-permute-done.8.rest_3_
  123.7 5.1 %after_self.1 = (f32[256,768]{1,0:T(8,128)}, bf16[256,768]{1,0:T(8,128)(2,1)}, bf16[256,768]{1,0:T(8,128)(2,1)}, bf16[256,768]{1,0:T(8,128)(2,1)}) custom-call(s32[3]{0:T(128)} %pad_add_fusion.info_ref, f32[1,1024,768]{2,1,0:T(8,128)} %x_ref.3, bf16[4,768,192]{2,1,0:T(8,128)(2,1)} %get-tuple-element.138.o_ref, bf16[768,768]{1,0:T(8,128)(2,1)} %get-tuple-element.139.cq_ref, ...), custom_call_target="tpu_custom_call" | custom-call | flops 6039797 | bytes 47185 | tf_op jit(solution)/shard_map/after_self/pallas_call | solution.py:711
  128.8 17.9 %cross_forward.1 = (bf16[256,768]{1,0:T(8,128)(2,1)}, f32[48,256]{1,0:T(8,128)}) custom-call(s32[3]{0:T(128)} %pad_add_fusion.info_ref, s32[1]{0:T(128)S(6)} %copy.64.length_ref, bf16[256,768]{1,0:T(8,128)(2,1)} %get-tuple-element.150.q_ref, bf16[1024,1536]{1,0:T(8,128)(2,1)} %get-tuple-element.146.k_ref.v_ref, bf16[1024,1536]{1,0:T(8,128)(2,1)} %get-tuple-element.146.k_ref.v_ref), custom_call_target="tpu_custom_call" | custom-call | flops 16106127 | bytes 39321 | tf_op jit(solution)/shard_map/cross_forward/pallas_call | solution.py:481
  146.7 22.5 %feed.1 = (bf16[256,768]{1,0:T(8,128)(2,1)}, bf16[4,4,2,192,768]{4,3,2,1,0:T(8,128)(2,1)}, f32[256,768]{1,0:T(8,128)}, bf16[256,768]{1,0:T(8,128)(2,1)}, bf16[256,768]{1,0:T(8,128)(2,1)}, /*index=5*/f32[16,768]{1,0:T(8,128)}) custom-call(s32[3]{0:T(128)} %pad_add_fusion.info_ref, f32[256,768]{1,0:T(8,128)} %get-tuple-element.151.sum_ref, ...), custom_call_target="tpu_custom_call" | custom-call | flops 81537272 | bytes 318504 | tf_op jit(solution)/shard_map/feed/pallas_call | solution.py:897
  170.2 3.3 collective-permute-start.11
  173.5 16.3 %cross_backward.1 = (bf16[256,768]{1,0:T(8,128)(2,1)}, bf16[1024,768]{1,0:T(8,128)(2,1)}, bf16[1024,768]{1,0:T(8,128)(2,1)}) custom-call(s32[3]{0:T(128)} %pad_add_fusion.info_ref, s32[1]{0:T(128)S(6)} %copy.64.length_ref, bf16[256,768]{1,0:T(8,128)(2,1)} %get-tuple-element.150.q_ref, bf16[1024,1536]{1,0:T(8,128)(2,1)} %get-tuple-element.146.k_ref.v_ref, ...), custom_call_target="tpu_custom_call" | custom-call | flops 40265320 | bytes 78643 | tf_op jit(solution)/shard_map/cross_backward/pallas_call | solution.py:536
  189.8 6.5 %before_self.1 = (f32[256,768]{1,0:T(8,128)}, bf16[256,768]{1,0:T(8,128)(2,1)}, f32[16,768]{1,0:T(8,128)}, bf16[256,192]{1,0:T(8,128)(2,1)}, bf16[256,192]{1,0:T...) custom-call(s32[3]{0:T(128)} %pad_add_fusion.info_ref, f32[256,768]{1,0:T(8,128)} %get-tuple-element.158.grad_ref, ...), custom_call_target="tpu_custom_call" | custom-call | flops 6039797 | bytes 62914 | tf_op jit(solution)/shard_map/before_self/pallas_call | solution.py:975
  196.3 1.7 collective-permute-start.13
  198.0 1.8 collective-permute-start.14
  199.8 7.1 %encoder_grad.1 = (f32[512,768]{1,0:T(8,128)}, bf16[512,768]{1,0:T(8,128)(2,1)}) custom-call(bf16[1024,768]{1,0:T(8,128)(2,1)} %get-tuple-element.164.dk_ref.refs_5_, bf16[1024,768]{1,0:T(8,128)(2,1)} %get-tuple-element.160.dv_ref.refs_6_, bf16[768,1536]{1,0:T(8,128)(2,1)} %get-tuple-element.145.w_ref), custom_call_target="tpu_custom_call" | custom-call | flops 24159192 | bytes 78643 | tf_op jit(solution)/shard_map/encoder_grad/pallas_call | solution.py:1015
  207.0 2.9 collective-permute-done.13.rest_2_
  209.9 16.4 %collective-permute-done.14.rest_3_ = bf16[256,192]{1,0:T(8,128)(2,1)S(1)} collective-permute-done((bf16[256,192]{1,0:T(8,128)(2,1)}, bf16[256,192]{1,0:T(8,128)(2,1)S(1)}, u32[]{:S(2)}, u32[]{:S(2)}) %collective-permute-start.14) | collective-permute-done | bytes 98336 | tf_op jit(solution)/shard_map/ppermute | solution.py:1234
  226.3 8.6 %collective-permute-start.15 = (bf16[512,768]{1,0:T(8,128)(2,1)}, bf16[512,768]{1,0:T(8,128)(2,1)S(1)}, u32[]{:S(2)}, u32[]{:S(2)}) collective-permute-start(bf16[512,768]{1,0:T(8,128)(2,1)} %get-tuple-element.170), channel_id=1, source_target_pairs={{0,4},{4,0},{1,5},{5,1},{2,6},{6,2},{3,7},{7,3},{8,12},{12,8},{9,1... | collective-permute-start | bytes 2359304 | tf_op jit(solution)/shard_map/ppermute | solution.py:1234
  234.9 16.1 %self_backward.1 = (bf16[1024,192]{1,0:T(8,128)(2,1)}, f32[1024,384]{1,0:T(8,128)}, bf16[1024,384]{1,0:T(8,128)(2,1)}, f32[8,768]{1,0:T(8,128)}) custom-call(s32[3]{0:T(128)} %pad_add_fusion.info_ref, s32[16]{0:T(128)} %bitcast.125, s32[2048]{0:T(1024)} %bitcast.123, bf16[1024,192]{1,0:T(8,128)(2,1)} %get-tuple-element.127.q_ref, ...), custom_call_target="tpu_custom_call" | custom-call | flops 40265320 | bytes 78643 | tf_op jit(solution)/shard_map/self_backward/pallas_call | solution.py:412
  252.3 9.2 %collective-permute-done.16.refs_3_ = bf16[256,768]{1,0:T(8,128)(2,1)S(1)} collective-permute-done((bf16[256,768]{1,0:T(8,128)(2,1)S(1)}, bf16[256,768]{1,0:T(8,128)(2,1)S(1)}, u32[]{:S(2)}, u32[]{:S(2)}) %collective-permute-start.16) | collective-permute-done | bytes 393248 | tf_op jit(solution)/shard_map/ppermute | solution.py:1234
  262.7 13.2 %square_grads.1 = (bf16[2,2,4,96,384]{4,3,2,1,0:T(8,128)(2,1)}, bf16[2,2,4,96,576]{4,3,2,1,0:T(8,128)(2,1)}, bf16[2,2,4,96,384]{4,3,2,1,0:T(8,128)(2,1)}, bf16[2,2,4,96,576]{4,3,2,1,0:T(8,128)(2,1)}) custom-call(s32[3]{0:T(128)} %pad_add_fusion.info_ref, bf16[1024,768]{1,0:T(8,128)(2,1)} %get-tuple-element.184.refs_0_.refs_1_, ...), custom_call_target="tpu_custom_call" | custom-call | flops 66437776 | bytes 47185 | tf_op jit(solution)/shard_map/square_grads/pallas_call | solution.py:1086
  277.3 8.7 %input_grad.1 = (f32[256,768]{1,0:T(8,128)}, bf16[256,768]{1,0:T(8,128)(2,1)}, bf16[256,768]{1,0:T(8,128)(2,1)}, bf16[256,768]{1,0:T(8,128)(2,1)}, bf16[2,2,96,5...) custom-call(s32[3]{0:T(128)} %pad_add_fusion.info_ref, bf16[1024,192]{1,0:T(8,128)(2,1)} %get-tuple-element.194.dq_ref, ...), custom_call_target="tpu_custom_call" | custom-call | flops 18119392 | bytes 110100 | tf_op jit(solution)/shard_map/input_grad/pallas_call | solution.py:1142
  286.6 1.4 collective-permute-done.24
  289.4 2.1 collective-permute-start.22
  291.4 10.3 %collective-permute-done.22 = f32[40,768]{1,0:T(8,128)S(1)} collective-permute-done((f32[40,768]{1,0:T(8,128)S(1)}, f32[40,768]{1,0:T(8,128)S(1)}, u32[]{:S(2)}, u32[]{:S(2)}) %collective-permute-start.22) | collective-permute-done | bytes 122912 | tf_op jit(solution)/shard_map/ppermute | solution.py:1234
  301.8 1.5 collective-permute-start.23
  303.3 4.4 lay_rows.2
  308.4 1.4 add_convert_fusion
  310.6 1.5 collective-permute-start.30
  313.3 2.9 collective-permute-start.19
  317.2 10.8 %collective-permute-done.27 = bf16[96,576]{1,0:T(8,128)(2,1)S(1)} collective-permute-done((bf16[96,576]{1,0:T(8,128)(2,1)S(1)}, bf16[96,576]{1,0:T(8,128)(2,1)S(1)}, u32[]{:S(2)}, u32[]{:S(2)}) %collective-permute-start.27) | collective-permute-done | bytes 110624 | tf_op jit(solution)/shard_map/ppermute | solution.py:1234
  328.0 5.4 %collective-permute-done.31 = bf16[2,4,96,576]{3,2,1,0:T(8,128)(2,1)} collective-permute-done((bf16[2,4,96,576]{3,2,1,0:T(8,128)(2,1)}, bf16[2,4,96,576]{3,2,1,0:T(8,128)(2,1)}, u32[]{:S(2)}, u32[]{:S(2)}) %collective-permute-start.31) | collective-permute-done | bytes 884768 | tf_op jit(solution)/shard_map/ppermute | solution.py:1234
  334.8 1.9 fusion.9
  339.6 2.6 collective-permute-done.33
  342.2 1.5 collective-permute-start.20
  344.8 6.4 %collective-permute-done.34 = bf16[4,96,576]{2,1,0:T(8,128)(2,1)} collective-permute-done((bf16[4,96,576]{2,1,0:T(8,128)(2,1)}, bf16[4,96,576]{2,1,0:T(8,128)(2,1)}, u32[]{:S(2)}, u32[]{:S(2)}) %collective-permute-start.34) | collective-permute-done | bytes 442400 | tf_op jit(solution)/shard_map/ppermute | solution.py:1234
  351.2 1.4 fusion.2
  352.6 8.7 %collective-permute-done.32 = bf16[384,768]{1,0:T(8,128)(2,1)} collective-permute-done((bf16[384,768]{1,0:T(8,128)(2,1)S(1)}, bf16[384,768]{1,0:T(8,128)(2,1)}, u32[]{:S(2)}, u32[]{:S(2)}) %collective-permute-start.32) | collective-permute-done | bytes 589856 | tf_op jit(solution)/shard_map/ppermute | solution.py:1234
  362.5 1.5 collective-permute-done.20
  365.4 2.9 collective-permute-start.46
  368.5 1.9 collective-permute-start.39
  370.4 1.5 collective-permute-start.40
  371.9 7.6 %collective-permute-done.38 = bf16[96,384]{1,0:T(8,128)(2,1)S(1)} collective-permute-done((bf16[96,384]{1,0:T(8,128)(2,1)S(1)}, bf16[96,384]{1,0:T(8,128)(2,1)S(1)}, u32[]{:S(2)}, u32[]{:S(2)}) %collective-permute-start.38) | collective-permute-done | bytes 73760 | tf_op jit(solution)/shard_map/ppermute | solution.py:1234
  379.5 6.6 %collective-permute-done.39 = bf16[96,384]{1,0:T(8,128)(2,1)S(1)} collective-permute-done((bf16[96,384]{1,0:T(8,128)(2,1)S(1)}, bf16[96,384]{1,0:T(8,128)(2,1)S(1)}, u32[]{:S(2)}, u32[]{:S(2)}) %collective-permute-start.39) | collective-permute-done | bytes 73760 | tf_op jit(solution)/shard_map/ppermute | solution.py:1234
  386.1 3.9 collective-permute-start.42
  390.2 3.6 collective-permute-start.43
  394.0 4.3 collective-permute-done.42
  398.2 3.9 collective-permute-start.36
  402.1 2.5 collective-permute-done.43
  405.9 2.4 broadcast_in_dim.15
  408.3 2.2 collective-permute-done.44
  410.5 1.8 collective-permute-start.37
  415.2 23.8 %collective-permute-done.47 = f32[40,768]{1,0:T(8,128)S(1)} collective-permute-done((f32[40,768]{1,0:T(8,128)S(1)}, f32[40,768]{1,0:T(8,128)S(1)}, u32[]{:S(2)}, u32[]{:S(2)}) %collective-permute-start.47) | collective-permute-done | bytes 122912 | tf_op jit(solution)/shard_map/ppermute | solution.py:1234
  440.5 4.2 lay_rows.3
  (208 shorter events, 35.8 us)
Async XLA Ops:
  7.2 139.5 %all-gather.2.cloned.1.call-start = ((), (), s32[]{:S(2)}) async-start(), calls=%async_computation.1 | async-start | bytes 11280384 | tf_op jit(solution)/shard_map/all_gather | solution.py:1312
  10.3 21.4 %collective-permute-start = (bf16[208,768]{1,0:T(8,128)(2,1)S(1)}, bf16[208,768]{1,0:T(8,128)(2,1)S(1)}, u32[]{:S(2)}, u32[]{:S(2)}) collective-permute-start(bf16[208,768]{1,0:T(8,128)(2,1)S(1)} %pad_maximum_fusion.2), channel_id=1, source_target_pairs={{0,1},{1,0},{2,3},{3,2},{4,5},{5,4},{6,7},{7,6},{8,9},{9,8},{10,11... | collective-permute-start | bytes 958472 | tf_op jit(solution)/shard_map/ppermute | solution.py:1234
  10.4 24.7 %collective-permute-start.1 = (bf16[208,768]{1,0:T(8,128)(2,1)S(1)}, bf16[208,768]{1,0:T(8,128)(2,1)S(1)}, u32[]{:S(2)}, u32[]{:S(2)}) collective-permute-start(bf16[208,768]{1,0:T(8,128)(2,1)S(1)} %pad_maximum_fusion.2), channel_id=1, source_target_pairs={{0,2},{1,3},{2,0},{3,1},{4,6},{5,7},{6,4},{7,5},{8,10},{9,11},{10,... | collective-permute-start | bytes 958472 | tf_op jit(solution)/shard_map/ppermute | solution.py:1234
  13.4 28.0 %collective-permute-start.2 = (bf16[208,768]{1,0:T(8,128)(2,1)S(1)}, bf16[208,768]{1,0:T(8,128)(2,1)S(1)}, u32[]{:S(2)}, u32[]{:S(2)}) collective-permute-start(bf16[208,768]{1,0:T(8,128)(2,1)S(1)} %pad_maximum_fusion.2), channel_id=1, source_target_pairs={{0,3},{1,2},{2,1},{3,0},{4,7},{5,6},{6,5},{7,4},{8,11},{9,10},{10,... | collective-permute-start | bytes 958472 | tf_op jit(solution)/shard_map/ppermute | solution.py:1234
  41.6 36.2 %copy-start.2 = (bf16[4,208,768]{2,1,0:T(8,128)(2,1)}, bf16[4,208,768]{2,1,0:T(8,128)(2,1)S(1)}, u32[]{:S(2)}) copy-start(bf16[4,208,768]{2,1,0:T(8,128)(2,1)S(1)} %pad_maximum_fusion.1) | copy-start | bytes 3833860
  41.6 291.8 %reduce-scatter.2.cloned.1.call-start = ((), (), s32[]{:S(2)}) async-start(), calls=%async_computation.2 | async-start | bytes 10027008 | tf_op jit(solution)/shard_map/reduce_scatter | solution.py:1352
  41.6 36.1 %collective-permute-start.3 = (bf16[4,208,768]{2,1,0:T(8,128)(2,1)S(1)}, bf16[4,208,768]{2,1,0:T(8,128)(2,1)}, u32[]{:S(2)}, u32[]{:S(2)}) collective-permute-start(bf16[4,208,768]{2,1,0:T(8,128)(2,1)S(1)} %pad_maximum_fusion.1), channel_id=1, source_target_pairs={{0,16},{8,24},{16,0},{24,8},{1,17},{9,25},{17,1},{25,9},{2,18},{10... | collective-permute-start | bytes 3833864 | tf_op jit(solution)/shard_map/ppermute | solution.py:1234
  43.2 18.8 %collective-permute-start.4 = (bf16[1024,384]{1,0:T(8,128)(2,1)S(1)}, bf16[1024,384]{1,0:T(8,128)(2,1)S(1)}, u32[]{:S(2)}, u32[]{:S(2)}) collective-permute-start(bf16[1024,384]{1,0:T(8,128)(2,1)S(1)} %copy-done.3), channel_id=1, source_target_pairs={{0,4},{1,5},{2,6},{3,7},{8,12},{9,13},{10,14},{11,15},{16,20},{17,... | collective-permute-start | bytes 2359304 | tf_op jit(solution)/shard_map/ppermute | solution.py:1313
  79.8 19.2 %copy-start = (bf16[2,4,208,768]{3,2,1,0:T(8,128)(2,1)}, bf16[2,4,208,768]{3,2,1,0:T(8,128)(2,1)S(1)}, u32[]{:S(2)}) copy-start(bf16[2,4,208,768]{3,2,1,0:T(8,128)(2,1)S(1)} %pad_maximum_fusion.near_ref) | copy-start | bytes 7667716
  79.8 17.1 %copy-start.38 = (f32[768]{0:T(1024)S(1)}, f32[768]{0:T(1024)}, u32[]{:S(2)}) copy-start(f32[768]{0:T(1024)} %param.54) | copy-start | bytes 9220
  79.8 17.8 %copy-start.39 = (f32[768]{0:T(1024)S(1)}, f32[768]{0:T(1024)}, u32[]{:S(2)}) copy-start(f32[768]{0:T(1024)} %param.50) | copy-start | bytes 9220
  79.9 17.8 %copy-start.40 = (f32[768]{0:T(1024)S(1)}, f32[768]{0:T(1024)}, u32[]{:S(2)}) copy-start(f32[768]{0:T(1024)} %param.55) | copy-start | bytes 9220
  79.9 17.8 %copy-start.41 = (f32[768]{0:T(1024)S(1)}, f32[768]{0:T(1024)}, u32[]{:S(2)}) copy-start(f32[768]{0:T(1024)} %param.56) | copy-start | bytes 9220
  79.9 17.8 %copy-start.42 = (f32[768]{0:T(1024)S(1)}, f32[768]{0:T(1024)}, u32[]{:S(2)}) copy-start(f32[768]{0:T(1024)} %param.52) | copy-start | bytes 9220
  79.9 17.8 %copy-start.43 = (f32[768]{0:T(1024)S(1)}, f32[768]{0:T(1024)}, u32[]{:S(2)}) copy-start(f32[768]{0:T(1024)} %param.57) | copy-start | bytes 9220
  79.9 17.8 %copy-start.44 = (f32[768]{0:T(1024)S(1)}, f32[768]{0:T(1024)}, u32[]{:S(2)}) copy-start(f32[768]{0:T(1024)} %param.58) | copy-start | bytes 9220
  79.9 19.1 %collective-permute-start.5 = (bf16[2,4,208,768]{3,2,1,0:T(8,128)(2,1)S(1)}, bf16[2,4,208,768]{3,2,1,0:T(8,128)(2,1)}, u32[]{:S(2)}, u32[]{:S(2)}) collective-permute-start(bf16[2,4,208,768]{3,2,1,0:T(8,128)(2,1)S(1)} %pad_maximum_fusion.near_ref), channel_id=1, source_target_pairs={{0,8},{8,0},{16,24},{24,16},{1,9},{9,1},{17,25},{25,17},{2,10},{10... | collective-permute-start | bytes 7667720 | tf_op jit(solution)/shard_map/ppermute | solution.py:1234
  81.0 30.8 %collective-permute-start.9 = (bf16[512,768]{1,0:T(8,128)(2,1)}, bf16[512,768]{1,0:T(8,128)(2,1)S(1)}, u32[]{:S(2)}, u32[]{:S(2)}) collective-permute-start(bf16[512,768]{1,0:T(8,128)(2,1)} %convert_bitcast_fusion), channel_id=1, source_target_pairs={{0,4},{4,0},{1,5},{5,1},{2,6},{6,2},{3,7},{7,3},{8,12},{12,8},{9,1... | collective-permute-start | bytes 2359304 | tf_op jit(solution)/shard_map/ppermute | solution.py:1234
  93.4 26.7 %collective-permute-start.6 = (bf16[256,192]{1,0:T(8,128)(2,1)S(1)}, bf16[256,192]{1,0:T(8,128)(2,1)}, u32[]{:S(2)}, u32[]{:S(2)}) collective-permute-start(bf16[256,192]{1,0:T(8,128)(2,1)S(1)} %copy-done.25), channel_id=1, source_target_pairs={{0,1},{1,0},{2,3},{3,2},{4,5},{5,4},{6,7},{7,6},{8,9},{9,8},{10,11... | collective-permute-start | bytes 294920 | tf_op jit(solution)/shard_map/ppermute | solution.py:1234
  93.4 26.7 %collective-permute-start.7 = (bf16[256,192]{1,0:T(8,128)(2,1)}, bf16[256,192]{1,0:T(8,128)(2,1)}, u32[]{:S(2)}, u32[]{:S(2)}) collective-permute-start(bf16[256,192]{1,0:T(8,128)(2,1)} %get-tuple-element.143.rest_6_), channel_id=1, source_target_pairs={{0,2},{1,3},{2,0},{3,1},{4,6},{5,7},{6,4},{7,5},{8,10},{9,11},{10,... | collective-permute-start | bytes 294920 | tf_op jit(solution)/shard_map/ppermute | solution.py:1234
  96.3 27.4 %collective-permute-start.8 = (bf16[256,192]{1,0:T(8,128)(2,1)}, bf16[256,192]{1,0:T(8,128)(2,1)}, u32[]{:S(2)}, u32[]{:S(2)}) collective-permute-start(bf16[256,192]{1,0:T(8,128)(2,1)} %get-tuple-element.144.rest_7_), channel_id=1, source_target_pairs={{0,3},{1,2},{2,1},{3,0},{4,7},{5,6},{6,5},{7,4},{8,11},{9,10},{10,... | collective-permute-start | bytes 294920 | tf_op jit(solution)/shard_map/ppermute | solution.py:1234
  169.3 236.6 %all-reduce.4.cloned.1.call-start = ((), (), s32[]{:S(2)}) async-start(), calls=%async_computation.3 | async-start | bytes 1572864 | tf_op jit(solution)/shard_map/psum | solution.py:1418
  170.2 29.5 %collective-permute-start.10 = (bf16[256,768]{1,0:T(8,128)(2,1)S(1)}, bf16[256,768]{1,0:T(8,128)(2,1)S(1)}, u32[]{:S(2)}, u32[]{:S(2)}) collective-permute-start(bf16[256,768]{1,0:T(8,128)(2,1)S(1)} %copy-done.14), channel_id=1, source_target_pairs={{0,1},{1,0},{2,3},{3,2},{4,5},{5,4},{6,7},{7,6},{8,9},{9,8},{10,11... | collective-permute-start | bytes 1179656 | tf_op jit(solution)/shard_map/ppermute | solution.py:1234
  170.2 29.5 %collective-permute-start.11 = (bf16[256,768]{1,0:T(8,128)(2,1)S(1)}, bf16[256,768]{1,0:T(8,128)(2,1)S(1)}, u32[]{:S(2)}, u32[]{:S(2)}) collective-permute-start(bf16[256,768]{1,0:T(8,128)(2,1)S(1)} %copy-done.14), channel_id=1, source_target_pairs={{0,2},{1,3},{2,0},{3,1},{4,6},{5,7},{6,4},{7,5},{8,10},{9,11},{10,... | collective-permute-start | bytes 1179656 | tf_op jit(solution)/shard_map/ppermute | solution.py:1234
  196.3 10.7 %collective-permute-start.12 = (bf16[256,192]{1,0:T(8,128)(2,1)}, bf16[256,192]{1,0:T(8,128)(2,1)S(1)}, u32[]{:S(2)}, u32[]{:S(2)}) collective-permute-start(bf16[256,192]{1,0:T(8,128)(2,1)} %get-tuple-element.167), channel_id=1, source_target_pairs={{0,1},{1,0},{2,3},{3,2},{4,5},{5,4},{6,7},{7,6},{8,9},{9,8},{10,11... | collective-permute-start | bytes 294920 | tf_op jit(solution)/shard_map/ppermute | solution.py:1234
  196.3 13.6 %collective-permute-start.13 = (bf16[256,192]{1,0:T(8,128)(2,1)}, bf16[256,192]{1,0:T(8,128)(2,1)S(1)}, u32[]{:S(2)}, u32[]{:S(2)}) collective-permute-start(bf16[256,192]{1,0:T(8,128)(2,1)} %get-tuple-element.168), channel_id=1, source_target_pairs={{0,2},{1,3},{2,0},{3,1},{4,6},{5,7},{6,4},{7,5},{8,10},{9,11},{10,... | collective-permute-start | bytes 294920 | tf_op jit(solution)/shard_map/ppermute | solution.py:1234
  198.0 28.3 %collective-permute-start.14 = (bf16[256,192]{1,0:T(8,128)(2,1)}, bf16[256,192]{1,0:T(8,128)(2,1)S(1)}, u32[]{:S(2)}, u32[]{:S(2)}) collective-permute-start(bf16[256,192]{1,0:T(8,128)(2,1)} %get-tuple-element.169), channel_id=1, source_target_pairs={{0,3},{1,2},{2,1},{3,0},{4,7},{5,6},{6,5},{7,4},{8,11},{9,10},{10,... | collective-permute-start | bytes 294920 | tf_op jit(solution)/shard_map/ppermute | solution.py:1234
  207.0 27.9 %copy-start.26 = (bf16[256,192]{1,0:T(8,128)(2,1)}, bf16[256,192]{1,0:T(8,128)(2,1)S(1)}, u32[]{:S(2)}) copy-start(bf16[256,192]{1,0:T(8,128)(2,1)S(1)} %collective-permute-done.12.rest_1_) | copy-start | bytes 294916
  209.9 25.1 %copy-start.27 = (bf16[256,192]{1,0:T(8,128)(2,1)}, bf16[256,192]{1,0:T(8,128)(2,1)S(1)}, u32[]{:S(2)}) copy-start(bf16[256,192]{1,0:T(8,128)(2,1)S(1)} %collective-permute-done.13.rest_2_) | copy-start | bytes 294916
  226.3 35.2 %copy-start.7 = (f32[512,768]{1,0:T(8,128)S(1)}, f32[512,768]{1,0:T(8,128)}, u32[]{:S(2)}) copy-start(f32[512,768]{1,0:T(8,128)} %get-tuple-element.182) | copy-start | bytes 4718596
  226.3 35.2 %collective-permute-start.15 = (bf16[512,768]{1,0:T(8,128)(2,1)}, bf16[512,768]{1,0:T(8,128)(2,1)S(1)}, u32[]{:S(2)}, u32[]{:S(2)}) collective-permute-start(bf16[512,768]{1,0:T(8,128)(2,1)} %get-tuple-element.170), channel_id=1, source_target_pairs={{0,4},{4,0},{1,5},{5,1},{2,6},{6,2},{3,7},{7,3},{8,12},{12,8},{9,1... | collective-permute-start | bytes 2359304 | tf_op jit(solution)/shard_map/ppermute | solution.py:1234
  234.9 26.6 %collective-permute-start.16 = (bf16[256,768]{1,0:T(8,128)(2,1)S(1)}, bf16[256,768]{1,0:T(8,128)(2,1)S(1)}, u32[]{:S(2)}, u32[]{:S(2)}) collective-permute-start(bf16[256,768]{1,0:T(8,128)(2,1)S(1)} %copy-done.14), channel_id=1, source_target_pairs={{0,3},{1,2},{2,1},{3,0},{4,7},{5,6},{6,5},{7,4},{8,11},{9,10},{10,... | collective-permute-start | bytes 1179656 | tf_op jit(solution)/shard_map/ppermute | solution.py:1234
  251.0 25.4 %collective-permute-start.17 = (bf16[1024,384]{1,0:T(8,128)(2,1)}, bf16[1024,384]{1,0:T(8,128)(2,1)S(1)}, u32[]{:S(2)}, u32[]{:S(2)}) collective-permute-start(bf16[1024,384]{1,0:T(8,128)(2,1)} %get-tuple-element.176.dtrunk_ref), channel_id=1, source_target_pairs={{4,0},{5,1},{6,2},{7,3},{12,8},{13,9},{14,10},{15,11},{20,16},{21,... | collective-permute-start | bytes 2359304 | tf_op jit(solution)/shard_map/ppermute | solution.py:1374
  275.9 32.5 %collective-permute-start.29 = (bf16[2,2,4,96,576]{4,3,2,1,0:T(8,128)(2,1)}, bf16[2,2,4,96,576]{4,3,2,1,0:T(8,128)(2,1)S(1)}, u32[]{:S(2)}, u32[]{:S(2)}) collective-permute-start(bf16[2,2,4,96,576]{4,3,2,1,0:T(8,128)(2,1)} %get-tuple-element.197), channel_id=1, source_target_pairs={{0,8},{8,0},{16,24},{24,16},{1,9},{9,1},{17,25},{25,17},{2,10},{10... | collective-permute-start | bytes 5308424 | tf_op jit(solution)/shard_map/ppermute | solution.py:1234
  275.9 32.4 %collective-permute-start.28 = (bf16[2,2,4,96,384]{4,3,2,1,0:T(8,128)(2,1)}, bf16[2,2,4,96,384]{4,3,2,1,0:T(8,128)(2,1)S(1)}, u32[]{:S(2)}, u32[]{:S(2)}) collective-permute-start(bf16[2,2,4,96,384]{4,3,2,1,0:T(8,128)(2,1)} %get-tuple-element.196), channel_id=1, source_target_pairs={{0,8},{8,0},{16,24},{24,16},{1,9},{9,1},{17,25},{25,17},{2,10},{10... | collective-permute-start | bytes 3538952 | tf_op jit(solution)/shard_map/ppermute | solution.py:1234
  286.0 2.1 collective-permute-start.24
  286.1 3.2 collective-permute-start.21
  289.2 18.4 %collective-permute-start.25 = (bf16[2,96,576]{2,1,0:T(8,128)(2,1)S(1)}, bf16[2,96,576]{2,1,0:T(8,128)(2,1)S(1)}, u32[]{:S(2)}, u32[]{:S(2)}) collective-permute-start(bf16[2,96,576]{2,1,0:T(8,128)(2,1)S(1)} %get-tuple-element.271), channel_id=1, source_target_pairs={{0,16},{8,24},{16,0},{24,8},{1,17},{9,25},{17,1},{25,9},{2,18},{10... | collective-permute-start | bytes 663560 | tf_op jit(solution)/shard_map/ppermute | solution.py:1234
  289.4 12.4 %collective-permute-start.22 = (f32[40,768]{1,0:T(8,128)S(1)}, f32[40,768]{1,0:T(8,128)S(1)}, u32[]{:S(2)}, u32[]{:S(2)}) collective-permute-start(f32[40,768]{1,0:T(8,128)S(1)} %add.146), channel_id=1, source_target_pairs={{0,16},{8,24},{16,0},{24,8},{1,17},{9,25},{17,1},{25,9},{2,18},{10... | collective-permute-start | bytes 368648 | tf_op jit(solution)/shard_map/ppermute | solution.py:1234
  301.8 11.6 %collective-permute-start.23 = (f32[40,768]{1,0:T(8,128)S(1)}, f32[40,768]{1,0:T(8,128)}, u32[]{:S(2)}, u32[]{:S(2)}) collective-permute-start(f32[40,768]{1,0:T(8,128)S(1)} %add.147), channel_id=1, source_target_pairs={{0,4},{4,0},{1,5},{5,1},{2,6},{6,2},{3,7},{7,3},{8,12},{12,8},{9,1... | collective-permute-start | bytes 368648 | tf_op jit(solution)/shard_map/ppermute | solution.py:1234
  307.7 5.0 %collective-permute-start.26 = (bf16[96,576]{1,0:T(8,128)(2,1)S(1)}, bf16[96,576]{1,0:T(8,128)(2,1)S(1)}, u32[]{:S(2)}, u32[]{:S(2)}) collective-permute-start(bf16[96,576]{1,0:T(8,128)(2,1)S(1)} %fusion.23), channel_id=1, source_target_pairs={{0,4},{4,0},{1,5},{5,1},{2,6},{6,2},{3,7},{7,3},{8,12},{12,8},{9,1... | collective-permute-start | bytes 331784 | tf_op jit(solution)/shard_map/ppermute | solution.py:1234
  309.8 23.6 %collective-permute-start.31 = (bf16[2,4,96,576]{3,2,1,0:T(8,128)(2,1)}, bf16[2,4,96,576]{3,2,1,0:T(8,128)(2,1)}, u32[]{:S(2)}, u32[]{:S(2)}) collective-permute-start(bf16[2,4,96,576]{3,2,1,0:T(8,128)(2,1)} %get-tuple-element.265), channel_id=1, source_target_pairs={{0,16},{8,24},{16,0},{24,8},{1,17},{9,25},{17,1},{25,9},{2,18},{10... | collective-permute-start | bytes 2654216 | tf_op jit(solution)/shard_map/ppermute | solution.py:1234
  310.6 17.4 %collective-permute-start.30 = (bf16[2,4,96,384]{3,2,1,0:T(8,128)(2,1)S(1)}, bf16[2,4,96,384]{3,2,1,0:T(8,128)(2,1)S(1)}, u32[]{:S(2)}, u32[]{:S(2)}) collective-permute-start(bf16[2,4,96,384]{3,2,1,0:T(8,128)(2,1)S(1)} %get-tuple-element.267), channel_id=1, source_target_pairs={{0,4},{4,0},{1,5},{5,1},{2,6},{6,2},{3,7},{7,3},{8,12},{12,8},{9,1... | collective-permute-start | bytes 1769480 | tf_op jit(solution)/shard_map/ppermute | solution.py:1234
  312.7 15.2 %collective-permute-start.27 = (bf16[96,576]{1,0:T(8,128)(2,1)S(1)}, bf16[96,576]{1,0:T(8,128)(2,1)S(1)}, u32[]{:S(2)}, u32[]{:S(2)}) collective-permute-start(bf16[96,576]{1,0:T(8,128)(2,1)S(1)} %fusion.17), channel_id=1, source_target_pairs={{0,4},{4,0},{1,5},{5,1},{2,6},{6,2},{3,7},{7,3},{8,12},{12,8},{9,1... | collective-permute-start | bytes 331784 | tf_op jit(solution)/shard_map/ppermute | solution.py:1234
  313.3 49.1 %collective-permute-start.18 = (bf16[256,768]{1,0:T(8,128)(2,1)}, bf16[256,768]{1,0:T(8,128)(2,1)}, u32[]{:S(2)}, u32[]{:S(2)}) collective-permute-start(bf16[256,768]{1,0:T(8,128)(2,1)} %get-tuple-element.201), channel_id=1, source_target_pairs={{0,1},{1,0},{2,3},{3,2},{4,5},{5,4},{6,7},{7,6},{8,9},{9,8},{10,11... | collective-permute-start | bytes 1179656 | tf_op jit(solution)/shard_map/ppermute | solution.py:1234
  313.3 49.1 %collective-permute-start.19 = (bf16[256,768]{1,0:T(8,128)(2,1)}, bf16[256,768]{1,0:T(8,128)(2,1)}, u32[]{:S(2)}, u32[]{:S(2)}) collective-permute-start(bf16[256,768]{1,0:T(8,128)(2,1)} %get-tuple-element.202), channel_id=1, source_target_pairs={{0,2},{1,3},{2,0},{3,1},{4,6},{5,7},{6,4},{7,5},{8,10},{9,11},{10,... | collective-permute-start | bytes 1179656 | tf_op jit(solution)/shard_map/ppermute | solution.py:1234
  334.2 8.0 %collective-permute-start.33 = (bf16[4,96,384]{2,1,0:T(8,128)(2,1)}, bf16[4,96,384]{2,1,0:T(8,128)(2,1)}, u32[]{:S(2)}, u32[]{:S(2)}) collective-permute-start(bf16[4,96,384]{2,1,0:T(8,128)(2,1)} %fusion.11), channel_id=1, source_target_pairs={{0,16},{8,24},{16,0},{24,8},{1,17},{9,25},{17,1},{25,9},{2,18},{10... | collective-permute-start | bytes 884744 | tf_op jit(solution)/shard_map/ppermute | solution.py:1234
  336.7 14.5 %collective-permute-start.34 = (bf16[4,96,576]{2,1,0:T(8,128)(2,1)}, bf16[4,96,576]{2,1,0:T(8,128)(2,1)}, u32[]{:S(2)}, u32[]{:S(2)}) collective-permute-start(bf16[4,96,576]{2,1,0:T(8,128)(2,1)} %fusion.9), channel_id=1, source_target_pairs={{0,4},{4,0},{1,5},{5,1},{2,6},{6,2},{3,7},{7,3},{8,12},{12,8},{9,1... | collective-permute-start | bytes 1327112 | tf_op jit(solution)/shard_map/ppermute | solution.py:1234
  337.9 23.4 %collective-permute-start.32 = (bf16[384,768]{1,0:T(8,128)(2,1)S(1)}, bf16[384,768]{1,0:T(8,128)(2,1)}, u32[]{:S(2)}, u32[]{:S(2)}) collective-permute-start(bf16[384,768]{1,0:T(8,128)(2,1)S(1)} %copy-done.13), channel_id=1, source_target_pairs={{0,4},{4,0},{1,5},{5,1},{2,6},{6,2},{3,7},{7,3},{8,12},{12,8},{9,1... | collective-permute-start | bytes 1769480 | tf_op jit(solution)/shard_map/ppermute | solution.py:1234
  342.2 21.7 %collective-permute-start.20 = (bf16[256,768]{1,0:T(8,128)(2,1)}, bf16[256,768]{1,0:T(8,128)(2,1)S(1)}, u32[]{:S(2)}, u32[]{:S(2)}) collective-permute-start(bf16[256,768]{1,0:T(8,128)(2,1)} %get-tuple-element.203), channel_id=1, source_target_pairs={{0,3},{1,2},{2,1},{3,0},{4,7},{5,6},{6,5},{7,4},{8,11},{9,10},{10,... | collective-permute-start | bytes 1179656 | tf_op jit(solution)/shard_map/ppermute | solution.py:1234
  365.3 45.2 %copy-start.6 = (bf16[256,768]{1,0:T(8,128)(2,1)}, bf16[256,768]{1,0:T(8,128)(2,1)S(1)}, u32[]{:S(2)}) copy-start(bf16[256,768]{1,0:T(8,128)(2,1)S(1)} %add_convert_fusion.5.refs_0_) | copy-start | bytes 1179652
  365.3 47.2 %collective-permute-start.45 = (f32[40,768]{1,0:T(8,128)S(1)}, f32[40,768]{1,0:T(8,128)S(1)}, u32[]{:S(2)}, u32[]{:S(2)}) collective-permute-start(f32[40,768]{1,0:T(8,128)S(1)} %add.148), channel_id=1, source_target_pairs={{0,1},{1,0},{2,3},{3,2},{4,5},{5,4},{6,7},{7,6},{8,9},{9,8},{10,11... | collective-permute-start | bytes 368648 | tf_op jit(solution)/shard_map/ppermute | solution.py:1234
  365.4 49.9 %collective-permute-start.46 = (f32[40,768]{1,0:T(8,128)S(1)}, f32[40,768]{1,0:T(8,128)S(1)}, u32[]{:S(2)}, u32[]{:S(2)}) collective-permute-start(f32[40,768]{1,0:T(8,128)S(1)} %add.148), channel_id=1, source_target_pairs={{0,2},{1,3},{2,0},{3,1},{4,6},{5,7},{6,4},{7,5},{8,10},{9,11},{10,... | collective-permute-start | bytes 368648 | tf_op jit(solution)/shard_map/ppermute | solution.py:1234
  368.3 11.2 %collective-permute-start.38 = (bf16[96,384]{1,0:T(8,128)(2,1)S(1)}, bf16[96,384]{1,0:T(8,128)(2,1)S(1)}, u32[]{:S(2)}, u32[]{:S(2)}) collective-permute-start(bf16[96,384]{1,0:T(8,128)(2,1)S(1)} %get-tuple-element.285), channel_id=1, source_target_pairs={{0,1},{1,0},{2,3},{3,2},{4,5},{5,4},{6,7},{7,6},{8,9},{9,8},{10,11... | collective-permute-start | bytes 221192 | tf_op jit(solution)/shard_map/ppermute | solution.py:1234
  368.5 17.7 %collective-permute-start.39 = (bf16[96,384]{1,0:T(8,128)(2,1)S(1)}, bf16[96,384]{1,0:T(8,128)(2,1)S(1)}, u32[]{:S(2)}, u32[]{:S(2)}) collective-permute-start(bf16[96,384]{1,0:T(8,128)(2,1)S(1)} %get-tuple-element.287), channel_id=1, source_target_pairs={{0,2},{1,3},{2,0},{3,1},{4,6},{5,7},{6,4},{7,5},{8,10},{9,11},{10,... | collective-permute-start | bytes 221192 | tf_op jit(solution)/shard_map/ppermute | solution.py:1234
  370.4 19.8 %collective-permute-start.40 = (bf16[96,384]{1,0:T(8,128)(2,1)S(1)}, bf16[96,384]{1,0:T(8,128)(2,1)S(1)}, u32[]{:S(2)}, u32[]{:S(2)}) collective-permute-start(bf16[96,384]{1,0:T(8,128)(2,1)S(1)} %get-tuple-element.286), channel_id=1, source_target_pairs={{0,3},{1,2},{2,1},{3,0},{4,7},{5,6},{6,5},{7,4},{8,11},{9,10},{10,... | collective-permute-start | bytes 221192 | tf_op jit(solution)/shard_map/ppermute | solution.py:1234
  379.5 14.3 %collective-permute-start.41 = (bf16[96,576]{1,0:T(8,128)(2,1)S(1)}, bf16[96,576]{1,0:T(8,128)(2,1)S(1)}, u32[]{:S(2)}, u32[]{:S(2)}) collective-permute-start(bf16[96,576]{1,0:T(8,128)(2,1)S(1)} %get-tuple-element.277), channel_id=1, source_target_pairs={{0,1},{1,0},{2,3},{3,2},{4,5},{5,4},{6,7},{7,6},{8,9},{9,8},{10,11... | collective-permute-start | bytes 331784 | tf_op jit(solution)/shard_map/ppermute | solution.py:1234
  386.1 12.1 %collective-permute-start.42 = (bf16[96,576]{1,0:T(8,128)(2,1)S(1)}, bf16[96,576]{1,0:T(8,128)(2,1)S(1)}, u32[]{:S(2)}, u32[]{:S(2)}) collective-permute-start(bf16[96,576]{1,0:T(8,128)(2,1)S(1)} %get-tuple-element.279), channel_id=1, source_target_pairs={{0,2},{1,3},{2,0},{3,1},{4,6},{5,7},{6,4},{7,5},{8,10},{9,11},{10,... | collective-permute-start | bytes 331784 | tf_op jit(solution)/shard_map/ppermute | solution.py:1234
  390.2 14.4 %collective-permute-start.43 = (bf16[96,576]{1,0:T(8,128)(2,1)S(1)}, bf16[96,576]{1,0:T(8,128)(2,1)S(1)}, u32[]{:S(2)}, u32[]{:S(2)}) collective-permute-start(bf16[96,576]{1,0:T(8,128)(2,1)S(1)} %get-tuple-element.278), channel_id=1, source_target_pairs={{0,3},{1,2},{2,1},{3,0},{4,7},{5,6},{6,5},{7,4},{8,11},{9,10},{10,... | collective-permute-start | bytes 331784 | tf_op jit(solution)/shard_map/ppermute | solution.py:1234
  393.9 45.1 %collective-permute-start.35 = (bf16[256,768]{1,0:T(8,128)(2,1)S(1)}, bf16[256,768]{1,0:T(8,128)(2,1)S(1)}, u32[]{:S(2)}, u32[]{:S(2)}) collective-permute-start(bf16[256,768]{1,0:T(8,128)(2,1)S(1)} %add_convert_fusion.5.refs_0_), channel_id=1, source_target_pairs={{0,1},{1,0},{2,3},{3,2},{4,5},{5,4},{6,7},{7,6},{8,9},{9,8},{10,11... | collective-permute-start | bytes 1179656 | tf_op jit(solution)/shard_map/ppermute | solution.py:1234
  398.2 40.8 %collective-permute-start.36 = (bf16[256,768]{1,0:T(8,128)(2,1)S(1)}, bf16[256,768]{1,0:T(8,128)(2,1)S(1)}, u32[]{:S(2)}, u32[]{:S(2)}) collective-permute-start(bf16[256,768]{1,0:T(8,128)(2,1)S(1)} %add_convert_fusion.5.refs_0_), channel_id=1, source_target_pairs={{0,2},{1,3},{2,0},{3,1},{4,6},{5,7},{6,4},{7,5},{8,10},{9,11},{10,... | collective-permute-start | bytes 1179656 | tf_op jit(solution)/shard_map/ppermute | solution.py:1234
  404.7 5.7 %collective-permute-start.44 = (bf16[96,960]{1,0:T(8,128)(2,1)S(1)}, bf16[96,960]{1,0:T(8,128)(2,1)S(1)}, u32[]{:S(2)}, u32[]{:S(2)}) collective-permute-start(bf16[96,960]{1,0:T(8,128)(2,1)S(1)} %pad_maximum_fusion.4), channel_id=1, source_target_pairs={{0,4},{4,0},{1,5},{5,1},{2,6},{6,2},{3,7},{7,3},{8,12},{12,8},{9,1... | collective-permute-start | bytes 552968 | tf_op jit(solution)/shard_map/ppermute | solution.py:1234
  410.5 28.6 %collective-permute-start.37 = (bf16[256,768]{1,0:T(8,128)(2,1)S(1)}, bf16[256,768]{1,0:T(8,128)(2,1)S(1)}, u32[]{:S(2)}, u32[]{:S(2)}) collective-permute-start(bf16[256,768]{1,0:T(8,128)(2,1)S(1)} %add_convert_fusion.5.refs_0_), channel_id=1, source_target_pairs={{0,3},{1,2},{2,1},{3,0},{4,7},{5,6},{6,5},{7,4},{8,11},{9,10},{10,... | collective-permute-start | bytes 1179656 | tf_op jit(solution)/shard_map/ppermute | solution.py:1234
  412.5 26.6 %collective-permute-start.47 = (f32[40,768]{1,0:T(8,128)S(1)}, f32[40,768]{1,0:T(8,128)S(1)}, u32[]{:S(2)}, u32[]{:S(2)}) collective-permute-start(f32[40,768]{1,0:T(8,128)S(1)} %add.148), channel_id=1, source_target_pairs={{0,3},{1,2},{2,1},{3,0},{4,7},{5,6},{6,5},{7,4},{8,11},{9,10},{10,... | collective-permute-start | bytes 368648 | tf_op jit(solution)/shard_map/ppermute | solution.py:1234
  (32 other events, 203.5 us)
Sparse Core Ops, SparseCore 0:
  41.7 96.9 all-gather.1
  169.4 138.4 reduce-scatter.1
  339.7 57.7 all-reduce.3

commit v3 on v2

--- a/solution.py
+++ b/solution.py
@@ -785,7 +785,8 @@
     goal_ref,
     w_ref,
     result_ref,
-    dw_ref,
+    near_ref,
+    far_ref,
     grad_ref,
     grad_low_ref,
     grad_mix_ref,
@@ -863,13 +864,29 @@
         sums_ref[pl.ds(8 + z, 1), :hidden_units] = jnp.sum(grad_pre, axis=0, keepdims=True)
         pre_low = grad_pre.astype(BF16)
         acc_ref[...] += nt(pre_low, up)
-        shards = dw_ref.shape[1]
-        dw_ref[0, :, 0] = (
-            nn(low_t_ref[...], pre_low).astype(BF16).reshape(shards, piece, hidden_units)
+        products = (
+            nn(low_t_ref[...], pre_low).astype(BF16),
+            nn(three_t_ref[...], act_ref[z]).astype(BF16),
         )
-        dw_ref[0, :, 1] = (
-            nn(three_t_ref[...], act_ref[z]).astype(BF16).reshape(shards, piece, hidden_units)
-        )
+        _, _, ctxs, _, share, _ = near_ref.shape
+
+        def put(core):
+            for mat, product in enumerate(products):
+                for s in range(w_ref.shape[1]):
+                    ref = near_ref if (s & 1) == core else far_ref
+                    for c in range(ctxs):
+                        start = s * piece + c * share
+                        ref[mat, (s >> 1) ^ (info_ref[0] >> 1), c ^ info_ref[1], 0] = product[
+                            start : start + share
+                        ]
+
+        @pl.when((info_ref[0] & 1) == 0)
+        def _():
+            put(0)
+
+        @pl.when((info_ref[0] & 1) != 0)
+        def _():
+            put(1)
 
     @pl.when((phase == 1) & (z == tensors - 1))
     def _():
@@ -886,12 +903,15 @@
             grad_mix_ref[:, j * columns : (j + 1) * columns] = part
 
 
-def feed(info, sum_one, vectors, mix, columns, chunk, bias, goal, w):
+def feed(info, sum_one, vectors, mix, columns, chunk, bias, goal, w, ctxs):
     rows, width = sum_one.shape
     tensors, shards, taller, hidden_units = w.shape
     piece = width // shards
     assert hidden_units == width
-    grads = (tensors, shards, 2, piece, hidden_units)
+    grads = (2, shards // 2, ctxs, tensors, piece // ctxs, hidden_units)
+    grads_spec = pl.BlockSpec(
+        grads[:3] + (1,) + grads[4:], lambda p, z, i: (0, 0, 0, (p * z) ^ i[2], 0, 0)
+    )
     head = (sum_one, vectors, mix)
     last = 2 * piece // chunk
     return pl.pallas_call(
@@ -910,7 +930,8 @@
             ],
             out_specs=[
                 whole((rows, width)),
-                pl.BlockSpec((1,) + grads[1:], lambda p, z, i: (p * z, 0, 0, 0, 0)),
+                grads_spec,
+                grads_spec,
                 whole((rows, width)),
                 whole((rows, width)),
                 whole((rows, width)),
@@ -930,6 +951,7 @@
         ),
         out_shape=[
             shape_of((rows, width), BF16),
+            shape_of(grads, BF16),
             shape_of(grads, BF16),
             shape_of((rows, width), F32),
             shape_of((rows, width), BF16),
@@ -1230,6 +1252,9 @@
     seg = token_segment.shape[1] // parent_ids.shape[1]
     assert local_rows == tensors * TILE and ctxs == 2
 
+    def bits_of(axis):
+        return [1 << k for k in range(sizes[axis].bit_length() - 1)]
+
     def swap(a, axis, bit):
         return lax.ppermute(a, axis, [(i, i ^ bit) for i in range(sizes[axis])])
 
@@ -1338,7 +1363,7 @@
     cross_scalars = (info, enc_length)
     cross_mix, cross_logs = cross_forward(cross_scalars, cq, ckv)
 
-    result, ffn_grads, grad_two, two_grad_low, grad_cmix, feed_sums = feed(
+    result, ffn_near, ffn_far, grad_two, two_grad_low, grad_cmix, feed_sums = feed(
         info,
         sum_one,
         vectors,
@@ -1348,36 +1373,55 @@
         bias,
         out_grad,
         ffn_all.reshape(tensors, shards, -1, width),
-    )
-    ffn_grads = lax.psum_scatter(
-        ffn_grads.reshape(-1, ffn_grads.shape[-1]),
-        ("tensor", "shard"),
-        scatter_dimension=0,
-        tiled=True,
-    )
-    result_parts = [result] + [swap(result, "tensor", j) for j in range(1, tensors - 1)]
+        ctxs,
+    )
+    ffn_came = swap(ffn_far, "shard", 1)
+    result_all = lax.all_gather(result, "tensor", axis=0, tiled=True)
+
+    class Path:
+        def __init__(self, near, came, order):
+            lead = (2,) * len(shard_bits) + near.shape[1:]
+            self.dims = list(reversed(shard_bits)) + [("ctx", 1)]
+            self.order = list(order)
+            self.keep, self.came = near.reshape(lead), came.reshape(lead)
+
+        def fold(self):
+            near, came = self.keep, self.came
+            if not self.order:
+                self.keep = add(near, came)
+                return
+            dim = self.dims.index(self.order[0])
+            self.dims.pop(dim)
+            index = (slice(None),) * dim
+            self.send = add(near[index + (1,)], came[index + (1,)])
+            self.keep = add(near[index + (0,)], came[index + (0,)])
+
+        def go(self):
+            axis, bit = self.order.pop(0)
+            self.came = swap(self.send, axis, bit)
+
+    high = list(reversed(shard_bits))
+    orders = [[("ctx", 1)] + high, high + [("ctx", 1)]]
 
     dcq, dck, dcv = cross_backward(cross_scalars, cq, ckv, grad_cmix, cross_mix, cross_logs, scale)
+    ffn_came = tie(ffn_came, dcq)
+    ffn_paths = [Path(ffn_near[i], ffn_came[i], order) for i, order in enumerate(orders)]
+    for p in ffn_paths:
+        p.fold()
+        grad_two = tie(grad_two, p.send, p.keep)
+        p.go()
     grad_one, one_grad_low, self_sums, *grad_mixes = before_self(
         info, grad_two, dcq, weight_cq, sum_one, vectors[1:2], dcv, weight_o
     )
     head_grads = grad_mixes[:1] + [swap(grad_mixes[j], "tensor", j) for j in range(1, tensors)]
     mesh_sizes = (shards, ctxs, tensors)
-    result_parts = result_parts[:1] + list(tie(result_parts[1:], one_grad_low))
-    enc_keep, enc_send = encoder_grad(tie(dck, result_parts[1:]), dcv, weight_ckv)
-    enc_send, head_grads = tie((enc_send, head_grads), enc_send)
-    result_parts.append(swap(tie(result, head_grads), "tensor", tensors - 1))
-
-    dq, down, dtrunk, late_sums = self_backward(
-        scalars, q, kv, kv_sent, head_grads, mixes, self_logs, heads, seg, scale, width
-    )
-    trunk_came = lax.ppermute(dtrunk, "ctx", [(1, 0)])
-    enc_came, result_parts = tie((swap(enc_send, "ctx", 1), result_parts), dtrunk)
-    enc_mine = (enc_keep + enc_came.astype(F32)).astype(BF16)
+    enc_keep, enc_send = encoder_grad(tie(dck, one_grad_low), dcv, weight_ckv)
+    early_sums = jnp.concatenate([feed_sums, self_sums], axis=0)
+    early_sums = early_sums + swap(early_sums, "tensor", 1)
     near_a, near_b, far_a, far_b = square_grads(
         info,
         [
-            (tie(enc_low, enc_mine), dck),
+            (tie(enc_low, enc_send, early_sums), dck),
             (enc_low, dcv),
             (one_grad_low, self_mix),
             (one_low, dcq),
@@ -1386,69 +1430,106 @@
         (2, 3),
         mesh_sizes,
     )
-    result_all = lay_rows(info, tie(result_parts, near_a))
-
-    def path(near, far, order):
-        lead = (2,) * len(shard_bits) + near.shape[1:]
-        dims = list(reversed(shard_bits)) + [("ctx", 1)]
-        came = yield swap(far, "shard", 1)
-        near, came = near.reshape(lead), came.reshape(lead)
-        for axis, bit in order:
-            dim = dims.index((axis, bit))
-            dims.pop(dim)
-            index = (slice(None),) * dim
-            send = add(near[index + (1,)], came[index + (1,)])
-            keep = add(near[index + (0,)], came[index + (0,)])
-            near, came = keep, (yield swap(send, axis, bit))
-        return add(near, came)
-
-    high = list(reversed(shard_bits))
-    paths = [path(near_a, far_a, [("ctx", 1)] + high), path(near_b, far_b, high + [("ctx", 1)])]
-    waits = tie([next(p) for p in paths], result_all)
-    waits = [p.send(w) for p, w in zip(paths, waits)]
-    sums = jnp.concatenate([feed_sums, self_sums, late_sums], axis=0)
+    enc_send, head_grads, far_a, far_b = tie((enc_send, head_grads, far_a, far_b), far_b)
+    for _ in range(len(high)):
+        for p in ffn_paths:
+            p.came = tie(p.came, far_b)
+            p.fold()
+            head_grads = tie(head_grads, p.send, p.keep)
+            p.go()
+    enc_came = tie(swap(enc_send, "ctx", 1), *(p.keep for p in ffn_paths))
+    enc_mine = (enc_keep + enc_came.astype(F32)).astype(BF16)
+    grad_encoder = lax.psum(enc_mine, "tensor")
+    for bit in bits_of("tensor")[1:]:
+        early_sums = early_sums + tie(swap(early_sums, "tensor", bit), far_b)
+    head_grads = tie(head_grads, enc_mine, result_all, early_sums)
+
+    dq, down, dtrunk, late_sums = self_backward(
+        scalars, q, kv, kv_sent, head_grads, mixes, self_logs, heads, seg, scale, width
+    )
+    trunk_came = lax.ppermute(dtrunk, "ctx", [(1, 0)])
+    for p in ffn_paths:
+        p.came = tie(p.came, dtrunk, grad_encoder)
+        p.fold()
+    ffn_blocks = jnp.concatenate([p.keep for p in ffn_paths], axis=1)
+    ffn_came = [swap(ffn_blocks[j], "tensor", j) for j in range(1, tensors)]
+    sums = jnp.concatenate([early_sums, late_sums], axis=0)
     for axis, bit in [("shard", 1)] + shard_bits:
         sums = sums + swap(sums, axis, bit)
-    trunk_came = tie(trunk_came, far_a, far_b)
+    paths = [
+        Path(near, tie(swap(far, "shard", 1), ffn_blocks), order)
+        for near, far, order in zip((near_a, near_b), (far_a, far_b), orders)
+    ]
+    for p in paths:
+        p.fold()
+        trunk_came = tie(trunk_came, p.send, p.keep)
+        p.go()
+    trunk_came = tie(trunk_came, ffn_blocks, sums)
     *parts, near, far = input_grad(
         info, dq, down, dtrunk, trunk_came, input_low, qkv_weights, mesh_sizes
     )
     part_came = [swap(parts[j], "tensor", j) for j in range(1, tensors)]
-    waits, ffn_grads = tie((waits, ffn_grads), parts[0])
-    grad_encoder = lax.psum(tie(enc_mine, ffn_grads), "tensor").astype(F32)
-    ffn_grads = ffn_grads.astype(F32) + swap(ffn_grads, "ctx", 1).astype(F32)
     for _ in range(len(high)):
-        waits = [p.send(w) for p, w in zip(paths, waits)]
-    blocks = []
-    for p, w in zip(paths, waits):
-        try:
-            p.send(w)
-        except StopIteration as end:
-            blocks.append(end.value)
-    qkv_grads = join_ctx(reduce_levels(near, far)).astype(F32)
-    grad_q, grad_k, grad_v = (qkv_grads[:, i * columns : (i + 1) * columns] for i in range(3))
-    sums = sums + swap(tie(sums, parts[0]), "ctx", 1)
-    part_came = tie(part_came, sums, qkv_grads, ffn_grads, blocks)
+        for p in paths:
+            p.came = tie(p.came, parts[0])
+            p.fold()
+            p.go()
+    lead = (2,) * len(shard_bits) + near.shape[1:]
+    near, far = near.reshape(lead), swap(far, "shard", 1).reshape(lead)
+    send, keep = add(near[1], far[1]), add(near[0], far[0])
+    for axis, bit in list(reversed(shard_bits))[:-1]:
+        came = swap(send, axis, bit)
+        send, keep = add(keep[1], came[1]), add(keep[0], came[0])
+    came = swap(send, *shard_bits[0])
+    keep = add(keep, came)
+    ffn_total = ffn_blocks[0].astype(F32)
+    for part in tie(ffn_came, parts[0]):
+        ffn_total = ffn_total + part.astype(F32)
+    ffn_total = ffn_total.astype(BF16)
+    sums_came = swap(tie(sums, parts[0]), "ctx", 1)
+    for p in paths:
+        p.fold()
+    squares = jnp.concatenate([p.keep for p in paths], axis=2)
+    square_came = [swap(squares[j], "tensor", j) for j in range(1, tensors)]
+    part_came, square_came = tie((part_came, square_came), keep, ffn_total)
+    square_total = squares[0].astype(F32)
+    for part in square_came:
+        square_total = square_total + part.astype(F32)
+    square_total = square_total.astype(BF16)
+    part_came = tie(part_came, square_total)
     input_mine = grad_one + parts[0]
     for part in part_came:
         input_mine = input_mine + part.astype(F32)
     input_mine = input_mine.astype(BF16)
     input_all = over_tensor(input_mine)
-    sums, blocks = tie((sums, blocks), input_mine)
-    others = over_tensor(sums)
-    square_sums = []
-    for block in blocks:
-        total = block[0].astype(F32)
-        for j in range(1, tensors):
-            total = total + swap(block[j], "tensor", j).astype(F32)
-        square_sums.append(total.astype(BF16))
-    sums = others[0]
-    for other in tie(others[1:], input_all):
-        sums = sums + other
-    squares = join_ctx(jnp.concatenate(square_sums, axis=1)).astype(F32)
+    ctx_came = [swap(a, "ctx", 1) for a in (keep, ffn_total, square_total)]
+    ctx_came, sums_came = tie((ctx_came, sums_came), input_mine)
+    qkv_came, ffn_came, square_came = ctx_came
+    sums = sums + sums_came
+    qkv_grads = [add(keep[r], qkv_came[r ^ 1]) for r in range(ctxs)]
+    first = me_ctx == 0
+    qkv_grads = jnp.concatenate(
+        [jnp.where(first, qkv_grads[r], qkv_grads[r ^ 1]) for r in range(ctxs)]
+    ).astype(F32)
+    grad_q, grad_k, grad_v = (qkv_grads[:, i * columns : (i + 1) * columns] for i in range(3))
+
+    def in_order(mine, other):
+        return [
+            jnp.where(first, mine, other).astype(F32),
+            jnp.where(first, other, mine).astype(F32),
+        ]
+
+    share = piece // ctxs
+    halves = in_order(ffn_total, ffn_came)
+    grad_up = jnp.concatenate([half[:share] for half in halves])
+    grad_down = jnp.concatenate([half[share:] for half in halves])
+    squares = jnp.concatenate(in_order(square_total, square_came))
     grad_ck, grad_cv, grad_o, grad_cq, grad_co = (
         squares[:, i * columns : (i + 1) * columns] for i in range(5)
     )
+    grad_encoder = tie(grad_encoder, input_mine).astype(F32)
+    result_all = tie(result_all, input_mine).astype(F32)
+    input_all = input_all[:1] + list(tie(input_all[1:], sums, qkv_grads, grad_up, squares))
     grad_input = lay_rows(info, input_all)
     me_tensor = info[2]
 
@@ -1470,8 +1551,8 @@
         grad_ck,
         grad_cv,
         grad_co.T,
-        ffn_grads[:piece],
-        ffn_grads[piece:].T,
+        grad_up,
+        grad_down.T,
         mine(later, columns),
         mine(later + tensors, columns),
         sums[18],

time: 453 us -> 440 us (0.971)
  other arithmetic: 22.5 us -> 36.4 us
  waiting for transfers between devices: 157 us -> 144 us
  starting transfers between devices: 76.6 us -> 65.4 us
    ppermute x46, waiting for transfers between devices: 142 us -> 109 us  [swap(): return lax.ppermute(a, axis, [(i, i ^ bit) for i in range(sizes[axis])])]
    psum x1, waiting for transfers between devices: 0.01 us -> 20.3 us  [local(): grad_encoder = lax.psum(enc_mine, 'tensor')]
    ppermute x46, starting transfers between devices: 71.7 us -> 60.5 us  [swap(): return lax.ppermute(a, axis, [(i, i ^ bit) for i in range(sizes[axis])])]
    convert_element_type x9 -> x13, other arithmetic: 8.13 us -> 17.3 us  [add(): return (a.astype(F32) + b.astype(F32)).astype(BF16)]
  transfers between devices with their start and end apart: 51 -> 51, of which waited for: 24 -> 21; matrix products, arithmetic and copies ran while one was open for 6% -> 10% of each run, Pallas kernels for 29% -> 28%
where the time goes in v3:
time: 440 us; the launch traced here: 439 us
  Pallas kernels  153 us (35%)
  waiting for transfers between devices  144 us (33%)
  starting transfers between devices  65.4 us (15%)
  other arithmetic  36.4 us (8%)
  between operations  15.3 us (3%)
  local copies, waits for them, and re-layouts  14.8 us (3%)
  blocking collectives  10.1 us (2%)
    ppermute x46, waiting for transfers between devices, swap(): return lax.ppermute(a, axis, [(i, i ^ bit) for i in range(sizes[axis])])  109 us
    ppermute x46, starting transfers between devices, swap(): return lax.ppermute(a, axis, [(i, i ^ bit) for i in range(sizes[axis])])  60.5 us
    pallas_call x1, Pallas kernels, feed(): pl.pallas_call(feed_kernel, grid_spec=pltpu.PrefetchScalarGridSpec(num_sc...  23.3 us
    psum x1, waiting for transfers between devices, local(): grad_encoder = lax.psum(enc_mine, 'tensor')  20.3 us
    pallas_call x1, Pallas kernels, cross_forward(): pl.pallas_call(cross_forward_kernel, grid_spec=pltpu.PrefetchScalarGridSp...  17.9 us
    convert_element_type x13, other arithmetic, add(): return (a.astype(F32) + b.astype(F32)).astype(BF16)  17.3 us
    pallas_call x1, Pallas kernels, cross_backward(): pl.pallas_call(functools.partial(cross_backward_kernel, scale=scale), gri...  16.6 us
    pallas_call x1, Pallas kernels, self_backward(): pl.pallas_call(functools.partial(self_backward_kernel, heads=heads, seg=s...  16.4 us
  transfers between devices with their start and end apart: 51, of which 21 were waited for; matrix products, arithmetic and copies ran while one was open for 10% of the time, Pallas kernels for 28%

profile of v3, /device:TPU:8, one launch (start us, length us, event | category | flops | bytes accessed | tf_op | source)
XLA Modules:
  0.0 438.8 jit_solution(13485114767285714147)
XLA Ops:
  10.4 3.0 collective-permute-start.1
  14.9 10.1 %all_gather.9.w_ref = bf16[768,576]{1,0:T(8,128)(2,1)} all-gather(bf16[192,576]{1,0:T(8,128)(2,1)S(1)} %pad_maximum_fusion.5), channel_id=1, replica_groups=mesh['shard'=4,'ctx'=2,'tensor'=4] {'shard'}, dimensions={0}, use_global_device_ids=true | all-gather | bytes 1105920 | tf_op jit(solution)/shard_map/all_gather | solution.py:1330
  25.2 5.5 %project.1 = (bf16[1024,192]{1,0:T(8,128)(2,1)}, bf16[1024,384]{1,0:T(8,128)(2,1)}, bf16[1024,768]{1,0:T(8,128)(2,1)}) custom-call(f32[1,1024,768]{2,1,0:T(8,128)} %x_ref.3, bf16[768,576]{1,0:T(8,128)(2,1)} %all_gather.9.w_ref, f32[1,192]{1,0:T(1,128)} %bitcast.158, f32[1,192]{1,0:T(1,128)} %bitcast.159), custom_call_target="tpu_custom_call" | custom-call | flops 9059696 | bytes 62914 | tf_op jit(solution)/shard_map/project/pallas_call | solution.py:591
  31.6 3.4 collective-permute-done.1
  35.1 6.3 %collective-permute-done.2 = bf16[208,768]{1,0:T(8,128)(2,1)S(1)} collective-permute-done((bf16[208,768]{1,0:T(8,128)(2,1)S(1)}, bf16[208,768]{1,0:T(8,128)(2,1)S(1)}, u32[]{:S(2)}, u32[]{:S(2)}) %collective-permute-start.2) | collective-permute-done | bytes 319520 | tf_op jit(solution)/shard_map/ppermute | solution.py:1259
  41.6 1.6 collective-permute-start.3
  43.2 3.5 collective-permute-start.4
  47.3 14.7 %collective-permute-done.4.sent_ref = bf16[1024,384]{1,0:T(8,128)(2,1)S(1)} collective-permute-done((bf16[1024,384]{1,0:T(8,128)(2,1)S(1)}, bf16[1024,384]{1,0:T(8,128)(2,1)S(1)}, u32[]{:S(2)}, u32[]{:S(2)}) %collective-permute-start.4) | collective-permute-done | bytes 786464 | tf_op jit(solution)/shard_map/ppermute | solution.py:1338
  62.9 14.8 %self_forward.1 = (bf16[256,192]{1,0:T(8,128)(2,1)}, bf16[256,192]{1,0:T(8,128)(2,1)}, bf16[256,192]{1,0:T(8,128)(2,1)}, bf16[256,192]{1,0:T(8,128)(2,1)}, f32[8,1024]{1,0:T(8,128)}) custom-call(s32[3]{0:T(128)} %pad_add_fusion.info_ref, s32[16]{0:T(128)} %bitcast.156, s32[2048]{0:T(1024)} %bitcast.154, bf16[1024,192]{1,0:T(8,128)(2,1)} %get-tuple-element.151.q_ref, ...), custom_call_target="tpu_custom_call" | custom-call | flops 16106127 | bytes 31457 | tf_op jit(solution)/shard_map/self_forward/pallas_call | solution.py:256
  77.7 2.0 pad_maximum_fusion.near_ref
  81.0 12.4 %collective-permute-start.9 = (bf16[512,768]{1,0:T(8,128)(2,1)}, bf16[512,768]{1,0:T(8,128)(2,1)S(1)}, u32[]{:S(2)}, u32[]{:S(2)}) collective-permute-start(bf16[512,768]{1,0:T(8,128)(2,1)} %convert_bitcast_fusion), channel_id=1, source_target_pairs={{0,4},{4,0},{1,5},{5,1},{2,6},{6,2},{3,7},{7,3},{8,12},{12,8},{9,1... | collective-permute-start | bytes 2359304 | tf_op jit(solution)/shard_map/ppermute | solution.py:1259
  93.4 3.0 collective-permute-start.7
  99.0 6.9 %assemble.1 = (bf16[768,1536]{1,0:T(8,128)(2,1)}, bf16[4,768,192]{2,1,0:T(8,128)(2,1)}, bf16[768,768]{1,0:T(8,128)(2,1)}, bf16[4,16,768]{2,1,0:T(8,128)(2,1)}) custom-call(s32[3]{0:T(128)} %pad_add_fusion.info_ref, bf16[2,4,208,768]{3,2,1,0:T(8,128)(2,1)} %copy-done, bf16[2,4,208,768]{3,2,1,0:T(8,128)(2,1)} %collective-permute-done.5.far_ref), custom_call_target="tpu_custom_call" | custom-call | bytes 102236 | tf_op jit(solution)/shard_map/assemble/pallas_call | solution.py:649
  106.0 5.8 %collective-permute-done.9.sent_ref = bf16[512,768]{1,0:T(8,128)(2,1)S(1)} collective-permute-done((bf16[512,768]{1,0:T(8,128)(2,1)}, bf16[512,768]{1,0:T(8,128)(2,1)S(1)}, u32[]{:S(2)}, u32[]{:S(2)}) %collective-permute-start.9) | collective-permute-done | bytes 786464 | tf_op jit(solution)/shard_map/ppermute | solution.py:1259
  112.7 7.4 %encode.1 = (bf16[1024,768]{1,0:T(8,128)(2,1)}, bf16[1024,1536]{1,0:T(8,128)(2,1)}) custom-call(s32[3]{0:T(128)} %pad_add_fusion.info_ref, f32[1,512,768]{2,1,0:T(8,128)} %own_ref.1, bf16[512,768]{1,0:T(8,128)(2,1)} %copy-done.12, bf16[768,1536]{1,0:T(8,128)(2,1)} %get-tuple-element.169.w_ref, bf16[4,16,768]{2,1,0:T(8,128)(2,1)} %get-tuple-element.164.bias_ref), custom_call_target="tpu_custom_call" | custom-call | flops 24159192 | bytes 55050 | tf_op jit(solution)/shard_map/encode/pallas_call | solution.py:749
  120.1 3.6 collective-permute-done.8.rest_3_
  123.7 5.1 %after_self.1 = (f32[256,768]{1,0:T(8,128)}, bf16[256,768]{1,0:T(8,128)(2,1)}, bf16[256,768]{1,0:T(8,128)(2,1)}, bf16[256,768]{1,0:T(8,128)(2,1)}) custom-call(s32[3]{0:T(128)} %pad_add_fusion.info_ref, f32[1,1024,768]{2,1,0:T(8,128)} %x_ref.3, bf16[4,768,192]{2,1,0:T(8,128)(2,1)} %get-tuple-element.162.o_ref, bf16[768,768]{1,0:T(8,128)(2,1)} %get-tuple-element.163.cq_ref, ...), custom_call_target="tpu_custom_call" | custom-call | flops 6039797 | bytes 47185 | tf_op jit(solution)/shard_map/after_self/pallas_call | solution.py:711
  128.8 17.9 %cross_forward.1 = (bf16[256,768]{1,0:T(8,128)(2,1)}, f32[48,256]{1,0:T(8,128)}) custom-call(s32[3]{0:T(128)} %pad_add_fusion.info_ref, s32[1]{0:T(128)S(6)} %copy.63.length_ref, bf16[256,768]{1,0:T(8,128)(2,1)} %get-tuple-element.175.q_ref, bf16[1024,1536]{1,0:T(8,128)(2,1)} %get-tuple-element.170.k_ref.v_ref, bf16[1024,1536]{1,0:T(8,128)(2,1)} %get-tuple-element.170.k_ref.v_ref), custom_call_target="tpu_custom_call" | custom-call | flops 16106127 | bytes 39321 | tf_op jit(solution)/shard_map/cross_forward/pallas_call | solution.py:481
  146.7 23.3 %feed.1 = (bf16[256,768]{1,0:T(8,128)(2,1)}, bf16[2,2,2,4,96,768]{5,4,3,2,1,0:T(8,128)(2,1)}, bf16[2,2,2,4,96,768]{5,4,3,2,1,0:T(8,128)(2,1)}, f32[256,768]{1,0:...) custom-call(s32[3]{0:T(128)} %pad_add_fusion.info_ref, ...), custom_call_target="tpu_custom_call" | custom-call | flops 81537272 | bytes 318504 | tf_op jit(solution)/shard_map/feed/pallas_call | solution.py:917
  170.2 16.6 %cross_backward.1 = (bf16[256,768]{1,0:T(8,128)(2,1)}, bf16[1024,768]{1,0:T(8,128)(2,1)}, bf16[1024,768]{1,0:T(8,128)(2,1)}) custom-call(s32[3]{0:T(128)} %pad_add_fusion.info_ref, s32[1]{0:T(128)S(6)} %copy.63.length_ref, bf16[256,768]{1,0:T(8,128)(2,1)} %get-tuple-element.175.q_ref, bf16[1024,1536]{1,0:T(8,128)(2,1)} %get-tuple-element.170.k_ref.v_ref, ...), custom_call_target="tpu_custom_call" | custom-call | flops 40265320 | bytes 78643 | tf_op jit(solution)/shard_map/cross_backward/pallas_call | solution.py:536
  187.0 2.3 add_convert_fusion
  189.3 1.4 collective-permute-start.16
  190.7 1.8 slice_bitcast_fusion
  193.7 6.1 %before_self.1 = (f32[256,768]{1,0:T(8,128)}, bf16[256,768]{1,0:T(8,128)(2,1)}, f32[16,768]{1,0:T(8,128)}, bf16[256,192]{1,0:T(8,128)(2,1)}, bf16[256,192]{1,0:T...) custom-call(s32[3]{0:T(128)} %pad_add_fusion.info_ref, f32[256,768]{1,0:T(8,128)} %get-tuple-element.187.grad_ref, ...), custom_call_target="tpu_custom_call" | custom-call | flops 6039797 | bytes 62914 | tf_op jit(solution)/shard_map/before_self/pallas_call | solution.py:997
  200.6 2.0 collective-permute-start.11
  202.6 2.4 collective-permute-start.12
  205.0 4.2 collective-permute-done.14
  209.2 1.6 collective-permute-start.13
  210.8 6.9 %encoder_grad.1 = (f32[512,768]{1,0:T(8,128)}, bf16[512,768]{1,0:T(8,128)(2,1)}) custom-call(bf16[1024,768]{1,0:T(8,128)(2,1)} %get-tuple-element.192.dk_ref.refs_5_, bf16[1024,768]{1,0:T(8,128)(2,1)} %get-tuple-element.188.dv_ref.refs_6_, bf16[768,1536]{1,0:T(8,128)(2,1)} %get-tuple-element.169.w_ref), custom_call_target="tpu_custom_call" | custom-call | flops 24159192 | bytes 78643 | tf_op jit(solution)/shard_map/encoder_grad/pallas_call | solution.py:1037
  217.7 12.8 %square_grads.1 = (bf16[2,2,4,96,384]{4,3,2,1,0:T(8,128)(2,1)}, bf16[2,2,4,96,576]{4,3,2,1,0:T(8,128)(2,1)}, bf16[2,2,4,96,384]{4,3,2,1,0:T(8,128)(2,1)}, bf16[2,2,4,96,576]{4,3,2,1,0:T(8,128)(2,1)}) custom-call(s32[3]{0:T(128)} %pad_add_fusion.info_ref, bf16[1024,768]{1,0:T(8,128)(2,1)} %get-tuple-element.201.refs_0_.refs_1_, ...), custom_call_target="tpu_custom_call" | custom-call | flops 66437776 | bytes 47185 | tf_op jit(solution)/shard_map/square_grads/pallas_call | solution.py:1108
  230.6 1.4 collective-permute-start.17
  232.0 3.3 collective-permute-start.18
  235.3 3.6 collective-permute-done.18
  239.0 1.7 fusion.12
  240.7 9.2 %collective-permute-done.17 = bf16[512,768]{1,0:T(8,128)(2,1)S(1)} collective-permute-done((bf16[512,768]{1,0:T(8,128)(2,1)}, bf16[512,768]{1,0:T(8,128)(2,1)S(1)}, u32[]{:S(2)}, u32[]{:S(2)}) %collective-permute-start.17) | collective-permute-done | bytes 786464 | tf_op jit(solution)/shard_map/ppermute | solution.py:1259
  251.0 1.7 collective-permute-start.21
  252.7 1.3 collective-permute-start.22
  253.9 16.4 %self_backward.1 = (bf16[1024,192]{1,0:T(8,128)(2,1)}, f32[1024,384]{1,0:T(8,128)}, bf16[1024,384]{1,0:T(8,128)(2,1)}, f32[8,768]{1,0:T(8,128)}) custom-call(s32[3]{0:T(128)} %pad_add_fusion.info_ref, s32[16]{0:T(128)} %bitcast.157, s32[2048]{0:T(1024)} %bitcast.155, bf16[1024,192]{1,0:T(8,128)(2,1)} %get-tuple-element.151.q_ref, ...), custom_call_target="tpu_custom_call" | custom-call | flops 40265320 | bytes 78643 | tf_op jit(solution)/shard_map/self_backward/pallas_call | solution.py:412
  272.6 1.3 collective-permute-start.19
  273.9 1.4 fusion.50
  276.0 20.3 %all-reduce.4.cloned.1.call-done = bf16[512,768]{1,0:T(8,128)(2,1)} async-done(((bf16[512,768]{1,0:T(8,128)(2,1)}), bf16[512,768]{1,0:T(8,128)(2,1)}) %all-reduce.4.cloned.1.call-update) | async-done | bytes 786448 | tf_op jit(solution)/shard_map/psum | solution.py:1442
  297.5 1.3 add_convert_fusion.9
  299.0 2.5 add_convert_fusion.7
  301.5 1.5 collective-permute-start.29
  302.9 3.0 add_convert_fusion.4
  305.9 1.5 collective-permute-start.31
  309.2 1.5 collective-permute-start.39
  312.8 8.6 %input_grad.1 = (f32[256,768]{1,0:T(8,128)}, bf16[256,768]{1,0:T(8,128)(2,1)}, bf16[256,768]{1,0:T(8,128)(2,1)}, bf16[256,768]{1,0:T(8,128)(2,1)}, bf16[2,2,96,5...) custom-call(s32[3]{0:T(128)} %pad_add_fusion.info_ref, bf16[1024,192]{1,0:T(8,128)(2,1)} %get-tuple-element.230.dq_ref, ...), custom_call_target="tpu_custom_call" | custom-call | flops 18119392 | bytes 110100 | tf_op jit(solution)/shard_map/input_grad/pallas_call | solution.py:1164
  321.5 9.6 %collective-permute-done.39 = bf16[192,768]{1,0:T(8,128)(2,1)} collective-permute-done((bf16[192,768]{1,0:T(8,128)(2,1)}, bf16[192,768]{1,0:T(8,128)(2,1)}, u32[]{:S(2)}, u32[]{:S(2)}) %collective-permute-start.39) | collective-permute-done | bytes 294944 | tf_op jit(solution)/shard_map/ppermute | solution.py:1259
  331.1 3.1 collective-permute-start.26
  334.2 2.6 collective-permute-done.40
  336.9 1.3 fusion.17
  342.8 4.7 %collective-permute-done.30 = bf16[4,96,384]{2,1,0:T(8,128)(2,1)S(1)} collective-permute-done((bf16[4,96,384]{2,1,0:T(8,128)(2,1)S(1)}, bf16[4,96,384]{2,1,0:T(8,128)(2,1)S(1)}, u32[]{:S(2)}, u32[]{:S(2)}) %collective-permute-start.30) | collective-permute-done | bytes 294944 | tf_op jit(solution)/shard_map/ppermute | solution.py:1259
  349.2 3.7 collective-permute-done.32
  354.2 2.9 collective-permute-start.33
  358.7 12.9 %collective-permute-done.27 = bf16[256,768]{1,0:T(8,128)(2,1)S(1)} collective-permute-done((bf16[256,768]{1,0:T(8,128)(2,1)}, bf16[256,768]{1,0:T(8,128)(2,1)S(1)}, u32[]{:S(2)}, u32[]{:S(2)}) %collective-permute-start.27) | collective-permute-done | bytes 393248 | tf_op jit(solution)/shard_map/ppermute | solution.py:1259
  372.2 9.1 %collective-permute-done.28 = bf16[256,768]{1,0:T(8,128)(2,1)S(1)} collective-permute-done((bf16[256,768]{1,0:T(8,128)(2,1)S(1)}, bf16[256,768]{1,0:T(8,128)(2,1)S(1)}, u32[]{:S(2)}, u32[]{:S(2)}) %collective-permute-start.28) | collective-permute-done | bytes 393248 | tf_op jit(solution)/shard_map/ppermute | solution.py:1259
  381.9 1.5 collective-permute-start.44
  383.9 3.9 collective-permute-done.35
  390.0 1.9 bitcast_convert_fusion
  394.2 1.3 collective-permute-start.43
  402.6 17.1 %collective-permute-done.42.refs_2_ = bf16[256,768]{1,0:T(8,128)(2,1)S(1)} collective-permute-done((bf16[256,768]{1,0:T(8,128)(2,1)S(1)}, bf16[256,768]{1,0:T(8,128)(2,1)S(1)}, u32[]{:S(2)}, u32[]{:S(2)}) %collective-permute-start.42) | collective-permute-done | bytes 393248 | tf_op jit(solution)/shard_map/ppermute | solution.py:1259
  419.7 7.6 %collective-permute-done.43.refs_3_ = bf16[256,768]{1,0:T(8,128)(2,1)S(1)} collective-permute-done((bf16[256,768]{1,0:T(8,128)(2,1)S(1)}, bf16[256,768]{1,0:T(8,128)(2,1)S(1)}, u32[]{:S(2)}, u32[]{:S(2)}) %collective-permute-start.43) | collective-permute-done | bytes 393248 | tf_op jit(solution)/shard_map/ppermute | solution.py:1259
  428.1 4.2 lay_rows.1
  (211 shorter events, 46.4 us)
Async XLA Ops:
  7.2 139.5 %all-gather.3.cloned.1.call-start = ((), (), s32[]{:S(2)}) async-start(), calls=%async_computation | async-start | bytes 11280384 | tf_op jit(solution)/shard_map/all_gather | solution.py:1337
  10.3 21.4 %collective-permute-start = (bf16[208,768]{1,0:T(8,128)(2,1)S(1)}, bf16[208,768]{1,0:T(8,128)(2,1)S(1)}, u32[]{:S(2)}, u32[]{:S(2)}) collective-permute-start(bf16[208,768]{1,0:T(8,128)(2,1)S(1)} %pad_maximum_fusion.4), channel_id=1, source_target_pairs={{0,1},{1,0},{2,3},{3,2},{4,5},{5,4},{6,7},{7,6},{8,9},{9,8},{10,11... | collective-permute-start | bytes 958472 | tf_op jit(solution)/shard_map/ppermute | solution.py:1259
  10.4 24.7 %collective-permute-start.1 = (bf16[208,768]{1,0:T(8,128)(2,1)S(1)}, bf16[208,768]{1,0:T(8,128)(2,1)S(1)}, u32[]{:S(2)}, u32[]{:S(2)}) collective-permute-start(bf16[208,768]{1,0:T(8,128)(2,1)S(1)} %pad_maximum_fusion.4), channel_id=1, source_target_pairs={{0,2},{1,3},{2,0},{3,1},{4,6},{5,7},{6,4},{7,5},{8,10},{9,11},{10,... | collective-permute-start | bytes 958472 | tf_op jit(solution)/shard_map/ppermute | solution.py:1259
  13.4 28.0 %collective-permute-start.2 = (bf16[208,768]{1,0:T(8,128)(2,1)S(1)}, bf16[208,768]{1,0:T(8,128)(2,1)S(1)}, u32[]{:S(2)}, u32[]{:S(2)}) collective-permute-start(bf16[208,768]{1,0:T(8,128)(2,1)S(1)} %pad_maximum_fusion.4), channel_id=1, source_target_pairs={{0,3},{1,2},{2,1},{3,0},{4,7},{5,6},{6,5},{7,4},{8,11},{9,10},{10,... | collective-permute-start | bytes 958472 | tf_op jit(solution)/shard_map/ppermute | solution.py:1259
  41.6 36.2 %copy-start.2 = (bf16[4,208,768]{2,1,0:T(8,128)(2,1)}, bf16[4,208,768]{2,1,0:T(8,128)(2,1)S(1)}, u32[]{:S(2)}) copy-start(bf16[4,208,768]{2,1,0:T(8,128)(2,1)S(1)} %pad_maximum_fusion.2) | copy-start | bytes 3833860
  41.6 209.4 %all-gather.5.cloned.1.call-start = ((), (), s32[]{:S(2)}) async-start(), calls=%async_computation.1 | async-start | bytes 1966080 | tf_op jit(solution)/shard_map/all_gather | solution.py:1379
  41.6 36.1 %collective-permute-start.3 = (bf16[4,208,768]{2,1,0:T(8,128)(2,1)S(1)}, bf16[4,208,768]{2,1,0:T(8,128)(2,1)}, u32[]{:S(2)}, u32[]{:S(2)}) collective-permute-start(bf16[4,208,768]{2,1,0:T(8,128)(2,1)S(1)} %pad_maximum_fusion.2), channel_id=1, source_target_pairs={{0,16},{8,24},{16,0},{24,8},{1,17},{9,25},{17,1},{25,9},{2,18},{10... | collective-permute-start | bytes 3833864 | tf_op jit(solution)/shard_map/ppermute | solution.py:1259
  43.2 18.8 %collective-permute-start.4 = (bf16[1024,384]{1,0:T(8,128)(2,1)S(1)}, bf16[1024,384]{1,0:T(8,128)(2,1)S(1)}, u32[]{:S(2)}, u32[]{:S(2)}) collective-permute-start(bf16[1024,384]{1,0:T(8,128)(2,1)S(1)} %copy-done.4), channel_id=1, source_target_pairs={{0,4},{1,5},{2,6},{3,7},{8,12},{9,13},{10,14},{11,15},{16,20},{17,... | collective-permute-start | bytes 2359304 | tf_op jit(solution)/shard_map/ppermute | solution.py:1338
  79.8 19.3 %copy-start = (bf16[2,4,208,768]{3,2,1,0:T(8,128)(2,1)}, bf16[2,4,208,768]{3,2,1,0:T(8,128)(2,1)S(1)}, u32[]{:S(2)}) copy-start(bf16[2,4,208,768]{3,2,1,0:T(8,128)(2,1)S(1)} %pad_maximum_fusion.near_ref) | copy-start | bytes 7667716
  79.8 17.1 %copy-start.32 = (f32[768]{0:T(1024)S(1)}, f32[768]{0:T(1024)}, u32[]{:S(2)}) copy-start(f32[768]{0:T(1024)} %param.53) | copy-start | bytes 9220
  79.8 17.1 %copy-start.34 = (f32[768]{0:T(1024)S(1)}, f32[768]{0:T(1024)}, u32[]{:S(2)}) copy-start(f32[768]{0:T(1024)} %param.54) | copy-start | bytes 9220
  79.8 17.8 %copy-start.35 = (f32[768]{0:T(1024)S(1)}, f32[768]{0:T(1024)}, u32[]{:S(2)}) copy-start(f32[768]{0:T(1024)} %param.50) | copy-start | bytes 9220
  79.9 17.8 %copy-start.36 = (f32[768]{0:T(1024)S(1)}, f32[768]{0:T(1024)}, u32[]{:S(2)}) copy-start(f32[768]{0:T(1024)} %param.55) | copy-start | bytes 9220
  79.9 17.8 %copy-start.37 = (f32[768]{0:T(1024)S(1)}, f32[768]{0:T(1024)}, u32[]{:S(2)}) copy-start(f32[768]{0:T(1024)} %param.56) | copy-start | bytes 9220
  79.9 17.8 %copy-start.38 = (f32[768]{0:T(1024)S(1)}, f32[768]{0:T(1024)}, u32[]{:S(2)}) copy-start(f32[768]{0:T(1024)} %param.52) | copy-start | bytes 9220
  79.9 17.8 %copy-start.39 = (f32[768]{0:T(1024)S(1)}, f32[768]{0:T(1024)}, u32[]{:S(2)}) copy-start(f32[768]{0:T(1024)} %param.57) | copy-start | bytes 9220
  79.9 17.8 %copy-start.40 = (f32[768]{0:T(1024)S(1)}, f32[768]{0:T(1024)}, u32[]{:S(2)}) copy-start(f32[768]{0:T(1024)} %param.58) | copy-start | bytes 9220
  79.9 19.1 %collective-permute-start.5 = (bf16[2,4,208,768]{3,2,1,0:T(8,128)(2,1)S(1)}, bf16[2,4,208,768]{3,2,1,0:T(8,128)(2,1)}, u32[]{:S(2)}, u32[]{:S(2)}) collective-permute-start(bf16[2,4,208,768]{3,2,1,0:T(8,128)(2,1)S(1)} %pad_maximum_fusion.near_ref), channel_id=1, source_target_pairs={{0,8},{8,0},{16,24},{24,16},{1,9},{9,1},{17,25},{25,17},{2,10},{10... | collective-permute-start | bytes 7667720 | tf_op jit(solution)/shard_map/ppermute | solution.py:1259
  81.0 30.8 %collective-permute-start.9 = (bf16[512,768]{1,0:T(8,128)(2,1)}, bf16[512,768]{1,0:T(8,128)(2,1)S(1)}, u32[]{:S(2)}, u32[]{:S(2)}) collective-permute-start(bf16[512,768]{1,0:T(8,128)(2,1)} %convert_bitcast_fusion), channel_id=1, source_target_pairs={{0,4},{4,0},{1,5},{5,1},{2,6},{6,2},{3,7},{7,3},{8,12},{12,8},{9,1... | collective-permute-start | bytes 2359304 | tf_op jit(solution)/shard_map/ppermute | solution.py:1259
  93.4 26.7 %collective-permute-start.6 = (bf16[256,192]{1,0:T(8,128)(2,1)S(1)}, bf16[256,192]{1,0:T(8,128)(2,1)}, u32[]{:S(2)}, u32[]{:S(2)}) collective-permute-start(bf16[256,192]{1,0:T(8,128)(2,1)S(1)} %copy-done.23), channel_id=1, source_target_pairs={{0,1},{1,0},{2,3},{3,2},{4,5},{5,4},{6,7},{7,6},{8,9},{9,8},{10,11... | collective-permute-start | bytes 294920 | tf_op jit(solution)/shard_map/ppermute | solution.py:1259
  93.4 26.7 %collective-permute-start.7 = (bf16[256,192]{1,0:T(8,128)(2,1)}, bf16[256,192]{1,0:T(8,128)(2,1)}, u32[]{:S(2)}, u32[]{:S(2)}) collective-permute-start(bf16[256,192]{1,0:T(8,128)(2,1)} %get-tuple-element.167.rest_6_), channel_id=1, source_target_pairs={{0,2},{1,3},{2,0},{3,1},{4,6},{5,7},{6,4},{7,5},{8,10},{9,11},{10,... | collective-permute-start | bytes 294920 | tf_op jit(solution)/shard_map/ppermute | solution.py:1259
  96.4 27.4 %collective-permute-start.8 = (bf16[256,192]{1,0:T(8,128)(2,1)}, bf16[256,192]{1,0:T(8,128)(2,1)}, u32[]{:S(2)}, u32[]{:S(2)}) collective-permute-start(bf16[256,192]{1,0:T(8,128)(2,1)} %get-tuple-element.168.rest_7_), channel_id=1, source_target_pairs={{0,3},{1,2},{2,1},{3,0},{4,7},{5,6},{6,5},{7,4},{8,11},{9,10},{10,... | collective-permute-start | bytes 294920 | tf_op jit(solution)/shard_map/ppermute | solution.py:1259
  170.0 17.0 %collective-permute-start.10 = (bf16[2,2,2,4,96,768]{5,4,3,2,1,0:T(8,128)(2,1)}, bf16[2,2,2,4,96,768]{5,4,3,2,1,0:T(8,128)(2,1)}, u32[]{:S(2)}, u32[]{:S(2)}) collective-permute-start(bf16[2,2,2,4,96,768]{5,4,3,2,1,0:T(8,128)(2,1)} %get-tuple-element.181), channel_id=1, source_target_pairs={{0,8},{8,0},{16,24},{24,16},{1,9},{9,1},{17,25},{25,17},{2,10},{10... | collective-permute-start | bytes 14155784 | tf_op jit(solution)/shard_map/ppermute | solution.py:1259
  170.1 126.2 %all-reduce.4.cloned.1.call-start = ((), (), s32[]{:S(2)}) async-start(), calls=%async_computation.2 | async-start | bytes 1572864 | tf_op jit(solution)/shard_map/psum | solution.py:1442
  189.3 49.6 %collective-permute-start.16 = (bf16[2,4,96,768]{3,2,1,0:T(8,128)(2,1)S(1)}, bf16[2,4,96,768]{3,2,1,0:T(8,128)(2,1)S(1)}, u32[]{:S(2)}, u32[]{:S(2)}) collective-permute-start(bf16[2,4,96,768]{3,2,1,0:T(8,128)(2,1)S(1)} %get-tuple-element.313), channel_id=1, source_target_pairs={{0,16},{8,24},{16,0},{24,8},{1,17},{9,25},{17,1},{25,9},{2,18},{10... | collective-permute-start | bytes 3538952 | tf_op jit(solution)/shard_map/ppermute | solution.py:1259
  193.2 45.7 %collective-permute-start.15 = (bf16[2,4,96,768]{3,2,1,0:T(8,128)(2,1)S(1)}, bf16[2,4,96,768]{3,2,1,0:T(8,128)(2,1)S(1)}, u32[]{:S(2)}, u32[]{:S(2)}) collective-permute-start(bf16[2,4,96,768]{3,2,1,0:T(8,128)(2,1)S(1)} %get-tuple-element.315), channel_id=1, source_target_pairs={{0,4},{4,0},{1,5},{5,1},{2,6},{6,2},{3,7},{7,3},{8,12},{12,8},{9,1... | collective-permute-start | bytes 3538952 | tf_op jit(solution)/shard_map/ppermute | solution.py:1259
  200.6 8.7 %collective-permute-start.14 = (f32[32,768]{1,0:T(8,128)S(1)}, f32[32,768]{1,0:T(8,128)S(1)}, u32[]{:S(2)}, u32[]{:S(2)}) collective-permute-start(f32[32,768]{1,0:T(8,128)S(1)} %constant_dynamic-update-slice_fusion), channel_id=1, source_target_pairs={{0,1},{1,0},{2,3},{3,2},{4,5},{5,4},{6,7},{7,6},{8,9},{9,8},{10,11... | collective-permute-start | bytes 294920 | tf_op jit(solution)/shard_map/ppermute | solution.py:1259
  200.6 30.0 %collective-permute-start.11 = (bf16[256,192]{1,0:T(8,128)(2,1)}, bf16[256,192]{1,0:T(8,128)(2,1)S(1)}, u32[]{:S(2)}, u32[]{:S(2)}) collective-permute-start(bf16[256,192]{1,0:T(8,128)(2,1)} %get-tuple-element.195), channel_id=1, source_target_pairs={{0,1},{1,0},{2,3},{3,2},{4,5},{5,4},{6,7},{7,6},{8,9},{9,8},{10,11... | collective-permute-start | bytes 294920 | tf_op jit(solution)/shard_map/ppermute | solution.py:1259
  202.6 28.0 %collective-permute-start.12 = (bf16[256,192]{1,0:T(8,128)(2,1)}, bf16[256,192]{1,0:T(8,128)(2,1)S(1)}, u32[]{:S(2)}, u32[]{:S(2)}) collective-permute-start(bf16[256,192]{1,0:T(8,128)(2,1)} %get-tuple-element.196), channel_id=1, source_target_pairs={{0,2},{1,3},{2,0},{3,1},{4,6},{5,7},{6,4},{7,5},{8,10},{9,11},{10,... | collective-permute-start | bytes 294920 | tf_op jit(solution)/shard_map/ppermute | solution.py:1259
  209.2 21.4 %collective-permute-start.13 = (bf16[256,192]{1,0:T(8,128)(2,1)}, bf16[256,192]{1,0:T(8,128)(2,1)S(1)}, u32[]{:S(2)}, u32[]{:S(2)}) collective-permute-start(bf16[256,192]{1,0:T(8,128)(2,1)} %get-tuple-element.197), channel_id=1, source_target_pairs={{0,3},{1,2},{2,1},{3,0},{4,7},{5,6},{6,5},{7,4},{8,11},{9,10},{10,... | collective-permute-start | bytes 294920 | tf_op jit(solution)/shard_map/ppermute | solution.py:1259
  230.6 19.3 %collective-permute-start.17 = (bf16[512,768]{1,0:T(8,128)(2,1)}, bf16[512,768]{1,0:T(8,128)(2,1)S(1)}, u32[]{:S(2)}, u32[]{:S(2)}) collective-permute-start(bf16[512,768]{1,0:T(8,128)(2,1)} %get-tuple-element.223), channel_id=1, source_target_pairs={{0,4},{4,0},{1,5},{5,1},{2,6},{6,2},{3,7},{7,3},{8,12},{12,8},{9,1... | collective-permute-start | bytes 2359304 | tf_op jit(solution)/shard_map/ppermute | solution.py:1259
  232.0 6.9 %collective-permute-start.18 = (f32[32,768]{1,0:T(8,128)S(1)}, f32[32,768]{1,0:T(8,128)S(1)}, u32[]{:S(2)}, u32[]{:S(2)}) collective-permute-start(f32[32,768]{1,0:T(8,128)S(1)} %add.176), channel_id=1, source_target_pairs={{0,2},{1,3},{2,0},{3,1},{4,6},{5,7},{6,4},{7,5},{8,10},{9,11},{10,... | collective-permute-start | bytes 294920 | tf_op jit(solution)/shard_map/ppermute | solution.py:1259
  235.3 63.5 %collective-permute-start.23 = (bf16[2,2,4,96,576]{4,3,2,1,0:T(8,128)(2,1)}, bf16[2,2,4,96,576]{4,3,2,1,0:T(8,128)(2,1)}, u32[]{:S(2)}, u32[]{:S(2)}) collective-permute-start(bf16[2,2,4,96,576]{4,3,2,1,0:T(8,128)(2,1)} %get-tuple-element.211), channel_id=1, source_target_pairs={{0,8},{8,0},{16,24},{24,16},{1,9},{9,1},{17,25},{25,17},{2,10},{10... | collective-permute-start | bytes 5308424 | tf_op jit(solution)/shard_map/ppermute | solution.py:1259
  251.0 24.3 %collective-permute-start.21 = (bf16[4,96,768]{2,1,0:T(8,128)(2,1)}, bf16[4,96,768]{2,1,0:T(8,128)(2,1)}, u32[]{:S(2)}, u32[]{:S(2)}) collective-permute-start(bf16[4,96,768]{2,1,0:T(8,128)(2,1)} %get-tuple-element.323), channel_id=1, source_target_pairs={{0,16},{8,24},{16,0},{24,8},{1,17},{9,25},{17,1},{25,9},{2,18},{10... | collective-permute-start | bytes 1769480 | tf_op jit(solution)/shard_map/ppermute | solution.py:1259
  252.7 43.6 %collective-permute-start.22 = (bf16[4,96,768]{2,1,0:T(8,128)(2,1)S(1)}, bf16[4,96,768]{2,1,0:T(8,128)(2,1)}, u32[]{:S(2)}, u32[]{:S(2)}) collective-permute-start(bf16[4,96,768]{2,1,0:T(8,128)(2,1)S(1)} %copy-done.16), channel_id=1, source_target_pairs={{0,4},{4,0},{1,5},{5,1},{2,6},{6,2},{3,7},{7,3},{8,12},{12,8},{9,1... | collective-permute-start | bytes 1769480 | tf_op jit(solution)/shard_map/ppermute | solution.py:1259
  253.9 44.9 %collective-permute-start.20 = (bf16[2,2,4,96,384]{4,3,2,1,0:T(8,128)(2,1)}, bf16[2,2,4,96,384]{4,3,2,1,0:T(8,128)(2,1)}, u32[]{:S(2)}, u32[]{:S(2)}) collective-permute-start(bf16[2,2,4,96,384]{4,3,2,1,0:T(8,128)(2,1)} %get-tuple-element.234), channel_id=1, source_target_pairs={{0,8},{8,0},{16,24},{24,16},{1,9},{9,1},{17,25},{25,17},{2,10},{10... | collective-permute-start | bytes 3538952 | tf_op jit(solution)/shard_map/ppermute | solution.py:1259
  271.1 1.5 collective-permute-start.24
  272.6 38.0 %collective-permute-start.19 = (bf16[1024,384]{1,0:T(8,128)(2,1)}, bf16[1024,384]{1,0:T(8,128)(2,1)S(1)}, u32[]{:S(2)}, u32[]{:S(2)}) collective-permute-start(bf16[1024,384]{1,0:T(8,128)(2,1)} %get-tuple-element.232.dtrunk_ref), channel_id=1, source_target_pairs={{4,0},{5,1},{6,2},{7,3},{12,8},{13,9},{14,10},{15,11},{20,16},{21,... | collective-permute-start | bytes 2359304 | tf_op jit(solution)/shard_map/ppermute | solution.py:1450
  275.3 33.9 %collective-permute-start.25 = (f32[40,768]{1,0:T(8,128)}, f32[40,768]{1,0:T(8,128)}, u32[]{:S(2)}, u32[]{:S(2)}) collective-permute-start(f32[40,768]{1,0:T(8,128)} %fusion.50), channel_id=1, source_target_pairs={{0,16},{8,24},{16,0},{24,8},{1,17},{9,25},{17,1},{25,9},{2,18},{10... | collective-permute-start | bytes 368648 | tf_op jit(solution)/shard_map/ppermute | solution.py:1259
  301.5 36.7 %collective-permute-start.29 = (bf16[2,4,96,384]{3,2,1,0:T(8,128)(2,1)}, bf16[2,4,96,384]{3,2,1,0:T(8,128)(2,1)}, u32[]{:S(2)}, u32[]{:S(2)}) collective-permute-start(bf16[2,4,96,384]{3,2,1,0:T(8,128)(2,1)} %get-tuple-element.319), channel_id=1, source_target_pairs={{0,4},{4,0},{1,5},{5,1},{2,6},{6,2},{3,7},{7,3},{8,12},{12,8},{9,1... | collective-permute-start | bytes 1769480 | tf_op jit(solution)/shard_map/ppermute | solution.py:1259
  305.9 34.5 %collective-permute-start.31 = (bf16[2,4,96,576]{3,2,1,0:T(8,128)(2,1)}, bf16[2,4,96,576]{3,2,1,0:T(8,128)(2,1)}, u32[]{:S(2)}, u32[]{:S(2)}) collective-permute-start(bf16[2,4,96,576]{3,2,1,0:T(8,128)(2,1)} %get-tuple-element.317), channel_id=1, source_target_pairs={{0,16},{8,24},{16,0},{24,8},{1,17},{9,25},{17,1},{25,9},{2,18},{10... | collective-permute-start | bytes 2654216 | tf_op jit(solution)/shard_map/ppermute | solution.py:1259
  308.3 13.1 %collective-permute-start.38 = (bf16[192,768]{1,0:T(8,128)(2,1)}, bf16[192,768]{1,0:T(8,128)(2,1)}, u32[]{:S(2)}, u32[]{:S(2)}) collective-permute-start(bf16[192,768]{1,0:T(8,128)(2,1)} %get-tuple-element.325), channel_id=1, source_target_pairs={{0,1},{1,0},{2,3},{3,2},{4,5},{5,4},{6,7},{7,6},{8,9},{9,8},{10,11... | collective-permute-start | bytes 884744 | tf_op jit(solution)/shard_map/ppermute | solution.py:1259
  309.2 21.9 %collective-permute-start.39 = (bf16[192,768]{1,0:T(8,128)(2,1)}, bf16[192,768]{1,0:T(8,128)(2,1)}, u32[]{:S(2)}, u32[]{:S(2)}) collective-permute-start(bf16[192,768]{1,0:T(8,128)(2,1)} %get-tuple-element.326), channel_id=1, source_target_pairs={{0,2},{1,3},{2,0},{3,1},{4,6},{5,7},{6,4},{7,5},{8,10},{9,11},{10,... | collective-permute-start | bytes 884744 | tf_op jit(solution)/shard_map/ppermute | solution.py:1259
  310.7 26.2 %collective-permute-start.40 = (bf16[192,768]{1,0:T(8,128)(2,1)}, bf16[192,768]{1,0:T(8,128)(2,1)}, u32[]{:S(2)}, u32[]{:S(2)}) collective-permute-start(bf16[192,768]{1,0:T(8,128)(2,1)} %get-tuple-element.324), channel_id=1, source_target_pairs={{0,3},{1,2},{2,1},{3,0},{4,7},{5,6},{6,5},{7,4},{8,11},{9,10},{10,... | collective-permute-start | bytes 884744 | tf_op jit(solution)/shard_map/ppermute | solution.py:1259
  321.4 20.7 %collective-permute-start.36 = (bf16[2,2,96,576]{3,2,1,0:T(8,128)(2,1)}, bf16[2,2,96,576]{3,2,1,0:T(8,128)(2,1)S(1)}, u32[]{:S(2)}, u32[]{:S(2)}) collective-permute-start(bf16[2,2,96,576]{3,2,1,0:T(8,128)(2,1)} %get-tuple-element.252), channel_id=1, source_target_pairs={{0,8},{8,0},{16,24},{24,16},{1,9},{9,1},{17,25},{25,17},{2,10},{10... | collective-permute-start | bytes 1327112 | tf_op jit(solution)/shard_map/ppermute | solution.py:1259
  331.1 26.0 %collective-permute-start.26 = (bf16[256,768]{1,0:T(8,128)(2,1)}, bf16[256,768]{1,0:T(8,128)(2,1)S(1)}, u32[]{:S(2)}, u32[]{:S(2)}) collective-permute-start(bf16[256,768]{1,0:T(8,128)(2,1)} %get-tuple-element.246), channel_id=1, source_target_pairs={{0,1},{1,0},{2,3},{3,2},{4,5},{5,4},{6,7},{7,6},{8,9},{9,8},{10,11... | collective-permute-start | bytes 1179656 | tf_op jit(solution)/shard_map/ppermute | solution.py:1259
  336.9 34.8 %collective-permute-start.27 = (bf16[256,768]{1,0:T(8,128)(2,1)}, bf16[256,768]{1,0:T(8,128)(2,1)S(1)}, u32[]{:S(2)}, u32[]{:S(2)}) collective-permute-start(bf16[256,768]{1,0:T(8,128)(2,1)} %get-tuple-element.247), channel_id=1, source_target_pairs={{0,2},{1,3},{2,0},{3,1},{4,6},{5,7},{6,4},{7,5},{8,10},{9,11},{10,... | collective-permute-start | bytes 1179656 | tf_op jit(solution)/shard_map/ppermute | solution.py:1259
  338.2 43.2 %collective-permute-start.28 = (bf16[256,768]{1,0:T(8,128)(2,1)S(1)}, bf16[256,768]{1,0:T(8,128)(2,1)S(1)}, u32[]{:S(2)}, u32[]{:S(2)}) collective-permute-start(bf16[256,768]{1,0:T(8,128)(2,1)S(1)} %copy-done.41), channel_id=1, source_target_pairs={{0,3},{1,2},{2,1},{3,0},{4,7},{5,6},{6,5},{7,4},{8,11},{9,10},{10,... | collective-permute-start | bytes 1179656 | tf_op jit(solution)/shard_map/ppermute | solution.py:1259
  340.4 7.2 %collective-permute-start.30 = (bf16[4,96,384]{2,1,0:T(8,128)(2,1)S(1)}, bf16[4,96,384]{2,1,0:T(8,128)(2,1)S(1)}, u32[]{:S(2)}, u32[]{:S(2)}) collective-permute-start(bf16[4,96,384]{2,1,0:T(8,128)(2,1)S(1)} %fusion.28), channel_id=1, source_target_pairs={{0,16},{8,24},{16,0},{24,8},{1,17},{9,25},{17,1},{25,9},{2,18},{10... | collective-permute-start | bytes 884744 | tf_op jit(solution)/shard_map/ppermute | solution.py:1259
  342.2 10.8 %collective-permute-start.32 = (bf16[4,96,576]{2,1,0:T(8,128)(2,1)S(1)}, bf16[4,96,576]{2,1,0:T(8,128)(2,1)S(1)}, u32[]{:S(2)}, u32[]{:S(2)}) collective-permute-start(bf16[4,96,576]{2,1,0:T(8,128)(2,1)S(1)} %fusion.22), channel_id=1, source_target_pairs={{0,4},{4,0},{1,5},{5,1},{2,6},{6,2},{3,7},{7,3},{8,12},{12,8},{9,1... | collective-permute-start | bytes 1327112 | tf_op jit(solution)/shard_map/ppermute | solution.py:1259
  347.6 10.3 %collective-permute-start.37 = (bf16[2,96,576]{2,1,0:T(8,128)(2,1)S(1)}, bf16[2,96,576]{2,1,0:T(8,128)(2,1)S(1)}, u32[]{:S(2)}, u32[]{:S(2)}) collective-permute-start(bf16[2,96,576]{2,1,0:T(8,128)(2,1)S(1)} %fusion.38), channel_id=1, source_target_pairs={{0,16},{8,24},{16,0},{24,8},{1,17},{9,25},{17,1},{25,9},{2,18},{10... | collective-permute-start | bytes 663560 | tf_op jit(solution)/shard_map/ppermute | solution.py:1259
  354.2 34.3 %copy-start.13 = (f32[256,768]{1,0:T(8,128)S(1)}, f32[256,768]{1,0:T(8,128)}, u32[]{:S(2)}) copy-start(f32[256,768]{1,0:T(8,128)} %get-tuple-element.189) | copy-start | bytes 2359300
  354.2 34.3 %copy-start.15 = (f32[256,768]{1,0:T(8,128)S(1)}, f32[256,768]{1,0:T(8,128)}, u32[]{:S(2)}) copy-start(f32[256,768]{1,0:T(8,128)} %get-tuple-element.245) | copy-start | bytes 2359300
  354.2 27.7 %collective-permute-start.33 = (bf16[96,960]{1,0:T(8,128)(2,1)S(1)}, bf16[96,960]{1,0:T(8,128)(2,1)S(1)}, u32[]{:S(2)}, u32[]{:S(2)}) collective-permute-start(bf16[96,960]{1,0:T(8,128)(2,1)S(1)} %get-tuple-element.333), channel_id=1, source_target_pairs={{0,1},{1,0},{2,3},{3,2},{4,5},{5,4},{6,7},{7,6},{8,9},{9,8},{10,11... | collective-permute-start | bytes 552968 | tf_op jit(solution)/shard_map/ppermute | solution.py:1259
  357.1 26.8 %collective-permute-start.34 = (bf16[96,960]{1,0:T(8,128)(2,1)S(1)}, bf16[96,960]{1,0:T(8,128)(2,1)S(1)}, u32[]{:S(2)}, u32[]{:S(2)}) collective-permute-start(bf16[96,960]{1,0:T(8,128)(2,1)S(1)} %get-tuple-element.334), channel_id=1, source_target_pairs={{0,2},{1,3},{2,0},{3,1},{4,6},{5,7},{6,4},{7,5},{8,10},{9,11},{10,... | collective-permute-start | bytes 552968 | tf_op jit(solution)/shard_map/ppermute | solution.py:1259
  357.9 29.9 %collective-permute-start.35 = (bf16[96,960]{1,0:T(8,128)(2,1)S(1)}, bf16[96,960]{1,0:T(8,128)(2,1)S(1)}, u32[]{:S(2)}, u32[]{:S(2)}) collective-permute-start(bf16[96,960]{1,0:T(8,128)(2,1)S(1)} %get-tuple-element.332), channel_id=1, source_target_pairs={{0,3},{1,2},{2,1},{3,0},{4,7},{5,6},{6,5},{7,4},{8,11},{9,10},{10,... | collective-permute-start | bytes 552968 | tf_op jit(solution)/shard_map/ppermute | solution.py:1259
  371.7 21.5 %collective-permute-start.47 = (f32[40,768]{1,0:T(8,128)S(1)}, f32[40,768]{1,0:T(8,128)S(1)}, u32[]{:S(2)}, u32[]{:S(2)}) collective-permute-start(f32[40,768]{1,0:T(8,128)S(1)} %add.190), channel_id=1, source_target_pairs={{0,4},{4,0},{1,5},{5,1},{2,6},{6,2},{3,7},{7,3},{8,12},{12,8},{9,1... | collective-permute-start | bytes 368648 | tf_op jit(solution)/shard_map/ppermute | solution.py:1259
  381.3 12.8 %collective-permute-start.45 = (bf16[192,768]{1,0:T(8,128)(2,1)S(1)}, bf16[192,768]{1,0:T(8,128)(2,1)S(1)}, u32[]{:S(2)}, u32[]{:S(2)}) collective-permute-start(bf16[192,768]{1,0:T(8,128)(2,1)S(1)} %fusion.17), channel_id=1, source_target_pairs={{0,4},{4,0},{1,5},{5,1},{2,6},{6,2},{3,7},{7,3},{8,12},{12,8},{9,1... | collective-permute-start | bytes 884744 | tf_op jit(solution)/shard_map/ppermute | solution.py:1259
  381.9 13.6 %collective-permute-start.44 = (bf16[2,96,576]{2,1,0:T(8,128)(2,1)S(1)}, bf16[2,96,576]{2,1,0:T(8,128)(2,1)S(1)}, u32[]{:S(2)}, u32[]{:S(2)}) collective-permute-start(bf16[2,96,576]{2,1,0:T(8,128)(2,1)S(1)} %fusion.23), channel_id=1, source_target_pairs={{0,4},{4,0},{1,5},{5,1},{2,6},{6,2},{3,7},{7,3},{8,12},{12,8},{9,1... | collective-permute-start | bytes 663560 | tf_op jit(solution)/shard_map/ppermute | solution.py:1259
  387.9 8.0 %collective-permute-start.46 = (bf16[96,960]{1,0:T(8,128)(2,1)S(1)}, bf16[96,960]{1,0:T(8,128)(2,1)S(1)}, u32[]{:S(2)}, u32[]{:S(2)}) collective-permute-start(bf16[96,960]{1,0:T(8,128)(2,1)S(1)} %fusion.26), channel_id=1, source_target_pairs={{0,4},{4,0},{1,5},{5,1},{2,6},{6,2},{3,7},{7,3},{8,12},{12,8},{9,1... | collective-permute-start | bytes 552968 | tf_op jit(solution)/shard_map/ppermute | solution.py:1259
  388.7 13.9 %collective-permute-start.41 = (bf16[256,768]{1,0:T(8,128)(2,1)S(1)}, bf16[256,768]{1,0:T(8,128)(2,1)S(1)}, u32[]{:S(2)}, u32[]{:S(2)}) collective-permute-start(bf16[256,768]{1,0:T(8,128)(2,1)S(1)} %add_convert_fusion.11.refs_0_), channel_id=1, source_target_pairs={{0,1},{1,0},{2,3},{3,2},{4,5},{5,4},{6,7},{7,6},{8,9},{9,8},{10,11... | collective-permute-start | bytes 1179656 | tf_op jit(solution)/shard_map/ppermute | solution.py:1259
  393.2 26.5 %collective-permute-start.42 = (bf16[256,768]{1,0:T(8,128)(2,1)S(1)}, bf16[256,768]{1,0:T(8,128)(2,1)S(1)}, u32[]{:S(2)}, u32[]{:S(2)}) collective-permute-start(bf16[256,768]{1,0:T(8,128)(2,1)S(1)} %add_convert_fusion.11.refs_0_), channel_id=1, source_target_pairs={{0,2},{1,3},{2,0},{3,1},{4,6},{5,7},{6,4},{7,5},{8,10},{9,11},{10,... | collective-permute-start | bytes 1179656 | tf_op jit(solution)/shard_map/ppermute | solution.py:1259
  394.2 33.2 %collective-permute-start.43 = (bf16[256,768]{1,0:T(8,128)(2,1)S(1)}, bf16[256,768]{1,0:T(8,128)(2,1)S(1)}, u32[]{:S(2)}, u32[]{:S(2)}) collective-permute-start(bf16[256,768]{1,0:T(8,128)(2,1)S(1)} %add_convert_fusion.11.refs_0_), channel_id=1, source_target_pairs={{0,3},{1,2},{2,1},{3,0},{4,7},{5,6},{6,5},{7,4},{8,11},{9,10},{10,... | collective-permute-start | bytes 1179656 | tf_op jit(solution)/shard_map/ppermute | solution.py:1259
  402.6 24.7 %copy-start.18 = (bf16[256,768]{1,0:T(8,128)(2,1)}, bf16[256,768]{1,0:T(8,128)(2,1)S(1)}, u32[]{:S(2)}) copy-start(bf16[256,768]{1,0:T(8,128)(2,1)S(1)} %collective-permute-done.41.refs_1_) | copy-start | bytes 1179652
  (29 other events, 197.7 us)
Sparse Core Ops, SparseCore 0:
  41.7 96.9 all-gather.2
  170.2 36.9 all-gather.4
  251.1 45.1 all-reduce.3

commit v4 on v3

--- a/solution.py
+++ b/solution.py
@@ -1404,24 +1404,29 @@
     orders = [[("ctx", 1)] + high, high + [("ctx", 1)]]
 
     dcq, dck, dcv = cross_backward(cross_scalars, cq, ckv, grad_cmix, cross_mix, cross_logs, scale)
-    ffn_came = tie(ffn_came, dcq)
+    enc_keep, enc_send = encoder_grad(dck, dcv, weight_ckv)
+    enc_came = swap(enc_send, "ctx", 1)
+    grad_two = tie(grad_two, enc_send)
+    grad_one, one_grad_low, self_sums, *grad_mixes = before_self(
+        info, grad_two, dcq, weight_cq, sum_one, vectors[1:2], dcv, weight_o
+    )
+    head_grads = grad_mixes[:1] + [swap(grad_mixes[j], "tensor", j) for j in range(1, tensors)]
+    mesh_sizes = (shards, ctxs, tensors)
+    early_sums = jnp.concatenate([feed_sums, self_sums], axis=0)
+    early_sums = early_sums + swap(early_sums, "tensor", 1)
+    ffn_came = tie(ffn_came, one_grad_low)
     ffn_paths = [Path(ffn_near[i], ffn_came[i], order) for i, order in enumerate(orders)]
+    sends = []
     for p in ffn_paths:
         p.fold()
-        grad_two = tie(grad_two, p.send, p.keep)
+        sends += [p.send, p.keep]
         p.go()
-    grad_one, one_grad_low, self_sums, *grad_mixes = before_self(
-        info, grad_two, dcq, weight_cq, sum_one, vectors[1:2], dcv, weight_o
-    )
-    head_grads = grad_mixes[:1] + [swap(grad_mixes[j], "tensor", j) for j in range(1, tensors)]
-    mesh_sizes = (shards, ctxs, tensors)
-    enc_keep, enc_send = encoder_grad(tie(dck, one_grad_low), dcv, weight_ckv)
-    early_sums = jnp.concatenate([feed_sums, self_sums], axis=0)
-    early_sums = early_sums + swap(early_sums, "tensor", 1)
+    enc_mine = (enc_keep + tie(enc_came, *sends).astype(F32)).astype(BF16)
+    grad_encoder = lax.psum(enc_mine, "tensor")
     near_a, near_b, far_a, far_b = square_grads(
         info,
         [
-            (tie(enc_low, enc_send, early_sums), dck),
+            (tie(enc_low, early_sums, enc_mine, result_all), dck),
             (enc_low, dcv),
             (one_grad_low, self_mix),
             (one_low, dcq),
@@ -1430,40 +1435,39 @@
         (2, 3),
         mesh_sizes,
     )
-    enc_send, head_grads, far_a, far_b = tie((enc_send, head_grads, far_a, far_b), far_b)
+    head_grads, far_a, far_b = tie((head_grads, far_a, far_b), far_b)
     for _ in range(len(high)):
         for p in ffn_paths:
             p.came = tie(p.came, far_b)
             p.fold()
             head_grads = tie(head_grads, p.send, p.keep)
             p.go()
-    enc_came = tie(swap(enc_send, "ctx", 1), *(p.keep for p in ffn_paths))
-    enc_mine = (enc_keep + enc_came.astype(F32)).astype(BF16)
-    grad_encoder = lax.psum(enc_mine, "tensor")
-    for bit in bits_of("tensor")[1:]:
-        early_sums = early_sums + tie(swap(early_sums, "tensor", bit), far_b)
-    head_grads = tie(head_grads, enc_mine, result_all, early_sums)
+    sums_came = [swap(early_sums, "tensor", bit) for bit in bits_of("tensor")[1:2]]
 
     dq, down, dtrunk, late_sums = self_backward(
         scalars, q, kv, kv_sent, head_grads, mixes, self_logs, heads, seg, scale, width
     )
     trunk_came = lax.ppermute(dtrunk, "ctx", [(1, 0)])
-    for p in ffn_paths:
-        p.came = tie(p.came, dtrunk, grad_encoder)
-        p.fold()
-    ffn_blocks = jnp.concatenate([p.keep for p in ffn_paths], axis=1)
-    ffn_came = [swap(ffn_blocks[j], "tensor", j) for j in range(1, tensors)]
-    sums = jnp.concatenate([early_sums, late_sums], axis=0)
-    for axis, bit in [("shard", 1)] + shard_bits:
-        sums = sums + swap(sums, axis, bit)
     paths = [
-        Path(near, tie(swap(far, "shard", 1), ffn_blocks), order)
+        Path(near, tie(swap(far, "shard", 1), dtrunk), order)
         for near, far, order in zip((near_a, near_b), (far_a, far_b), orders)
     ]
     for p in paths:
         p.fold()
         trunk_came = tie(trunk_came, p.send, p.keep)
         p.go()
+    for p in ffn_paths:
+        p.came = tie(p.came, dtrunk, grad_encoder, *(q.keep for q in paths))
+        p.fold()
+    ffn_blocks = jnp.concatenate([p.keep for p in ffn_paths], axis=1)
+    ffn_came = [swap(ffn_blocks[j], "tensor", j) for j in range(1, tensors)]
+    for came in tie(sums_came, dtrunk):
+        early_sums = early_sums + came
+    for bit in bits_of("tensor")[2:]:
+        early_sums = early_sums + swap(early_sums, "tensor", bit)
+    sums = jnp.concatenate([early_sums, late_sums], axis=0)
+    for axis, bit in [("shard", 1)] + shard_bits:
+        sums = sums + swap(sums, axis, bit)
     trunk_came = tie(trunk_came, ffn_blocks, sums)
     *parts, near, far = input_grad(
         info, dq, down, dtrunk, trunk_came, input_low, qkv_weights, mesh_sizes
@@ -1527,8 +1531,8 @@
     grad_ck, grad_cv, grad_o, grad_cq, grad_co = (
         squares[:, i * columns : (i + 1) * columns] for i in range(5)
     )
-    grad_encoder = tie(grad_encoder, input_mine).astype(F32)
-    result_all = tie(result_all, input_mine).astype(F32)
+    grad_encoder = tie(grad_encoder, input_all[1]).astype(F32)
+    result_all = tie(result_all, input_all[1]).astype(F32)
     input_all = input_all[:1] + list(tie(input_all[1:], sums, qkv_grads, grad_up, squares))
     grad_input = lay_rows(info, input_all)
     me_tensor = info[2]

time: 440 us -> 418 us (0.950)
  waiting for transfers between devices: 144 us -> 112 us
  starting transfers between devices: 65.4 us -> 74.8 us
    psum x1, waiting for transfers between devices: 20.3 us -> 0.01 us  [local(): grad_encoder = lax.psum(enc_mine, 'tensor')]
    ppermute x46, waiting for transfers between devices: 109 us -> 95.5 us  [swap(): return lax.ppermute(a, axis, [(i, i ^ bit) for i in range(sizes[axis])])]
    ppermute x46, starting transfers between devices: 60.5 us -> 69.9 us  [swap(): return lax.ppermute(a, axis, [(i, i ^ bit) for i in range(sizes[axis])])]
  transfers between devices with their start and end apart: 51 -> 51, of which waited for: 21 -> 19; matrix products, arithmetic and copies ran while one was open for 10% -> 11% of each run, Pallas kernels for 28% -> 30%
where the time goes in v4:
time: 418 us; the launch traced here: 417 us
  Pallas kernels  153 us (37%)
  waiting for transfers between devices  112 us (27%)
  starting transfers between devices  74.8 us (18%)
  other arithmetic  38.9 us (9%)
  between operations  15.4 us (4%)
  local copies, waits for them, and re-layouts  12.8 us (3%)
  blocking collectives  10.1 us (2%)
    ppermute x46, waiting for transfers between devices, swap(): return lax.ppermute(a, axis, [(i, i ^ bit) for i in range(sizes[axis])])  95.5 us
    ppermute x46, starting transfers between devices, swap(): return lax.ppermute(a, axis, [(i, i ^ bit) for i in range(sizes[axis])])  69.9 us
    pallas_call x1, Pallas kernels, feed(): pl.pallas_call(feed_kernel, grid_spec=pltpu.PrefetchScalarGridSpec(num_sc...  23.4 us
    convert_element_type x13, other arithmetic, add(): return (a.astype(F32) + b.astype(F32)).astype(BF16)  19.7 us
    pallas_call x1, Pallas kernels, cross_forward(): pl.pallas_call(cross_forward_kernel, grid_spec=pltpu.PrefetchScalarGridSp...  17.9 us
    pallas_call x1, Pallas kernels, self_backward(): pl.pallas_call(functools.partial(self_backward_kernel, heads=heads, seg=s...  16.5 us
    pallas_call x1, Pallas kernels, cross_backward(): pl.pallas_call(functools.partial(cross_backward_kernel, scale=scale), gri...  16.4 us
    pallas_call x1, Pallas kernels, self_forward(): pl.pallas_call(functools.partial(self_forward_kernel, heads=heads, seg=se...  14.8 us
  transfers between devices with their start and end apart: 51, of which 19 were waited for; matrix products, arithmetic and copies ran while one was open for 11% of the time, Pallas kernels for 30%

profile of v4, /device:TPU:8, one launch (start us, length us, event | category | flops | bytes accessed | tf_op | source)
XLA Modules:
  0.0 416.6 jit_solution(1212404973497108181)
XLA Ops:
  10.4 3.0 collective-permute-start.1
  14.9 10.1 %all_gather.9.w_ref = bf16[768,576]{1,0:T(8,128)(2,1)} all-gather(bf16[192,576]{1,0:T(8,128)(2,1)S(1)} %pad_maximum_fusion.5), channel_id=1, replica_groups=mesh['shard'=4,'ctx'=2,'tensor'=4] {'shard'}, dimensions={0}, use_global_device_ids=true | all-gather | bytes 1105920 | tf_op jit(solution)/shard_map/all_gather | solution.py:1330
  25.2 5.5 %project.1 = (bf16[1024,192]{1,0:T(8,128)(2,1)}, bf16[1024,384]{1,0:T(8,128)(2,1)}, bf16[1024,768]{1,0:T(8,128)(2,1)}) custom-call(f32[1,1024,768]{2,1,0:T(8,128)} %x_ref.3, bf16[768,576]{1,0:T(8,128)(2,1)} %all_gather.9.w_ref, f32[1,192]{1,0:T(1,128)} %bitcast.162, f32[1,192]{1,0:T(1,128)} %bitcast.163), custom_call_target="tpu_custom_call" | custom-call | flops 9059696 | bytes 62914 | tf_op jit(solution)/shard_map/project/pallas_call | solution.py:591
  31.6 3.4 collective-permute-done.1
  35.0 6.3 %collective-permute-done.2 = bf16[208,768]{1,0:T(8,128)(2,1)S(1)} collective-permute-done((bf16[208,768]{1,0:T(8,128)(2,1)S(1)}, bf16[208,768]{1,0:T(8,128)(2,1)S(1)}, u32[]{:S(2)}, u32[]{:S(2)}) %collective-permute-start.2) | collective-permute-done | bytes 319520 | tf_op jit(solution)/shard_map/ppermute | solution.py:1259
  41.6 1.6 collective-permute-start.3
  43.2 3.5 collective-permute-start.4
  47.3 14.7 %collective-permute-done.4.sent_ref = bf16[1024,384]{1,0:T(8,128)(2,1)S(1)} collective-permute-done((bf16[1024,384]{1,0:T(8,128)(2,1)S(1)}, bf16[1024,384]{1,0:T(8,128)(2,1)S(1)}, u32[]{:S(2)}, u32[]{:S(2)}) %collective-permute-start.4) | collective-permute-done | bytes 786464 | tf_op jit(solution)/shard_map/ppermute | solution.py:1338
  62.8 14.8 %self_forward.1 = (bf16[256,192]{1,0:T(8,128)(2,1)}, bf16[256,192]{1,0:T(8,128)(2,1)}, bf16[256,192]{1,0:T(8,128)(2,1)}, bf16[256,192]{1,0:T(8,128)(2,1)}, f32[8,1024]{1,0:T(8,128)}) custom-call(s32[3]{0:T(128)} %pad_add_fusion.info_ref, s32[16]{0:T(128)} %bitcast.160, s32[2048]{0:T(1024)} %bitcast.158, bf16[1024,192]{1,0:T(8,128)(2,1)} %get-tuple-element.144.q_ref, ...), custom_call_target="tpu_custom_call" | custom-call | flops 16106127 | bytes 31457 | tf_op jit(solution)/shard_map/self_forward/pallas_call | solution.py:256
  77.7 2.0 pad_maximum_fusion.near_ref
  81.0 12.4 %collective-permute-start.9 = (bf16[512,768]{1,0:T(8,128)(2,1)}, bf16[512,768]{1,0:T(8,128)(2,1)S(1)}, u32[]{:S(2)}, u32[]{:S(2)}) collective-permute-start(bf16[512,768]{1,0:T(8,128)(2,1)} %convert_bitcast_fusion), channel_id=1, source_target_pairs={{0,4},{4,0},{1,5},{5,1},{2,6},{6,2},{3,7},{7,3},{8,12},{12,8},{9,1... | collective-permute-start | bytes 2359304 | tf_op jit(solution)/shard_map/ppermute | solution.py:1259
  93.4 3.0 collective-permute-start.7
  97.7 1.3 stack.87.vectors_ref
  99.0 6.9 %assemble.1 = (bf16[768,1536]{1,0:T(8,128)(2,1)}, bf16[4,768,192]{2,1,0:T(8,128)(2,1)}, bf16[768,768]{1,0:T(8,128)(2,1)}, bf16[4,16,768]{2,1,0:T(8,128)(2,1)}) custom-call(s32[3]{0:T(128)} %pad_add_fusion.info_ref, bf16[2,4,208,768]{3,2,1,0:T(8,128)(2,1)} %copy-done, bf16[2,4,208,768]{3,2,1,0:T(8,128)(2,1)} %collective-permute-done.5.far_ref), custom_call_target="tpu_custom_call" | custom-call | bytes 102236 | tf_op jit(solution)/shard_map/assemble/pallas_call | solution.py:649
  106.0 5.8 %collective-permute-done.9.sent_ref = bf16[512,768]{1,0:T(8,128)(2,1)S(1)} collective-permute-done((bf16[512,768]{1,0:T(8,128)(2,1)}, bf16[512,768]{1,0:T(8,128)(2,1)S(1)}, u32[]{:S(2)}, u32[]{:S(2)}) %collective-permute-start.9) | collective-permute-done | bytes 786464 | tf_op jit(solution)/shard_map/ppermute | solution.py:1259
  112.7 7.4 %encode.1 = (bf16[1024,768]{1,0:T(8,128)(2,1)}, bf16[1024,1536]{1,0:T(8,128)(2,1)}) custom-call(s32[3]{0:T(128)} %pad_add_fusion.info_ref, f32[1,512,768]{2,1,0:T(8,128)} %own_ref.1, bf16[512,768]{1,0:T(8,128)(2,1)} %copy-done.13, bf16[768,1536]{1,0:T(8,128)(2,1)} %get-tuple-element.162.w_ref, bf16[4,16,768]{2,1,0:T(8,128)(2,1)} %get-tuple-element.157.bias_ref), custom_call_target="tpu_custom_call" | custom-call | flops 24159192 | bytes 55050 | tf_op jit(solution)/shard_map/encode/pallas_call | solution.py:749
  120.1 3.6 collective-permute-done.8.rest_3_
  123.7 5.1 %after_self.1 = (f32[256,768]{1,0:T(8,128)}, bf16[256,768]{1,0:T(8,128)(2,1)}, bf16[256,768]{1,0:T(8,128)(2,1)}, bf16[256,768]{1,0:T(8,128)(2,1)}) custom-call(s32[3]{0:T(128)} %pad_add_fusion.info_ref, f32[1,1024,768]{2,1,0:T(8,128)} %x_ref.3, bf16[4,768,192]{2,1,0:T(8,128)(2,1)} %get-tuple-element.155.o_ref, bf16[768,768]{1,0:T(8,128)(2,1)} %get-tuple-element.156.cq_ref, ...), custom_call_target="tpu_custom_call" | custom-call | flops 6039797 | bytes 47185 | tf_op jit(solution)/shard_map/after_self/pallas_call | solution.py:711
  128.8 17.9 %cross_forward.1 = (bf16[256,768]{1,0:T(8,128)(2,1)}, f32[48,256]{1,0:T(8,128)}) custom-call(s32[3]{0:T(128)} %pad_add_fusion.info_ref, s32[1]{0:T(128)S(6)} %copy.63.length_ref, bf16[256,768]{1,0:T(8,128)(2,1)} %get-tuple-element.168.q_ref, bf16[1024,1536]{1,0:T(8,128)(2,1)} %get-tuple-element.163.k_ref.v_ref, bf16[1024,1536]{1,0:T(8,128)(2,1)} %get-tuple-element.163.k_ref.v_ref), custom_call_target="tpu_custom_call" | custom-call | flops 16106127 | bytes 39321 | tf_op jit(solution)/shard_map/cross_forward/pallas_call | solution.py:481
  146.7 23.4 %feed.1 = (bf16[256,768]{1,0:T(8,128)(2,1)}, bf16[2,2,2,4,96,768]{5,4,3,2,1,0:T(8,128)(2,1)}, bf16[2,2,2,4,96,768]{5,4,3,2,1,0:T(8,128)(2,1)}, f32[256,768]{1,0:...) custom-call(s32[3]{0:T(128)} %pad_add_fusion.info_ref, ...), custom_call_target="tpu_custom_call" | custom-call | flops 81537272 | bytes 318504 | tf_op jit(solution)/shard_map/feed/pallas_call | solution.py:917
  170.3 16.4 %cross_backward.1 = (bf16[256,768]{1,0:T(8,128)(2,1)}, bf16[1024,768]{1,0:T(8,128)(2,1)}, bf16[1024,768]{1,0:T(8,128)(2,1)}) custom-call(s32[3]{0:T(128)} %pad_add_fusion.info_ref, s32[1]{0:T(128)S(6)} %copy.63.length_ref, bf16[256,768]{1,0:T(8,128)(2,1)} %get-tuple-element.168.q_ref, bf16[1024,1536]{1,0:T(8,128)(2,1)} %get-tuple-element.163.k_ref.v_ref, ...), custom_call_target="tpu_custom_call" | custom-call | flops 40265320 | bytes 78643 | tf_op jit(solution)/shard_map/cross_backward/pallas_call | solution.py:536
  186.8 6.9 %encoder_grad.1 = (f32[512,768]{1,0:T(8,128)}, bf16[512,768]{1,0:T(8,128)(2,1)}) custom-call(bf16[1024,768]{1,0:T(8,128)(2,1)} %get-tuple-element.175.dk_ref.refs_5_, bf16[1024,768]{1,0:T(8,128)(2,1)} %get-tuple-element.176.dv_ref.refs_6_, bf16[768,1536]{1,0:T(8,128)(2,1)} %get-tuple-element.162.w_ref), custom_call_target="tpu_custom_call" | custom-call | flops 24159192 | bytes 78643 | tf_op jit(solution)/shard_map/encoder_grad/pallas_call | solution.py:1037
  194.2 6.1 %before_self.1 = (f32[256,768]{1,0:T(8,128)}, bf16[256,768]{1,0:T(8,128)(2,1)}, f32[16,768]{1,0:T(8,128)}, bf16[256,192]{1,0:T(8,128)(2,1)}, bf16[256,192]{1,0:T...) custom-call(s32[3]{0:T(128)} %pad_add_fusion.info_ref, f32[256,768]{1,0:T(8,128)} %get-tuple-element.178.grad_ref, ...), custom_call_target="tpu_custom_call" | custom-call | flops 6039797 | bytes 62914 | tf_op jit(solution)/shard_map/before_self/pallas_call | solution.py:997
  200.4 1.8 slice_bitcast_fusion
  202.3 3.3 add_convert_fusion
  206.8 1.8 add_convert_fusion.1
  208.6 1.7 collective-permute-start.16
  210.4 2.0 collective-permute-start.10
  212.4 3.7 collective-permute-done.13
  218.6 2.2 add_convert_fusion.6
  220.8 12.8 %square_grads.1 = (bf16[2,2,4,96,384]{4,3,2,1,0:T(8,128)(2,1)}, bf16[2,2,4,96,576]{4,3,2,1,0:T(8,128)(2,1)}, bf16[2,2,4,96,384]{4,3,2,1,0:T(8,128)(2,1)}, bf16[2,2,4,96,576]{4,3,2,1,0:T(8,128)(2,1)}) custom-call(s32[3]{0:T(128)} %pad_add_fusion.info_ref, bf16[1024,768]{1,0:T(8,128)(2,1)} %get-tuple-element.194.refs_0_.refs_1_, ...), custom_call_target="tpu_custom_call" | custom-call | flops 66437776 | bytes 47185 | tf_op jit(solution)/shard_map/square_grads/pallas_call | solution.py:1108
  234.3 3.8 collective-permute-start.23
  239.2 2.4 fusion.12
  241.7 1.3 collective-permute-start.21
  243.8 16.5 %self_backward.1 = (bf16[1024,192]{1,0:T(8,128)(2,1)}, f32[1024,384]{1,0:T(8,128)}, bf16[1024,384]{1,0:T(8,128)(2,1)}, f32[8,768]{1,0:T(8,128)}) custom-call(s32[3]{0:T(128)} %pad_add_fusion.info_ref, s32[16]{0:T(128)} %bitcast.161, s32[2048]{0:T(1024)} %bitcast.159, bf16[1024,192]{1,0:T(8,128)(2,1)} %get-tuple-element.144.q_ref, ...), custom_call_target="tpu_custom_call" | custom-call | flops 40265320 | bytes 78643 | tf_op jit(solution)/shard_map/self_backward/pallas_call | solution.py:412
  260.3 1.3 collective-permute-start.18
  263.4 2.7 add_convert_fusion.9
  266.2 11.5 %collective-permute-start.29 = (bf16[2,4,96,384]{3,2,1,0:T(8,128)(2,1)}, bf16[2,4,96,384]{3,2,1,0:T(8,128)(2,1)}, u32[]{:S(2)}, u32[]{:S(2)}) collective-permute-start(bf16[2,4,96,384]{3,2,1,0:T(8,128)(2,1)} %get-tuple-element.305), channel_id=1, source_target_pairs={{0,4},{4,0},{1,5},{5,1},{2,6},{6,2},{3,7},{7,3},{8,12},{12,8},{9,1... | collective-permute-start | bytes 1769480 | tf_op jit(solution)/shard_map/ppermute | solution.py:1259
  278.5 2.9 add_convert_fusion.4
  282.2 1.4 collective-permute-start.31
  283.6 1.5 add_convert_fusion.7
  286.0 3.3 collective-permute-start.39
  289.3 1.7 collective-permute-done.18.came_ref
  291.0 1.9 collective-permute-start.40
  293.8 8.8 %input_grad.1 = (f32[256,768]{1,0:T(8,128)}, bf16[256,768]{1,0:T(8,128)(2,1)}, bf16[256,768]{1,0:T(8,128)(2,1)}, bf16[256,768]{1,0:T(8,128)(2,1)}, bf16[2,2,96,5...) custom-call(s32[3]{0:T(128)} %pad_add_fusion.info_ref, bf16[1024,192]{1,0:T(8,128)(2,1)} %get-tuple-element.215.dq_ref, ...), custom_call_target="tpu_custom_call" | custom-call | flops 18119392 | bytes 110100 | tf_op jit(solution)/shard_map/input_grad/pallas_call | solution.py:1164
  304.4 5.4 %collective-permute-done.39 = bf16[192,768]{1,0:T(8,128)(2,1)S(1)} collective-permute-done((bf16[192,768]{1,0:T(8,128)(2,1)}, bf16[192,768]{1,0:T(8,128)(2,1)S(1)}, u32[]{:S(2)}, u32[]{:S(2)}) %collective-permute-start.39) | collective-permute-done | bytes 294944 | tf_op jit(solution)/shard_map/ppermute | solution.py:1259
  309.8 2.0 collective-permute-start.26
  311.8 3.2 collective-permute-done.40
  315.2 2.1 collective-permute-start.28
  320.4 9.2 %collective-permute-done.32 = bf16[4,96,576]{2,1,0:T(8,128)(2,1)S(1)} collective-permute-done((bf16[4,96,576]{2,1,0:T(8,128)(2,1)S(1)}, bf16[4,96,576]{2,1,0:T(8,128)(2,1)S(1)}, u32[]{:S(2)}, u32[]{:S(2)}) %collective-permute-start.32) | collective-permute-done | bytes 442400 | tf_op jit(solution)/shard_map/ppermute | solution.py:1259
  330.9 2.4 collective-permute-start.33
  333.3 1.3 collective-permute-start.34
  335.3 14.9 %collective-permute-done.27 = bf16[256,768]{1,0:T(8,128)(2,1)S(1)} collective-permute-done((bf16[256,768]{1,0:T(8,128)(2,1)}, bf16[256,768]{1,0:T(8,128)(2,1)S(1)}, u32[]{:S(2)}, u32[]{:S(2)}) %collective-permute-start.27) | collective-permute-done | bytes 393248 | tf_op jit(solution)/shard_map/ppermute | solution.py:1259
  350.5 9.7 %collective-permute-done.28 = bf16[256,768]{1,0:T(8,128)(2,1)S(1)} collective-permute-done((bf16[256,768]{1,0:T(8,128)(2,1)S(1)}, bf16[256,768]{1,0:T(8,128)(2,1)S(1)}, u32[]{:S(2)}, u32[]{:S(2)}) %collective-permute-start.28) | collective-permute-done | bytes 393248 | tf_op jit(solution)/shard_map/ppermute | solution.py:1259
  360.6 1.7 collective-permute-start.44
  362.7 4.2 %collective-permute-done.35 = bf16[96,960]{1,0:T(8,128)(2,1)S(1)} collective-permute-done((bf16[96,960]{1,0:T(8,128)(2,1)S(1)}, bf16[96,960]{1,0:T(8,128)(2,1)S(1)}, u32[]{:S(2)}, u32[]{:S(2)}) %collective-permute-start.35) | collective-permute-done | bytes 184352 | tf_op jit(solution)/shard_map/ppermute | solution.py:1259
  368.0 1.7 collective-permute-start.42
  369.8 1.8 collective-permute-start.43
  371.5 1.7 collective-permute-done.44
  373.2 2.1 collective-permute-done.46
  383.4 12.8 %collective-permute-done.42.refs_2_ = bf16[256,768]{1,0:T(8,128)(2,1)S(1)} collective-permute-done((bf16[256,768]{1,0:T(8,128)(2,1)S(1)}, bf16[256,768]{1,0:T(8,128)(2,1)S(1)}, u32[]{:S(2)}, u32[]{:S(2)}) %collective-permute-start.42) | collective-permute-done | bytes 393248 | tf_op jit(solution)/shard_map/ppermute | solution.py:1259
  396.2 7.7 %collective-permute-done.43.refs_3_ = bf16[256,768]{1,0:T(8,128)(2,1)S(1)} collective-permute-done((bf16[256,768]{1,0:T(8,128)(2,1)S(1)}, bf16[256,768]{1,0:T(8,128)(2,1)S(1)}, u32[]{:S(2)}, u32[]{:S(2)}) %collective-permute-start.43) | collective-permute-done | bytes 393248 | tf_op jit(solution)/shard_map/ppermute | solution.py:1259
  403.9 1.9 bitcast_convert_fusion
  405.8 4.2 %lay_rows.1 = f32[1024,768]{1,0:T(8,128)} custom-call(s32[3]{0:T(128)} %pad_add_fusion.info_ref, bf16[256,768]{1,0:T(8,128)(2,1)} %copy-done.7, bf16[256,768]{1,0:T(8,128)(2,1)} %copy-done.19, bf16[256,768]{1,0:T(8,128)(2,1)} %copy-done.20, bf16[256,768]{1,0:T(8,128)(2,1)} %copy-done.21), custom_call_target="tpu_custom_call" | custom-call | bytes 47185 | tf_op jit(solution)/shard_map/lay_rows/pallas_call | solution.py:1197
  (216 shorter events, 39.6 us)
Async XLA Ops:
  7.2 139.5 %all-gather.3.cloned.1.call-start = ((), (), s32[]{:S(2)}) async-start(), calls=%async_computation | async-start | bytes 11280384 | tf_op jit(solution)/shard_map/all_gather | solution.py:1337
  10.3 21.3 %collective-permute-start = (bf16[208,768]{1,0:T(8,128)(2,1)S(1)}, bf16[208,768]{1,0:T(8,128)(2,1)S(1)}, u32[]{:S(2)}, u32[]{:S(2)}) collective-permute-start(bf16[208,768]{1,0:T(8,128)(2,1)S(1)} %pad_maximum_fusion.4), channel_id=1, source_target_pairs={{0,1},{1,0},{2,3},{3,2},{4,5},{5,4},{6,7},{7,6},{8,9},{9,8},{10,11... | collective-permute-start | bytes 958472 | tf_op jit(solution)/shard_map/ppermute | solution.py:1259
  10.4 24.7 %collective-permute-start.1 = (bf16[208,768]{1,0:T(8,128)(2,1)S(1)}, bf16[208,768]{1,0:T(8,128)(2,1)S(1)}, u32[]{:S(2)}, u32[]{:S(2)}) collective-permute-start(bf16[208,768]{1,0:T(8,128)(2,1)S(1)} %pad_maximum_fusion.4), channel_id=1, source_target_pairs={{0,2},{1,3},{2,0},{3,1},{4,6},{5,7},{6,4},{7,5},{8,10},{9,11},{10,... | collective-permute-start | bytes 958472 | tf_op jit(solution)/shard_map/ppermute | solution.py:1259
  13.4 28.0 %collective-permute-start.2 = (bf16[208,768]{1,0:T(8,128)(2,1)S(1)}, bf16[208,768]{1,0:T(8,128)(2,1)S(1)}, u32[]{:S(2)}, u32[]{:S(2)}) collective-permute-start(bf16[208,768]{1,0:T(8,128)(2,1)S(1)} %pad_maximum_fusion.4), channel_id=1, source_target_pairs={{0,3},{1,2},{2,1},{3,0},{4,7},{5,6},{6,5},{7,4},{8,11},{9,10},{10,... | collective-permute-start | bytes 958472 | tf_op jit(solution)/shard_map/ppermute | solution.py:1259
  41.6 36.1 %copy-start.2 = (bf16[4,208,768]{2,1,0:T(8,128)(2,1)}, bf16[4,208,768]{2,1,0:T(8,128)(2,1)S(1)}, u32[]{:S(2)}) copy-start(bf16[4,208,768]{2,1,0:T(8,128)(2,1)S(1)} %pad_maximum_fusion.2) | copy-start | bytes 3833860
  41.6 179.3 %all-gather.5.cloned.1.call-start = ((), (), s32[]{:S(2)}) async-start(), calls=%async_computation.1 | async-start | bytes 1966080 | tf_op jit(solution)/shard_map/all_gather | solution.py:1379
  41.6 36.1 %collective-permute-start.3 = (bf16[4,208,768]{2,1,0:T(8,128)(2,1)S(1)}, bf16[4,208,768]{2,1,0:T(8,128)(2,1)}, u32[]{:S(2)}, u32[]{:S(2)}) collective-permute-start(bf16[4,208,768]{2,1,0:T(8,128)(2,1)S(1)} %pad_maximum_fusion.2), channel_id=1, source_target_pairs={{0,16},{8,24},{16,0},{24,8},{1,17},{9,25},{17,1},{25,9},{2,18},{10... | collective-permute-start | bytes 3833864 | tf_op jit(solution)/shard_map/ppermute | solution.py:1259
  43.2 18.8 %collective-permute-start.4 = (bf16[1024,384]{1,0:T(8,128)(2,1)S(1)}, bf16[1024,384]{1,0:T(8,128)(2,1)S(1)}, u32[]{:S(2)}, u32[]{:S(2)}) collective-permute-start(bf16[1024,384]{1,0:T(8,128)(2,1)S(1)} %copy-done.3), channel_id=1, source_target_pairs={{0,4},{1,5},{2,6},{3,7},{8,12},{9,13},{10,14},{11,15},{16,20},{17,... | collective-permute-start | bytes 2359304 | tf_op jit(solution)/shard_map/ppermute | solution.py:1338
  79.8 19.2 %copy-start = (bf16[2,4,208,768]{3,2,1,0:T(8,128)(2,1)}, bf16[2,4,208,768]{3,2,1,0:T(8,128)(2,1)S(1)}, u32[]{:S(2)}) copy-start(bf16[2,4,208,768]{3,2,1,0:T(8,128)(2,1)S(1)} %pad_maximum_fusion.near_ref) | copy-start | bytes 7667716
  79.8 17.8 %copy-start.36 = (f32[768]{0:T(1024)S(1)}, f32[768]{0:T(1024)}, u32[]{:S(2)}) copy-start(f32[768]{0:T(1024)} %param.55) | copy-start | bytes 9220
  79.9 17.8 %copy-start.37 = (f32[768]{0:T(1024)S(1)}, f32[768]{0:T(1024)}, u32[]{:S(2)}) copy-start(f32[768]{0:T(1024)} %param.56) | copy-start | bytes 9220
  79.9 17.8 %copy-start.38 = (f32[768]{0:T(1024)S(1)}, f32[768]{0:T(1024)}, u32[]{:S(2)}) copy-start(f32[768]{0:T(1024)} %param.52) | copy-start | bytes 9220
  79.9 17.8 %copy-start.39 = (f32[768]{0:T(1024)S(1)}, f32[768]{0:T(1024)}, u32[]{:S(2)}) copy-start(f32[768]{0:T(1024)} %param.57) | copy-start | bytes 9220
  79.9 17.8 %copy-start.40 = (f32[768]{0:T(1024)S(1)}, f32[768]{0:T(1024)}, u32[]{:S(2)}) copy-start(f32[768]{0:T(1024)} %param.58) | copy-start | bytes 9220
  79.9 19.1 %collective-permute-start.5 = (bf16[2,4,208,768]{3,2,1,0:T(8,128)(2,1)S(1)}, bf16[2,4,208,768]{3,2,1,0:T(8,128)(2,1)}, u32[]{:S(2)}, u32[]{:S(2)}) collective-permute-start(bf16[2,4,208,768]{3,2,1,0:T(8,128)(2,1)S(1)} %pad_maximum_fusion.near_ref), channel_id=1, source_target_pairs={{0,8},{8,0},{16,24},{24,16},{1,9},{9,1},{17,25},{25,17},{2,10},{10... | collective-permute-start | bytes 7667720 | tf_op jit(solution)/shard_map/ppermute | solution.py:1259
  81.0 30.8 %collective-permute-start.9 = (bf16[512,768]{1,0:T(8,128)(2,1)}, bf16[512,768]{1,0:T(8,128)(2,1)S(1)}, u32[]{:S(2)}, u32[]{:S(2)}) collective-permute-start(bf16[512,768]{1,0:T(8,128)(2,1)} %convert_bitcast_fusion), channel_id=1, source_target_pairs={{0,4},{4,0},{1,5},{5,1},{2,6},{6,2},{3,7},{7,3},{8,12},{12,8},{9,1... | collective-permute-start | bytes 2359304 | tf_op jit(solution)/shard_map/ppermute | solution.py:1259
  93.4 26.7 %collective-permute-start.6 = (bf16[256,192]{1,0:T(8,128)(2,1)S(1)}, bf16[256,192]{1,0:T(8,128)(2,1)}, u32[]{:S(2)}, u32[]{:S(2)}) collective-permute-start(bf16[256,192]{1,0:T(8,128)(2,1)S(1)} %copy-done.24), channel_id=1, source_target_pairs={{0,1},{1,0},{2,3},{3,2},{4,5},{5,4},{6,7},{7,6},{8,9},{9,8},{10,11... | collective-permute-start | bytes 294920 | tf_op jit(solution)/shard_map/ppermute | solution.py:1259
  93.4 26.7 %collective-permute-start.7 = (bf16[256,192]{1,0:T(8,128)(2,1)}, bf16[256,192]{1,0:T(8,128)(2,1)}, u32[]{:S(2)}, u32[]{:S(2)}) collective-permute-start(bf16[256,192]{1,0:T(8,128)(2,1)} %get-tuple-element.160.rest_6_), channel_id=1, source_target_pairs={{0,2},{1,3},{2,0},{3,1},{4,6},{5,7},{6,4},{7,5},{8,10},{9,11},{10,... | collective-permute-start | bytes 294920 | tf_op jit(solution)/shard_map/ppermute | solution.py:1259
  96.3 27.4 %collective-permute-start.8 = (bf16[256,192]{1,0:T(8,128)(2,1)}, bf16[256,192]{1,0:T(8,128)(2,1)}, u32[]{:S(2)}, u32[]{:S(2)}) collective-permute-start(bf16[256,192]{1,0:T(8,128)(2,1)} %get-tuple-element.161.rest_7_), channel_id=1, source_target_pairs={{0,3},{1,2},{2,1},{3,0},{4,7},{5,6},{6,5},{7,4},{8,11},{9,10},{10,... | collective-permute-start | bytes 294920 | tf_op jit(solution)/shard_map/ppermute | solution.py:1259
  170.1 30.3 %collective-permute-start.15 = (bf16[2,2,2,4,96,768]{5,4,3,2,1,0:T(8,128)(2,1)}, bf16[2,2,2,4,96,768]{5,4,3,2,1,0:T(8,128)(2,1)}, u32[]{:S(2)}, u32[]{:S(2)}) collective-permute-start(bf16[2,2,2,4,96,768]{5,4,3,2,1,0:T(8,128)(2,1)} %get-tuple-element.190), channel_id=1, source_target_pairs={{0,8},{8,0},{16,24},{24,16},{1,9},{9,1},{17,25},{25,17},{2,10},{10... | collective-permute-start | bytes 14155784 | tf_op jit(solution)/shard_map/ppermute | solution.py:1259
  170.3 111.1 %all-reduce.4.cloned.1.call-start = ((), (), s32[]{:S(2)}) async-start(), calls=%async_computation.2 | async-start | bytes 1572864 | tf_op jit(solution)/shard_map/psum | solution.py:1425
  170.3 29.9 %slice-start = ((s8[4718592]{0:T(1024)(128)(4,1)}), s8[4194304]{0:T(1024)(128)(4,1)S(1)}, s32[]{:S(2)}) async-start(s8[4718592]{0:T(1024)(128)(4,1)} %bitcast.148), calls=%async_computation.3 | async-start | bytes 8388608
  193.7 23.9 %collective-permute-start.14 = (bf16[512,768]{1,0:T(8,128)(2,1)}, bf16[512,768]{1,0:T(8,128)(2,1)}, u32[]{:S(2)}, u32[]{:S(2)}) collective-permute-start(bf16[512,768]{1,0:T(8,128)(2,1)} %get-tuple-element.177), channel_id=1, source_target_pairs={{0,4},{4,0},{1,5},{5,1},{2,6},{6,2},{3,7},{7,3},{8,12},{12,8},{9,1... | collective-permute-start | bytes 2359304 | tf_op jit(solution)/shard_map/ppermute | solution.py:1259
  205.6 32.5 %collective-permute-start.17 = (bf16[2,4,96,768]{3,2,1,0:T(8,128)(2,1)}, bf16[2,4,96,768]{3,2,1,0:T(8,128)(2,1)S(1)}, u32[]{:S(2)}, u32[]{:S(2)}) collective-permute-start(bf16[2,4,96,768]{3,2,1,0:T(8,128)(2,1)} %get-tuple-element.299), channel_id=1, source_target_pairs={{0,16},{8,24},{16,0},{24,8},{1,17},{9,25},{17,1},{25,9},{2,18},{10... | collective-permute-start | bytes 3538952 | tf_op jit(solution)/shard_map/ppermute | solution.py:1259
  208.6 30.6 %collective-permute-start.16 = (bf16[2,4,96,768]{3,2,1,0:T(8,128)(2,1)}, bf16[2,4,96,768]{3,2,1,0:T(8,128)(2,1)}, u32[]{:S(2)}, u32[]{:S(2)}) collective-permute-start(bf16[2,4,96,768]{3,2,1,0:T(8,128)(2,1)} %get-tuple-element.301), channel_id=1, source_target_pairs={{0,4},{4,0},{1,5},{5,1},{2,6},{6,2},{3,7},{7,3},{8,12},{12,8},{9,1... | collective-permute-start | bytes 3538952 | tf_op jit(solution)/shard_map/ppermute | solution.py:1259
  210.3 5.8 %collective-permute-start.13 = (f32[32,768]{1,0:T(8,128)S(1)}, f32[32,768]{1,0:T(8,128)S(1)}, u32[]{:S(2)}, u32[]{:S(2)}) collective-permute-start(f32[32,768]{1,0:T(8,128)S(1)} %constant_dynamic-update-slice_fusion), channel_id=1, source_target_pairs={{0,1},{1,0},{2,3},{3,2},{4,5},{5,4},{6,7},{7,6},{8,9},{9,8},{10,11... | collective-permute-start | bytes 294920 | tf_op jit(solution)/shard_map/ppermute | solution.py:1259
  210.4 23.3 %collective-permute-start.10 = (bf16[256,192]{1,0:T(8,128)(2,1)}, bf16[256,192]{1,0:T(8,128)(2,1)}, u32[]{:S(2)}, u32[]{:S(2)}) collective-permute-start(bf16[256,192]{1,0:T(8,128)(2,1)} %get-tuple-element.182), channel_id=1, source_target_pairs={{0,1},{1,0},{2,3},{3,2},{4,5},{5,4},{6,7},{7,6},{8,9},{9,8},{10,11... | collective-permute-start | bytes 294920 | tf_op jit(solution)/shard_map/ppermute | solution.py:1259
  216.1 17.6 %collective-permute-start.11 = (bf16[256,192]{1,0:T(8,128)(2,1)}, bf16[256,192]{1,0:T(8,128)(2,1)}, u32[]{:S(2)}, u32[]{:S(2)}) collective-permute-start(bf16[256,192]{1,0:T(8,128)(2,1)} %get-tuple-element.183), channel_id=1, source_target_pairs={{0,2},{1,3},{2,0},{3,1},{4,6},{5,7},{6,4},{7,5},{8,10},{9,11},{10,... | collective-permute-start | bytes 294920 | tf_op jit(solution)/shard_map/ppermute | solution.py:1259
  217.6 16.1 %collective-permute-start.12 = (bf16[256,192]{1,0:T(8,128)(2,1)}, bf16[256,192]{1,0:T(8,128)(2,1)}, u32[]{:S(2)}, u32[]{:S(2)}) collective-permute-start(bf16[256,192]{1,0:T(8,128)(2,1)} %get-tuple-element.184), channel_id=1, source_target_pairs={{0,3},{1,2},{2,1},{3,0},{4,7},{5,6},{6,5},{7,4},{8,11},{9,10},{10,... | collective-permute-start | bytes 294920 | tf_op jit(solution)/shard_map/ppermute | solution.py:1259
  233.7 44.0 %collective-permute-start.20 = (bf16[2,2,4,96,576]{4,3,2,1,0:T(8,128)(2,1)}, bf16[2,2,4,96,576]{4,3,2,1,0:T(8,128)(2,1)}, u32[]{:S(2)}, u32[]{:S(2)}) collective-permute-start(bf16[2,2,4,96,576]{4,3,2,1,0:T(8,128)(2,1)} %get-tuple-element.204), channel_id=1, source_target_pairs={{0,8},{8,0},{16,24},{24,16},{1,9},{9,1},{17,25},{25,17},{2,10},{10... | collective-permute-start | bytes 5308424 | tf_op jit(solution)/shard_map/ppermute | solution.py:1259
  233.8 29.6 %collective-permute-start.19 = (bf16[2,2,4,96,384]{4,3,2,1,0:T(8,128)(2,1)}, bf16[2,2,4,96,384]{4,3,2,1,0:T(8,128)(2,1)}, u32[]{:S(2)}, u32[]{:S(2)}) collective-permute-start(bf16[2,2,4,96,384]{4,3,2,1,0:T(8,128)(2,1)} %get-tuple-element.219), channel_id=1, source_target_pairs={{0,8},{8,0},{16,24},{24,16},{1,9},{9,1},{17,25},{25,17},{2,10},{10... | collective-permute-start | bytes 3538952 | tf_op jit(solution)/shard_map/ppermute | solution.py:1259
  234.3 26.1 %collective-permute-start.23 = (f32[32,768]{1,0:T(8,128)}, f32[32,768]{1,0:T(8,128)}, u32[]{:S(2)}, u32[]{:S(2)}) collective-permute-start(f32[32,768]{1,0:T(8,128)} %add.174), channel_id=1, source_target_pairs={{0,2},{1,3},{2,0},{3,1},{4,6},{5,7},{6,4},{7,5},{8,10},{9,11},{10,... | collective-permute-start | bytes 294920 | tf_op jit(solution)/shard_map/ppermute | solution.py:1259
  241.7 39.7 %collective-permute-start.21 = (bf16[4,96,768]{2,1,0:T(8,128)(2,1)}, bf16[4,96,768]{2,1,0:T(8,128)(2,1)}, u32[]{:S(2)}, u32[]{:S(2)}) collective-permute-start(bf16[4,96,768]{2,1,0:T(8,128)(2,1)} %get-tuple-element.309), channel_id=1, source_target_pairs={{0,16},{8,24},{16,0},{24,8},{1,17},{9,25},{17,1},{25,9},{2,18},{10... | collective-permute-start | bytes 1769480 | tf_op jit(solution)/shard_map/ppermute | solution.py:1259
  243.3 38.1 %collective-permute-start.22 = (bf16[4,96,768]{2,1,0:T(8,128)(2,1)S(1)}, bf16[4,96,768]{2,1,0:T(8,128)(2,1)S(1)}, u32[]{:S(2)}, u32[]{:S(2)}) collective-permute-start(bf16[4,96,768]{2,1,0:T(8,128)(2,1)S(1)} %get-tuple-element.307), channel_id=1, source_target_pairs={{0,4},{4,0},{1,5},{5,1},{2,6},{6,2},{3,7},{7,3},{8,12},{12,8},{9,1... | collective-permute-start | bytes 1769480 | tf_op jit(solution)/shard_map/ppermute | solution.py:1259
  243.8 19.6 %copy-start.12 = (bf16[2,2,4,96,384]{4,3,2,1,0:T(8,128)(2,1)S(1)}, bf16[2,2,4,96,384]{4,3,2,1,0:T(8,128)(2,1)}, u32[]{:S(2)}) copy-start(bf16[2,2,4,96,384]{4,3,2,1,0:T(8,128)(2,1)} %get-tuple-element.218) | copy-start | bytes 3538948
  260.3 30.7 %collective-permute-start.18 = (bf16[1024,384]{1,0:T(8,128)(2,1)}, bf16[1024,384]{1,0:T(8,128)(2,1)}, u32[]{:S(2)}, u32[]{:S(2)}) collective-permute-start(bf16[1024,384]{1,0:T(8,128)(2,1)} %get-tuple-element.217.dtrunk_ref), channel_id=1, source_target_pairs={{4,0},{5,1},{6,2},{7,3},{12,8},{13,9},{14,10},{15,11},{20,16},{21,... | collective-permute-start | bytes 2359304 | tf_op jit(solution)/shard_map/ppermute | solution.py:1450
  263.3 2.8 collective-permute-start.24
  266.2 36.4 %collective-permute-start.29 = (bf16[2,4,96,384]{3,2,1,0:T(8,128)(2,1)}, bf16[2,4,96,384]{3,2,1,0:T(8,128)(2,1)}, u32[]{:S(2)}, u32[]{:S(2)}) collective-permute-start(bf16[2,4,96,384]{3,2,1,0:T(8,128)(2,1)} %get-tuple-element.305), channel_id=1, source_target_pairs={{0,4},{4,0},{1,5},{5,1},{2,6},{6,2},{3,7},{7,3},{8,12},{12,8},{9,1... | collective-permute-start | bytes 1769480 | tf_op jit(solution)/shard_map/ppermute | solution.py:1259
  277.7 8.3 %collective-permute-start.25 = (f32[40,768]{1,0:T(8,128)S(1)}, f32[40,768]{1,0:T(8,128)}, u32[]{:S(2)}, u32[]{:S(2)}) collective-permute-start(f32[40,768]{1,0:T(8,128)S(1)} %fusion.50), channel_id=1, source_target_pairs={{0,16},{8,24},{16,0},{24,8},{1,17},{9,25},{17,1},{25,9},{2,18},{10... | collective-permute-start | bytes 368648 | tf_op jit(solution)/shard_map/ppermute | solution.py:1259
  282.2 32.9 %collective-permute-start.31 = (bf16[2,4,96,576]{3,2,1,0:T(8,128)(2,1)}, bf16[2,4,96,576]{3,2,1,0:T(8,128)(2,1)}, u32[]{:S(2)}, u32[]{:S(2)}) collective-permute-start(bf16[2,4,96,576]{3,2,1,0:T(8,128)(2,1)} %get-tuple-element.303), channel_id=1, source_target_pairs={{0,16},{8,24},{16,0},{24,8},{1,17},{9,25},{17,1},{25,9},{2,18},{10... | collective-permute-start | bytes 2654216 | tf_op jit(solution)/shard_map/ppermute | solution.py:1259
  286.0 17.7 %collective-permute-start.38 = (bf16[192,768]{1,0:T(8,128)(2,1)}, bf16[192,768]{1,0:T(8,128)(2,1)S(1)}, u32[]{:S(2)}, u32[]{:S(2)}) collective-permute-start(bf16[192,768]{1,0:T(8,128)(2,1)} %get-tuple-element.311), channel_id=1, source_target_pairs={{0,1},{1,0},{2,3},{3,2},{4,5},{5,4},{6,7},{7,6},{8,9},{9,8},{10,11... | collective-permute-start | bytes 884744 | tf_op jit(solution)/shard_map/ppermute | solution.py:1259
  286.0 23.8 %collective-permute-start.39 = (bf16[192,768]{1,0:T(8,128)(2,1)}, bf16[192,768]{1,0:T(8,128)(2,1)S(1)}, u32[]{:S(2)}, u32[]{:S(2)}) collective-permute-start(bf16[192,768]{1,0:T(8,128)(2,1)} %get-tuple-element.312), channel_id=1, source_target_pairs={{0,2},{1,3},{2,0},{3,1},{4,6},{5,7},{6,4},{7,5},{8,10},{9,11},{10,... | collective-permute-start | bytes 884744 | tf_op jit(solution)/shard_map/ppermute | solution.py:1259
  291.0 24.0 %collective-permute-start.40 = (bf16[192,768]{1,0:T(8,128)(2,1)S(1)}, bf16[192,768]{1,0:T(8,128)(2,1)S(1)}, u32[]{:S(2)}, u32[]{:S(2)}) collective-permute-start(bf16[192,768]{1,0:T(8,128)(2,1)S(1)} %get-tuple-element.310), channel_id=1, source_target_pairs={{0,3},{1,2},{2,1},{3,0},{4,7},{5,6},{6,5},{7,4},{8,11},{9,10},{10,... | collective-permute-start | bytes 884744 | tf_op jit(solution)/shard_map/ppermute | solution.py:1259
  302.6 17.1 %collective-permute-start.36 = (bf16[2,2,96,576]{3,2,1,0:T(8,128)(2,1)}, bf16[2,2,96,576]{3,2,1,0:T(8,128)(2,1)S(1)}, u32[]{:S(2)}, u32[]{:S(2)}) collective-permute-start(bf16[2,2,96,576]{3,2,1,0:T(8,128)(2,1)} %get-tuple-element.238), channel_id=1, source_target_pairs={{0,8},{8,0},{16,24},{24,16},{1,9},{9,1},{17,25},{25,17},{2,10},{10... | collective-permute-start | bytes 1327112 | tf_op jit(solution)/shard_map/ppermute | solution.py:1259
  303.7 14.7 %collective-permute-start.30 = (bf16[4,96,384]{2,1,0:T(8,128)(2,1)S(1)}, bf16[4,96,384]{2,1,0:T(8,128)(2,1)S(1)}, u32[]{:S(2)}, u32[]{:S(2)}) collective-permute-start(bf16[4,96,384]{2,1,0:T(8,128)(2,1)S(1)} %fusion.28), channel_id=1, source_target_pairs={{0,16},{8,24},{16,0},{24,8},{1,17},{9,25},{17,1},{25,9},{2,18},{10... | collective-permute-start | bytes 884744 | tf_op jit(solution)/shard_map/ppermute | solution.py:1259
  309.8 23.5 %collective-permute-start.26 = (bf16[256,768]{1,0:T(8,128)(2,1)}, bf16[256,768]{1,0:T(8,128)(2,1)S(1)}, u32[]{:S(2)}, u32[]{:S(2)}) collective-permute-start(bf16[256,768]{1,0:T(8,128)(2,1)} %get-tuple-element.232), channel_id=1, source_target_pairs={{0,1},{1,0},{2,3},{3,2},{4,5},{5,4},{6,7},{7,6},{8,9},{9,8},{10,11... | collective-permute-start | bytes 1179656 | tf_op jit(solution)/shard_map/ppermute | solution.py:1259
  315.0 35.2 %collective-permute-start.27 = (bf16[256,768]{1,0:T(8,128)(2,1)}, bf16[256,768]{1,0:T(8,128)(2,1)S(1)}, u32[]{:S(2)}, u32[]{:S(2)}) collective-permute-start(bf16[256,768]{1,0:T(8,128)(2,1)} %get-tuple-element.233), channel_id=1, source_target_pairs={{0,2},{1,3},{2,0},{3,1},{4,6},{5,7},{6,4},{7,5},{8,10},{9,11},{10,... | collective-permute-start | bytes 1179656 | tf_op jit(solution)/shard_map/ppermute | solution.py:1259
  315.2 45.0 %collective-permute-start.28 = (bf16[256,768]{1,0:T(8,128)(2,1)S(1)}, bf16[256,768]{1,0:T(8,128)(2,1)S(1)}, u32[]{:S(2)}, u32[]{:S(2)}) collective-permute-start(bf16[256,768]{1,0:T(8,128)(2,1)S(1)} %copy-done.41), channel_id=1, source_target_pairs={{0,3},{1,2},{2,1},{3,0},{4,7},{5,6},{6,5},{7,4},{8,11},{9,10},{10,... | collective-permute-start | bytes 1179656 | tf_op jit(solution)/shard_map/ppermute | solution.py:1259
  318.4 11.2 %collective-permute-start.32 = (bf16[4,96,576]{2,1,0:T(8,128)(2,1)S(1)}, bf16[4,96,576]{2,1,0:T(8,128)(2,1)S(1)}, u32[]{:S(2)}, u32[]{:S(2)}) collective-permute-start(bf16[4,96,576]{2,1,0:T(8,128)(2,1)S(1)} %fusion.22), channel_id=1, source_target_pairs={{0,4},{4,0},{1,5},{5,1},{2,6},{6,2},{3,7},{7,3},{8,12},{12,8},{9,1... | collective-permute-start | bytes 1327112 | tf_op jit(solution)/shard_map/ppermute | solution.py:1259
  319.8 14.9 %collective-permute-start.37 = (bf16[2,96,576]{2,1,0:T(8,128)(2,1)S(1)}, bf16[2,96,576]{2,1,0:T(8,128)(2,1)S(1)}, u32[]{:S(2)}, u32[]{:S(2)}) collective-permute-start(bf16[2,96,576]{2,1,0:T(8,128)(2,1)S(1)} %fusion.38), channel_id=1, source_target_pairs={{0,16},{8,24},{16,0},{24,8},{1,17},{9,25},{17,1},{25,9},{2,18},{10... | collective-permute-start | bytes 663560 | tf_op jit(solution)/shard_map/ppermute | solution.py:1259
  330.9 36.8 %copy-start.15 = (f32[256,768]{1,0:T(8,128)S(1)}, f32[256,768]{1,0:T(8,128)}, u32[]{:S(2)}) copy-start(f32[256,768]{1,0:T(8,128)} %get-tuple-element.180) | copy-start | bytes 2359300
  330.9 36.8 %copy-start.16 = (f32[256,768]{1,0:T(8,128)S(1)}, f32[256,768]{1,0:T(8,128)}, u32[]{:S(2)}) copy-start(f32[256,768]{1,0:T(8,128)} %get-tuple-element.231) | copy-start | bytes 2359300
  330.9 29.6 %collective-permute-start.33 = (bf16[96,960]{1,0:T(8,128)(2,1)S(1)}, bf16[96,960]{1,0:T(8,128)(2,1)S(1)}, u32[]{:S(2)}, u32[]{:S(2)}) collective-permute-start(bf16[96,960]{1,0:T(8,128)(2,1)S(1)} %get-tuple-element.319), channel_id=1, source_target_pairs={{0,1},{1,0},{2,3},{3,2},{4,5},{5,4},{6,7},{7,6},{8,9},{9,8},{10,11... | collective-permute-start | bytes 552968 | tf_op jit(solution)/shard_map/ppermute | solution.py:1259
  333.3 29.4 %collective-permute-start.34 = (bf16[96,960]{1,0:T(8,128)(2,1)S(1)}, bf16[96,960]{1,0:T(8,128)(2,1)S(1)}, u32[]{:S(2)}, u32[]{:S(2)}) collective-permute-start(bf16[96,960]{1,0:T(8,128)(2,1)S(1)} %get-tuple-element.320), channel_id=1, source_target_pairs={{0,2},{1,3},{2,0},{3,1},{4,6},{5,7},{6,4},{7,5},{8,10},{9,11},{10,... | collective-permute-start | bytes 552968 | tf_op jit(solution)/shard_map/ppermute | solution.py:1259
  334.6 32.3 %collective-permute-start.35 = (bf16[96,960]{1,0:T(8,128)(2,1)S(1)}, bf16[96,960]{1,0:T(8,128)(2,1)S(1)}, u32[]{:S(2)}, u32[]{:S(2)}) collective-permute-start(bf16[96,960]{1,0:T(8,128)(2,1)S(1)} %get-tuple-element.318), channel_id=1, source_target_pairs={{0,3},{1,2},{2,1},{3,0},{4,7},{5,6},{6,5},{7,4},{8,11},{9,10},{10,... | collective-permute-start | bytes 552968 | tf_op jit(solution)/shard_map/ppermute | solution.py:1259
  350.2 17.8 %collective-permute-start.47 = (f32[40,768]{1,0:T(8,128)S(1)}, f32[40,768]{1,0:T(8,128)S(1)}, u32[]{:S(2)}, u32[]{:S(2)}) collective-permute-start(f32[40,768]{1,0:T(8,128)S(1)} %add.192), channel_id=1, source_target_pairs={{0,4},{4,0},{1,5},{5,1},{2,6},{6,2},{3,7},{7,3},{8,12},{12,8},{9,1... | collective-permute-start | bytes 368648 | tf_op jit(solution)/shard_map/ppermute | solution.py:1259
  360.2 9.5 %collective-permute-start.45 = (bf16[192,768]{1,0:T(8,128)(2,1)S(1)}, bf16[192,768]{1,0:T(8,128)(2,1)S(1)}, u32[]{:S(2)}, u32[]{:S(2)}) collective-permute-start(bf16[192,768]{1,0:T(8,128)(2,1)S(1)} %fusion.17), channel_id=1, source_target_pairs={{0,4},{4,0},{1,5},{5,1},{2,6},{6,2},{3,7},{7,3},{8,12},{12,8},{9,1... | collective-permute-start | bytes 884744 | tf_op jit(solution)/shard_map/ppermute | solution.py:1259
  360.6 12.6 %collective-permute-start.44 = (bf16[2,96,576]{2,1,0:T(8,128)(2,1)S(1)}, bf16[2,96,576]{2,1,0:T(8,128)(2,1)S(1)}, u32[]{:S(2)}, u32[]{:S(2)}) collective-permute-start(bf16[2,96,576]{2,1,0:T(8,128)(2,1)S(1)} %fusion.23), channel_id=1, source_target_pairs={{0,4},{4,0},{1,5},{5,1},{2,6},{6,2},{3,7},{7,3},{8,12},{12,8},{9,1... | collective-permute-start | bytes 663560 | tf_op jit(solution)/shard_map/ppermute | solution.py:1259
  367.1 8.2 %collective-permute-start.46 = (bf16[96,960]{1,0:T(8,128)(2,1)S(1)}, bf16[96,960]{1,0:T(8,128)(2,1)S(1)}, u32[]{:S(2)}, u32[]{:S(2)}) collective-permute-start(bf16[96,960]{1,0:T(8,128)(2,1)S(1)} %fusion.26), channel_id=1, source_target_pairs={{0,4},{4,0},{1,5},{5,1},{2,6},{6,2},{3,7},{7,3},{8,12},{12,8},{9,1... | collective-permute-start | bytes 552968 | tf_op jit(solution)/shard_map/ppermute | solution.py:1259
  367.9 14.2 %collective-permute-start.41 = (bf16[256,768]{1,0:T(8,128)(2,1)S(1)}, bf16[256,768]{1,0:T(8,128)(2,1)S(1)}, u32[]{:S(2)}, u32[]{:S(2)}) collective-permute-start(bf16[256,768]{1,0:T(8,128)(2,1)S(1)} %add_convert_fusion.11.refs_0_), channel_id=1, source_target_pairs={{0,1},{1,0},{2,3},{3,2},{4,5},{5,4},{6,7},{7,6},{8,9},{9,8},{10,11... | collective-permute-start | bytes 1179656 | tf_op jit(solution)/shard_map/ppermute | solution.py:1259
  368.0 28.1 %collective-permute-start.42 = (bf16[256,768]{1,0:T(8,128)(2,1)S(1)}, bf16[256,768]{1,0:T(8,128)(2,1)S(1)}, u32[]{:S(2)}, u32[]{:S(2)}) collective-permute-start(bf16[256,768]{1,0:T(8,128)(2,1)S(1)} %add_convert_fusion.11.refs_0_), channel_id=1, source_target_pairs={{0,2},{1,3},{2,0},{3,1},{4,6},{5,7},{6,4},{7,5},{8,10},{9,11},{10,... | collective-permute-start | bytes 1179656 | tf_op jit(solution)/shard_map/ppermute | solution.py:1259
  369.8 34.1 %collective-permute-start.43 = (bf16[256,768]{1,0:T(8,128)(2,1)S(1)}, bf16[256,768]{1,0:T(8,128)(2,1)S(1)}, u32[]{:S(2)}, u32[]{:S(2)}) collective-permute-start(bf16[256,768]{1,0:T(8,128)(2,1)S(1)} %add_convert_fusion.11.refs_0_), channel_id=1, source_target_pairs={{0,3},{1,2},{2,1},{3,0},{4,7},{5,6},{6,5},{7,4},{8,11},{9,10},{10,... | collective-permute-start | bytes 1179656 | tf_op jit(solution)/shard_map/ppermute | solution.py:1259
  381.5 22.4 %copy-start.9 = (bf16[1024,768]{1,0:T(8,128)(2,1)S(1)}, bf16[1024,768]{1,0:T(8,128)(2,1)}, u32[]{:S(2)}) copy-start(bf16[1024,768]{1,0:T(8,128)(2,1)} %all-gather.5.cloned.1.call-done) | copy-start | bytes 4718596
  382.1 23.7 %copy-start.19 = (bf16[256,768]{1,0:T(8,128)(2,1)}, bf16[256,768]{1,0:T(8,128)(2,1)S(1)}, u32[]{:S(2)}) copy-start(bf16[256,768]{1,0:T(8,128)(2,1)S(1)} %collective-permute-done.41.refs_1_) | copy-start | bytes 1179652
  (31 other events, 261.0 us)
Sparse Core Ops, SparseCore 0:
  41.7 96.9 all-gather.2
  170.4 36.3 all-gather.4
  238.2 41.3 all-reduce.3
